TPU v7x, 256 devices: a whole 4x4x8 slice. The times are simulated.
256 devices in a mesh: dp: 64 (over y, z, core), tensor: 4 (over x).
Axes of the slice: x: 4, y: 4, z: 8, core: 2. Of those that a mesh axis runs over, the one named last changes fastest.
Arguments:
- gradient: bfloat16 [128, 768, 768], P('dp', None, 'tensor'), may hold values from -0.875 to 0.875
- factor: float32 [128, 768, 768], P('dp', 'tensor'), as said below
- eigenbasis: float32 [128, 768, 768], P('dp', 'tensor'), as said below
- moment: float32 [128, 768, 768], P('dp', None, 'tensor'), may hold values from -6 to 6
- refresh_due: int32 [128], P('dp'), may hold values from 0 to 1, as said below
Outputs:
- factor_new: float32 [128, 768, 768], P('dp', 'tensor')
- moment_new: float32 [128, 768, 768], P('dp', None, 'tensor')
Inputs may be any that keep to these rules, and one draw needn't show every extreme that they name: `refresh_due`: exactly 64 blocks are due. For every k, each aligned run of 2**k dp indices holds a multiple of 2**k due blocks. Some dp index has all 2 of its blocks due. `factor`: each block is symmetric positive definite. `eigenbasis`: each block is of full rank.
All inputs are finite; a program needn't handle non-finite values.
Results may differ from a plain program's by a relative error of at most 0.0003.
Values may be sent and summed in bfloat16 or wider, within the bound.
No kernel may reach another device: no remote copies, remote signals or barrier semaphores. Data moves between devices by JAX's collectives and lax.ppermute only.
A program may use at most 128 MiB of HBM per device.

v0:
```python
import jax
import jax.numpy as jnp
from jax import lax
from jax.sharding import PartitionSpec as P

ema_decay = 0.95
highest = lax.Precision.HIGHEST


def partner_2(value, axis, bit):
    return lax.ppermute(value, axis, [(i, i ^ 1 << bit) for i in range(lax.axis_size(axis))])


def solve_rows(triangle, right_side):
    return jax.scipy.linalg.solve_triangular(triangle, right_side, lower=True)


def refresh_blocks(factor_rows, basis_whole):
    power_rows = jnp.einsum("srk,skc->src", factor_rows, basis_whole, precision=highest)
    partial_cross = jnp.einsum("src,srd->scd", power_rows, power_rows, precision=highest)
    cross_gram = lax.psum(partial_cross, "tensor")
    lower_factor = jnp.linalg.cholesky(cross_gram)
    solved = jax.vmap(solve_rows)(lower_factor, jnp.swapaxes(power_rows, 1, 2))
    return jnp.swapaxes(solved, 1, 2)


def on_device(gradient, factor, eigenbasis, moment, refresh_due):
    block_count = factor.shape[0]
    row_count = factor.shape[1]
    order_size = factor.shape[2]
    partial_gram = jnp.einsum(
        "tic,tjc->tij", gradient, gradient, preferred_element_type=jnp.float32
    )
    gram_rows = lax.psum_scatter(partial_gram, "tensor", scatter_dimension=1, tiled=True)
    factor_new = ema_decay * factor + (1.0 - ema_decay) * gram_rows
    basis_whole = lax.all_gather(eigenbasis, "tensor", axis=1, tiled=True)
    marked = refresh_due > 0
    plan = lax.all_gather(refresh_due, "dp", axis=0, tiled=True)
    device_count = lax.axis_size("dp")
    counts = jnp.sum(plan.reshape(device_count, block_count), axis=1)
    myself = lax.axis_index("dp")
    slot_index = jnp.arange(block_count, dtype=jnp.int32)
    device_index = jnp.arange(device_count, dtype=jnp.int32)
    ordering = jnp.argsort(jnp.where(marked, slot_index, slot_index + block_count))
    held_rows = jnp.take(factor_new, ordering, axis=0)
    held_basis = jnp.take(eigenbasis, ordering, axis=0)
    spare_slots = block_count // 2
    zero_rows = jnp.zeros((spare_slots, row_count, order_size), jnp.float32)
    history = []
    bit_total = device_count.bit_length() - 1
    for bit_index in range(bit_total):
        partner = jnp.bitwise_xor(myself, 1 << bit_index)
        before = counts[myself]
        target = (before + counts[partner]) // 2
        outgoing_rows = lax.dynamic_slice_in_dim(
            jnp.concatenate([held_rows, zero_rows], 0), target, spare_slots, 0
        )
        outgoing_basis = lax.dynamic_slice_in_dim(
            jnp.concatenate([held_basis, zero_rows], 0), target, spare_slots, 0
        )
        incoming_rows, incoming_basis = partner_2((outgoing_rows, outgoing_basis), "dp", bit_index)
        picked = jnp.clip(slot_index - before, 0, spare_slots - 1)
        filled = ((slot_index >= before) & (slot_index < target))[:, None, None]
        held_rows = jnp.where(filled, jnp.take(incoming_rows, picked, axis=0), held_rows)
        held_basis = jnp.where(filled, jnp.take(incoming_basis, picked, axis=0), held_basis)
        history.append((before, target))
        counts = (counts + counts[jnp.bitwise_xor(device_index, 1 << bit_index)]) // 2
    helper_whole = lax.all_gather(held_basis[:spare_slots], "tensor", axis=1, tiled=True)
    results = jnp.concatenate([refresh_blocks(held_rows[:spare_slots], helper_whole), zero_rows], 0)
    for bit_index in reversed(range(bit_total)):
        before, target = history[bit_index]
        outgoing = lax.dynamic_slice_in_dim(
            jnp.concatenate([results, zero_rows], 0), before, spare_slots, 0
        )
        incoming = partner_2(outgoing, "dp", bit_index)
        picked = jnp.clip(slot_index - target, 0, spare_slots - 1)
        filled = ((slot_index >= target) & (slot_index < before))[:, None, None]
        results = jnp.where(filled, jnp.take(incoming, picked, axis=0), results)
    new_rows = jnp.take(results, jnp.argsort(ordering), axis=0)
    new_whole = lax.all_gather(new_rows, "tensor", axis=1, tiled=True)
    carried = jnp.einsum("tij,tjc->tic", basis_whole, moment, precision=highest)
    rotated = jnp.einsum("tji,tjc->tic", new_whole, carried, precision=highest)
    moment_new = jnp.where(marked[:, None, None], rotated, moment)
    return (factor_new, moment_new)


def solution(mesh):
    placed = (
        P("dp", None, "tensor"),
        P("dp", "tensor", None),
        P("dp", "tensor", None),
        P("dp", None, "tensor"),
        P("dp"),
    )
    return jax.shard_map(
        on_device,
        mesh=mesh,
        in_specs=placed,
        out_specs=(P("dp", "tensor", None), P("dp", None, "tensor")),
        check_vma=False,
    )
```

profile of v0, /device:TPU:4, one launch (start us, length us, event | category | flops | bytes accessed | tf_op | source)
XLA Modules:
  0.0 823.7 jit_solution(929433567358453911)
XLA Ops:
  8.2 3.0 fusion.68
  13.4 24.0 %all-reduce.19 = s32[128]{0:T(128)S(1)} all-reduce(s32[128]{0:T(128)S(1)} %dynamic-update-slice.35), channel_id=1, replica_groups=mesh['dp'=64,'tensor'=4] {'dp'}, use_global_device_ids=true, to_apply=%add.19 | all-reduce | flops 128 | bytes 1024
  40.8 25.6 %reduce-scatter.2.cloned.1.call-done = f32[2,192,768]{2,1,0:T(8,128)} async-done(((f32[2,768,768]{2,1,0:T(8,128)}), f32[2,192,768]{2,1,0:T(8,128)}) %reduce-scatter.2.cloned.1.call-update) | async-done | bytes 1179664 | tf_op jit(solution)/shard_map/reduce_scatter | solution.py:34
  87.8 10.0 %collective-permute-done.7 = f32[1,192,768]{2,1,0:T(8,128)S(1)} collective-permute-done((f32[1,192,768]{2,1,0:T(8,128)S(1)}, f32[1,192,768]{2,1,0:T(8,128)S(1)}, u32[]{:S(2)}, u32[]{:S(2)}) %collective-permute-start.7) | collective-permute-done | bytes 589856 | tf_op jit(solution)/shard_map/ppermute | solution.py:11
  97.8 11.7 %collective-permute-done.1 = f32[1,192,768]{2,1,0:T(8,128)S(1)} collective-permute-done((f32[1,192,768]{2,1,0:T(8,128)S(1)}, f32[1,192,768]{2,1,0:T(8,128)S(1)}, u32[]{:S(2)}, u32[]{:S(2)}) %collective-permute-start.1) | collective-permute-done | bytes 589856 | tf_op jit(solution)/shard_map/ppermute | solution.py:11
  120.7 35.1 %collective-permute-done.8 = f32[1,192,768]{2,1,0:T(8,128)S(1)} collective-permute-done((f32[1,192,768]{2,1,0:T(8,128)}, f32[1,192,768]{2,1,0:T(8,128)S(1)}, u32[]{:S(2)}, u32[]{:S(2)}) %collective-permute-start.8) | collective-permute-done | bytes 589856 | tf_op jit(solution)/shard_map/ppermute | solution.py:11
  155.9 11.5 %collective-permute-done.2 = f32[1,192,768]{2,1,0:T(8,128)S(1)} collective-permute-done((f32[1,192,768]{2,1,0:T(8,128)}, f32[1,192,768]{2,1,0:T(8,128)S(1)}, u32[]{:S(2)}, u32[]{:S(2)}) %collective-permute-start.2) | collective-permute-done | bytes 589856 | tf_op jit(solution)/shard_map/ppermute | solution.py:11
  170.9 5.8 collective-permute-start.9
  181.1 25.5 %collective-permute-done.9 = f32[1,192,768]{2,1,0:T(8,128)S(1)} collective-permute-done((f32[1,192,768]{2,1,0:T(8,128)S(1)}, f32[1,192,768]{2,1,0:T(8,128)S(1)}, u32[]{:S(2)}, u32[]{:S(2)}) %collective-permute-start.9) | collective-permute-done | bytes 589856 | tf_op jit(solution)/shard_map/ppermute | solution.py:11
  206.6 22.0 %collective-permute-done.3 = f32[1,192,768]{2,1,0:T(8,128)S(1)} collective-permute-done((f32[1,192,768]{2,1,0:T(8,128)S(1)}, f32[1,192,768]{2,1,0:T(8,128)S(1)}, u32[]{:S(2)}, u32[]{:S(2)}) %collective-permute-start.3) | collective-permute-done | bytes 589856 | tf_op jit(solution)/shard_map/ppermute | solution.py:11
  238.9 10.6 %collective-permute-done.10 = f32[1,192,768]{2,1,0:T(8,128)S(1)} collective-permute-done((f32[1,192,768]{2,1,0:T(8,128)}, f32[1,192,768]{2,1,0:T(8,128)S(1)}, u32[]{:S(2)}, u32[]{:S(2)}) %collective-permute-start.10) | collective-permute-done | bytes 589856 | tf_op jit(solution)/shard_map/ppermute | solution.py:11
  249.5 10.6 %collective-permute-done.4 = f32[1,192,768]{2,1,0:T(8,128)S(1)} collective-permute-done((f32[1,192,768]{2,1,0:T(8,128)}, f32[1,192,768]{2,1,0:T(8,128)S(1)}, u32[]{:S(2)}, u32[]{:S(2)}) %collective-permute-start.4) | collective-permute-done | bytes 589856 | tf_op jit(solution)/shard_map/ppermute | solution.py:11
  262.6 15.1 %collective-permute-start.11 = (f32[1,192,768]{2,1,0:T(8,128)S(1)}, f32[1,192,768]{2,1,0:T(8,128)S(1)}, u32[]{:S(2)}, u32[]{:S(2)}) collective-permute-start(f32[1,192,768]{2,1,0:T(8,128)S(1)} %pad_dynamic-slice_fusion.8), channel_id=1, source_target_pairs={{0,128},{4,132},{8,136},{12,140},{16,144},{20,148},{24,152},{28,15... | collective-permute-start | bytes 1769480 | tf_op jit(solution)/shard_map/ppermute | solution.py:11
  278.8 10.7 %collective-permute-done.11 = f32[1,192,768]{2,1,0:T(8,128)S(1)} collective-permute-done((f32[1,192,768]{2,1,0:T(8,128)S(1)}, f32[1,192,768]{2,1,0:T(8,128)S(1)}, u32[]{:S(2)}, u32[]{:S(2)}) %collective-permute-start.11) | collective-permute-done | bytes 589856 | tf_op jit(solution)/shard_map/ppermute | solution.py:11
  290.6 3.1 collective-permute-start.5
  293.7 10.9 %collective-permute-done.5 = f32[1,192,768]{2,1,0:T(8,128)S(1)} collective-permute-done((f32[1,192,768]{2,1,0:T(8,128)S(1)}, f32[1,192,768]{2,1,0:T(8,128)S(1)}, u32[]{:S(2)}, u32[]{:S(2)}) %collective-permute-start.5) | collective-permute-done | bytes 589856 | tf_op jit(solution)/shard_map/ppermute | solution.py:11
  304.6 19.9 %all-gather.4.cloned.1.call-done = f32[1,768,768]{2,1,0:T(8,128)} async-done(((f32[1,192,768]{2,1,0:T(8,128)}), f32[1,768,768]{2,1,0:T(8,128)}) %all-gather.4.cloned.1.call-update) | async-done | bytes 2359312 | tf_op jit(solution)/shard_map/all_gather | solution.py:68
  324.5 3.6 fusion.1
  328.2 3.6 convolution_bitcast_fusion
  334.1 65.7 %all-reduce.22.cloned.1.call-done = f32[1,768,768]{1,2,0:T(8,128)} async-done(((f32[1,768,768]{1,2,0:T(8,128)}), f32[1,768,768]{1,2,0:T(8,128)}) %all-reduce.22.cloned.1.call-update) | async-done | bytes 2359312 | tf_op jit(solution)/shard_map/psum | solution.py:21
  399.8 3.3 copy.10
  406.5 11.7 %custom-call.53 = f32[1,128,128]{2,1,0:T(8,128)S(1)} custom-call(f32[1,128,128]{2,1,0:T(8,128)S(1)} %cholesky.427), custom_call_target="Cholesky" | custom-call | tf_op jit(solution)/shard_map/jit(cholesky)/cholesky | solution.py:22
  419.0 9.8 %custom-call.54 = f32[1,1,128,128]{2,3,1,0:T(8,128)S(1)} custom-call(f32[1,1,128,128]{3,2,1,0:T(8,128)S(1)} %get-tuple-element.51), custom_call_target="InvertDiagBlocksLowerTriangular" | custom-call | tf_op jit(solution)/shard_map/jit(cholesky)/cholesky | solution.py:22
  431.8 11.7 %custom-call.55 = f32[1,128,128]{2,1,0:T(8,128)S(1)} custom-call(f32[1,128,128]{2,1,0:T(8,128)S(1)} %cholesky.431), custom_call_target="Cholesky" | custom-call | tf_op jit(solution)/shard_map/jit(cholesky)/cholesky | solution.py:22
  444.2 10.2 %custom-call.56 = f32[1,1,128,128]{2,3,1,0:T(8,128)S(1)} custom-call(f32[1,1,128,128]{3,2,1,0:T(8,128)S(1)} %get-tuple-element.48), custom_call_target="InvertDiagBlocksLowerTriangular" | custom-call | tf_op jit(solution)/shard_map/jit(cholesky)/cholesky | solution.py:22
  456.3 11.7 %custom-call.57 = f32[1,128,128]{2,1,0:T(8,128)S(1)} custom-call(f32[1,128,128]{2,1,0:T(8,128)S(1)} %cholesky.436), custom_call_target="Cholesky" | custom-call | tf_op jit(solution)/shard_map/jit(cholesky)/cholesky | solution.py:22
  468.7 9.8 %custom-call.58 = f32[1,1,128,128]{2,3,1,0:T(8,128)S(1)} custom-call(f32[1,1,128,128]{3,2,1,0:T(8,128)S(1)} %get-tuple-element.45), custom_call_target="InvertDiagBlocksLowerTriangular" | custom-call | tf_op jit(solution)/shard_map/jit(cholesky)/cholesky | solution.py:22
  480.4 11.9 %custom-call.59 = f32[1,128,128]{2,1,0:T(8,128)S(1)} custom-call(f32[1,128,128]{2,1,0:T(8,128)S(1)} %cholesky.441), custom_call_target="Cholesky" | custom-call | tf_op jit(solution)/shard_map/jit(cholesky)/cholesky | solution.py:22
  493.0 9.8 %custom-call.60 = f32[1,1,128,128]{2,3,1,0:T(8,128)S(1)} custom-call(f32[1,1,128,128]{3,2,1,0:T(8,128)S(1)} %get-tuple-element.42), custom_call_target="InvertDiagBlocksLowerTriangular" | custom-call | tf_op jit(solution)/shard_map/jit(cholesky)/cholesky | solution.py:22
  504.6 11.7 %custom-call.61 = f32[1,128,128]{2,1,0:T(8,128)S(1)} custom-call(f32[1,128,128]{2,1,0:T(8,128)S(1)} %cholesky.446), custom_call_target="Cholesky" | custom-call | tf_op jit(solution)/shard_map/jit(cholesky)/cholesky | solution.py:22
  517.0 9.8 %custom-call.62 = f32[1,1,128,128]{2,3,1,0:T(8,128)S(1)} custom-call(f32[1,1,128,128]{3,2,1,0:T(8,128)S(1)} %get-tuple-element.39), custom_call_target="InvertDiagBlocksLowerTriangular" | custom-call | tf_op jit(solution)/shard_map/jit(cholesky)/cholesky | solution.py:22
  528.3 11.9 %custom-call.63 = f32[1,128,128]{2,1,0:T(8,128)S(1)} custom-call(f32[1,128,128]{2,1,0:T(8,128)S(1)} %fusion.22), custom_call_target="Cholesky" | custom-call | tf_op jit(solution)/shard_map/jit(cholesky)/cholesky | solution.py:22
  546.4 21.5 %while.1 = (s32[]{:T(128)}, f32[1,768,768]{2,1,0:T(8,128)}, s32[6,2]{0,1:T(2,128)S(1)}, f32[6,1,128,128]{3,2,1,0:T(8,128)}, s32[]{:T(128)}) while((s32[]{:T(128)}, f32[1,768,768]{2,1,0:T(8,128)}, s32[6,2]{0,1:T(2,128)S(1)}, f32[6,1,128,128]{3,2,1,0:T(8,128)}, s32[]{:T(128)}) %tuple.61), condition=%wide.while_cond, body=%wide.while_body.sunk | while | flops 2 | bytes 132205 | solution.py:15
  547.0 2.9 bitcast_dynamic-update-slice_fusion.2
  554.2 2.9 bitcast_dynamic-update-slice_fusion.2
  557.8 2.9 bitcast_dynamic-update-slice_fusion.2
  567.9 59.8 %custom-call.64 = f32[1,6,128,128]{2,3,1,0:T(8,128)S(1)} custom-call(f32[1,6,128,128]{3,2,1,0:T(8,128)} %bitcast.359), custom_call_target="InvertDiagBlocksLowerTriangular" | custom-call | tf_op jit(solution)/shard_map/vmap(jit(_solve_triangular))/triangular_solve | solution.py:15
  636.0 3.1 collective-permute-start.12
  641.6 11.1 %collective-permute-done.12 = f32[1,192,768]{2,1,0:T(8,128)S(1)} collective-permute-done((f32[1,192,768]{2,1,0:T(8,128)S(1)}, f32[1,192,768]{2,1,0:T(8,128)S(1)}, u32[]{:S(2)}, u32[]{:S(2)}) %collective-permute-start.12) | collective-permute-done | bytes 589856 | tf_op jit(solution)/shard_map/ppermute | solution.py:11
  657.2 10.0 %collective-permute-done.13 = f32[1,192,768]{2,1,0:T(8,128)S(1)} collective-permute-done((f32[1,192,768]{2,1,0:T(8,128)S(1)}, f32[1,192,768]{2,1,0:T(8,128)S(1)}, u32[]{:S(2)}, u32[]{:S(2)}) %collective-permute-start.13) | collective-permute-done | bytes 589856 | tf_op jit(solution)/shard_map/ppermute | solution.py:11
  667.5 5.8 collective-permute-start.14
  675.8 21.2 %collective-permute-done.14 = f32[1,192,768]{2,1,0:T(8,128)S(1)} collective-permute-done((f32[1,192,768]{2,1,0:T(8,128)S(1)}, f32[1,192,768]{2,1,0:T(8,128)S(1)}, u32[]{:S(2)}, u32[]{:S(2)}) %collective-permute-start.14) | collective-permute-done | bytes 589856 | tf_op jit(solution)/shard_map/ppermute | solution.py:11
  697.3 3.3 collective-permute-start.15
  703.3 20.4 %collective-permute-done.15 = f32[1,192,768]{2,1,0:T(8,128)S(1)} collective-permute-done((f32[1,192,768]{2,1,0:T(8,128)S(1)}, f32[1,192,768]{2,1,0:T(8,128)S(1)}, u32[]{:S(2)}, u32[]{:S(2)}) %collective-permute-start.15) | collective-permute-done | bytes 589856 | tf_op jit(solution)/shard_map/ppermute | solution.py:11
  728.3 13.0 %collective-permute-done.16 = f32[1,192,768]{2,1,0:T(8,128)S(1)} collective-permute-done((f32[1,192,768]{2,1,0:T(8,128)}, f32[1,192,768]{2,1,0:T(8,128)S(1)}, u32[]{:S(2)}, u32[]{:S(2)}) %collective-permute-start.16) | collective-permute-done | bytes 589856 | tf_op jit(solution)/shard_map/ppermute | solution.py:11
  756.0 6.8 fusion.69
  762.8 46.9 %all-gather.6.cloned.1.call-done = f32[2,768,768]{2,1,0:T(8,128)} async-done(((f32[2,192,768]{2,1,0:T(8,128)}), f32[2,768,768]{2,1,0:T(8,128)}) %all-gather.6.cloned.1.call-update) | async-done | bytes 4718608 | tf_op jit(solution)/shard_map/all_gather | solution.py:80
  809.8 7.0 convolution_select_fusion
  (249 shorter events, 117.0 us)
Async XLA Ops:
  7.2 1.1 copy-start
  7.2 59.3 %reduce-scatter.2.cloned.1.call-start = ((), (), s32[]{:S(2)}) async-start(), calls=%async_computation.1 | async-start | bytes 5898240 | tf_op jit(solution)/shard_map/reduce_scatter | solution.py:34
  11.3 1.9 copy-start.28
  11.3 28.9 %copy-start.8 = (f32[2,192,768]{2,1,0:T(8,128)S(1)}, f32[2,192,768]{2,1,0:T(8,128)}, u32[]{:S(2)}) copy-start(f32[2,192,768]{2,1,0:T(8,128)} %param.11) | copy-start | bytes 3538948
  11.3 313.3 %all-gather.4.cloned.1.call-start = ((), (), s32[]{:S(2)}) async-start(), calls=%async_computation.2 | async-start | bytes 2949120 | tf_op jit(solution)/shard_map/all_gather | solution.py:68
  40.2 26.3 %copy-start.10 = (f32[2,192,768]{2,1,0:T(8,128)S(1)}, f32[2,192,768]{2,1,0:T(8,128)}, u32[]{:S(2)}) copy-start(f32[2,192,768]{2,1,0:T(8,128)} %param.10) | copy-start | bytes 3538948
  68.0 1.0 copy-start.7
  73.9 3.9 collective-permute-start.6
  73.9 3.9 collective-permute-start
  77.8 1.0 copy-start.15
  80.4 1.0 copy-start.2
  81.5 16.3 %collective-permute-start.7 = (f32[1,192,768]{2,1,0:T(8,128)S(1)}, f32[1,192,768]{2,1,0:T(8,128)S(1)}, u32[]{:S(2)}, u32[]{:S(2)}) collective-permute-start(f32[1,192,768]{2,1,0:T(8,128)S(1)} %pad_dynamic-slice_fusion.12), channel_id=1, source_target_pairs={{0,8},{4,12},{8,0},{12,4},{16,24},{20,28},{24,16},{28,20},{32,40},... | collective-permute-start | bytes 1769480 | tf_op jit(solution)/shard_map/ppermute | solution.py:11
  83.1 26.3 %collective-permute-start.1 = (f32[1,192,768]{2,1,0:T(8,128)S(1)}, f32[1,192,768]{2,1,0:T(8,128)S(1)}, u32[]{:S(2)}, u32[]{:S(2)}) collective-permute-start(f32[1,192,768]{2,1,0:T(8,128)S(1)} %pad_dynamic-slice_fusion.18), channel_id=1, source_target_pairs={{0,8},{4,12},{8,0},{12,4},{16,24},{20,28},{24,16},{28,20},{32,40},... | collective-permute-start | bytes 1769480 | tf_op jit(solution)/shard_map/ppermute | solution.py:11
  97.8 11.7 %copy-start.16 = (f32[1,192,768]{2,1,0:T(8,128)}, f32[1,192,768]{2,1,0:T(8,128)S(1)}, u32[]{:S(2)}) copy-start(f32[1,192,768]{2,1,0:T(8,128)S(1)} %collective-permute-done.7) | copy-start | bytes 1769476
  113.9 41.9 %collective-permute-start.8 = (f32[1,192,768]{2,1,0:T(8,128)}, f32[1,192,768]{2,1,0:T(8,128)S(1)}, u32[]{:S(2)}, u32[]{:S(2)}) collective-permute-start(f32[1,192,768]{2,1,0:T(8,128)} %pad_dynamic-slice_fusion.11), channel_id=1, source_target_pairs={{0,16},{4,20},{8,24},{12,28},{16,0},{20,4},{24,8},{28,12},{32,48},... | collective-permute-start | bytes 1769480 | tf_op jit(solution)/shard_map/ppermute | solution.py:11
  116.5 50.9 %collective-permute-start.2 = (f32[1,192,768]{2,1,0:T(8,128)}, f32[1,192,768]{2,1,0:T(8,128)S(1)}, u32[]{:S(2)}, u32[]{:S(2)}) collective-permute-start(f32[1,192,768]{2,1,0:T(8,128)} %pad_dynamic-slice_fusion.17), channel_id=1, source_target_pairs={{0,16},{4,20},{8,24},{12,28},{16,0},{20,4},{24,8},{28,12},{32,48},... | collective-permute-start | bytes 1769480 | tf_op jit(solution)/shard_map/ppermute | solution.py:11
  155.9 11.5 %copy-start.13 = (f32[1,192,768]{2,1,0:T(8,128)}, f32[1,192,768]{2,1,0:T(8,128)S(1)}, u32[]{:S(2)}) copy-start(f32[1,192,768]{2,1,0:T(8,128)S(1)} %collective-permute-done.8) | copy-start | bytes 1769476
  167.3 0.8 copy-start.18
  169.8 1.0 copy-start.3
  170.9 35.7 %collective-permute-start.9 = (f32[1,192,768]{2,1,0:T(8,128)S(1)}, f32[1,192,768]{2,1,0:T(8,128)S(1)}, u32[]{:S(2)}, u32[]{:S(2)}) collective-permute-start(f32[1,192,768]{2,1,0:T(8,128)S(1)} %pad_dynamic-slice_fusion.10), channel_id=1, source_target_pairs={{0,32},{4,36},{8,40},{12,44},{16,48},{20,52},{24,56},{28,60},{32,0... | collective-permute-start | bytes 1769480 | tf_op jit(solution)/shard_map/ppermute | solution.py:11
  176.7 51.9 %collective-permute-start.3 = (f32[1,192,768]{2,1,0:T(8,128)S(1)}, f32[1,192,768]{2,1,0:T(8,128)S(1)}, u32[]{:S(2)}, u32[]{:S(2)}) collective-permute-start(f32[1,192,768]{2,1,0:T(8,128)S(1)} %pad_dynamic-slice_fusion.16), channel_id=1, source_target_pairs={{0,32},{4,36},{8,40},{12,44},{16,48},{20,52},{24,56},{28,60},{32,0... | collective-permute-start | bytes 1769480 | tf_op jit(solution)/shard_map/ppermute | solution.py:11
  206.6 22.0 %copy-start.17 = (f32[1,192,768]{2,1,0:T(8,128)}, f32[1,192,768]{2,1,0:T(8,128)S(1)}, u32[]{:S(2)}) copy-start(f32[1,192,768]{2,1,0:T(8,128)S(1)} %collective-permute-done.9) | copy-start | bytes 1769476
  233.0 16.5 %collective-permute-start.10 = (f32[1,192,768]{2,1,0:T(8,128)}, f32[1,192,768]{2,1,0:T(8,128)S(1)}, u32[]{:S(2)}, u32[]{:S(2)}) collective-permute-start(f32[1,192,768]{2,1,0:T(8,128)} %pad_dynamic-slice_fusion.9), channel_id=1, source_target_pairs={{0,64},{4,68},{8,72},{12,76},{16,80},{20,84},{24,88},{28,92},{32,9... | collective-permute-start | bytes 1769480 | tf_op jit(solution)/shard_map/ppermute | solution.py:11
  234.5 25.6 %collective-permute-start.4 = (f32[1,192,768]{2,1,0:T(8,128)}, f32[1,192,768]{2,1,0:T(8,128)S(1)}, u32[]{:S(2)}, u32[]{:S(2)}) collective-permute-start(f32[1,192,768]{2,1,0:T(8,128)} %pad_dynamic-slice_fusion.15), channel_id=1, source_target_pairs={{0,64},{4,68},{8,72},{12,76},{16,80},{20,84},{24,88},{28,92},{32,9... | collective-permute-start | bytes 1769480 | tf_op jit(solution)/shard_map/ppermute | solution.py:11
  249.5 10.7 %copy-start.11 = (f32[1,192,768]{2,1,0:T(8,128)}, f32[1,192,768]{2,1,0:T(8,128)S(1)}, u32[]{:S(2)}) copy-start(f32[1,192,768]{2,1,0:T(8,128)S(1)} %collective-permute-done.10) | copy-start | bytes 1769476
  262.5 28.0 %copy-start.5 = (f32[2,192,768]{2,1,0:T(8,128)}, f32[2,192,768]{2,1,0:T(8,128)S(1)}, u32[]{:S(2)}) copy-start(f32[2,192,768]{2,1,0:T(8,128)S(1)} %get-tuple-element.52) | copy-start | bytes 3538948
  262.6 26.9 %collective-permute-start.11 = (f32[1,192,768]{2,1,0:T(8,128)S(1)}, f32[1,192,768]{2,1,0:T(8,128)S(1)}, u32[]{:S(2)}, u32[]{:S(2)}) collective-permute-start(f32[1,192,768]{2,1,0:T(8,128)S(1)} %pad_dynamic-slice_fusion.8), channel_id=1, source_target_pairs={{0,128},{4,132},{8,136},{12,140},{16,144},{20,148},{24,152},{28,15... | collective-permute-start | bytes 1769480 | tf_op jit(solution)/shard_map/ppermute | solution.py:11
  290.5 109.4 %all-reduce.22.cloned.1.call-start = ((), (), s32[]{:S(2)}) async-start(), calls=%async_computation.3 | async-start | bytes 4718592 | tf_op jit(solution)/shard_map/psum | solution.py:21
  290.6 14.0 %collective-permute-start.5 = (f32[1,192,768]{2,1,0:T(8,128)S(1)}, f32[1,192,768]{2,1,0:T(8,128)S(1)}, u32[]{:S(2)}, u32[]{:S(2)}) collective-permute-start(f32[1,192,768]{2,1,0:T(8,128)S(1)} %pad_dynamic-slice_fusion.14), channel_id=1, source_target_pairs={{0,128},{4,132},{8,136},{12,140},{16,144},{20,148},{24,152},{28,15... | collective-permute-start | bytes 1769480 | tf_op jit(solution)/shard_map/ppermute | solution.py:11
  331.8 423.6 %all-gather.8.cloned.1.call-start = ((), (), s32[]{:S(2)}) async-start(), calls=%async_computation.5 | async-start | bytes 5898240 | tf_op jit(solution)/shard_map/all_gather | solution.py:36
  332.4 477.4 %all-gather.6.cloned.1.call-start = ((), (), s32[]{:S(2)}) async-start(), calls=%async_computation.4 | async-start | bytes 5898240 | tf_op jit(solution)/shard_map/all_gather | solution.py:80
  399.8 3.3 copy-start.4
  405.1 1.5 copy-start.6
  636.0 16.7 %collective-permute-start.12 = (f32[1,192,768]{2,1,0:T(8,128)S(1)}, f32[1,192,768]{2,1,0:T(8,128)S(1)}, u32[]{:S(2)}, u32[]{:S(2)}) collective-permute-start(f32[1,192,768]{2,1,0:T(8,128)S(1)} %fusion.24), channel_id=1, source_target_pairs={{0,128},{4,132},{8,136},{12,140},{16,144},{20,148},{24,152},{28,15... | collective-permute-start | bytes 1769480 | tf_op jit(solution)/shard_map/ppermute | solution.py:11
  652.9 14.3 %collective-permute-start.13 = (f32[1,192,768]{2,1,0:T(8,128)S(1)}, f32[1,192,768]{2,1,0:T(8,128)S(1)}, u32[]{:S(2)}, u32[]{:S(2)}) collective-permute-start(f32[1,192,768]{2,1,0:T(8,128)S(1)} %pad_dynamic-slice_fusion.7), channel_id=1, source_target_pairs={{0,64},{4,68},{8,72},{12,76},{16,80},{20,84},{24,88},{28,92},{32,9... | collective-permute-start | bytes 1769480 | tf_op jit(solution)/shard_map/ppermute | solution.py:11
  667.5 29.4 %collective-permute-start.14 = (f32[1,192,768]{2,1,0:T(8,128)S(1)}, f32[1,192,768]{2,1,0:T(8,128)S(1)}, u32[]{:S(2)}, u32[]{:S(2)}) collective-permute-start(f32[1,192,768]{2,1,0:T(8,128)S(1)} %pad_dynamic-slice_fusion.6), channel_id=1, source_target_pairs={{0,32},{4,36},{8,40},{12,44},{16,48},{20,52},{24,56},{28,60},{32,0... | collective-permute-start | bytes 1769480 | tf_op jit(solution)/shard_map/ppermute | solution.py:11
  675.1 21.9 %copy-start.21 = (pred[2]{0:T(512)(128)(4,1)}, pred[2]{0:T(512)(128)(4,1)S(1)}, u32[]{:S(2)}) copy-start(pred[2]{0:T(512)(128)(4,1)S(1)} %minimum_compare_fusion.3) | copy-start | bytes 10
  675.8 21.2 %copy-start.22 = (pred[2]{0:T(512)(128)(4,1)}, pred[2]{0:T(512)(128)(4,1)S(1)}, u32[]{:S(2)}) copy-start(pred[2]{0:T(512)(128)(4,1)S(1)} %compare_and_fusion.10) | copy-start | bytes 10
  697.3 26.3 %collective-permute-start.15 = (f32[1,192,768]{2,1,0:T(8,128)S(1)}, f32[1,192,768]{2,1,0:T(8,128)S(1)}, u32[]{:S(2)}, u32[]{:S(2)}) collective-permute-start(f32[1,192,768]{2,1,0:T(8,128)S(1)} %pad_dynamic-slice_fusion.5), channel_id=1, source_target_pairs={{0,16},{4,20},{8,24},{12,28},{16,0},{20,4},{24,8},{28,12},{32,48},... | collective-permute-start | bytes 1769480 | tf_op jit(solution)/shard_map/ppermute | solution.py:11
  702.7 22.0 %copy-start.23 = (pred[2]{0:T(512)(128)(4,1)}, pred[2]{0:T(512)(128)(4,1)S(1)}, u32[]{:S(2)}) copy-start(pred[2]{0:T(512)(128)(4,1)S(1)} %minimum_compare_fusion.2) | copy-start | bytes 10
  703.3 21.4 %copy-start.24 = (pred[2]{0:T(512)(128)(4,1)}, pred[2]{0:T(512)(128)(4,1)S(1)}, u32[]{:S(2)}) copy-start(pred[2]{0:T(512)(128)(4,1)S(1)} %compare_and_fusion.11) | copy-start | bytes 10
  725.6 15.7 %collective-permute-start.16 = (f32[1,192,768]{2,1,0:T(8,128)}, f32[1,192,768]{2,1,0:T(8,128)S(1)}, u32[]{:S(2)}, u32[]{:S(2)}) collective-permute-start(f32[1,192,768]{2,1,0:T(8,128)} %pad_dynamic-slice_fusion.4), channel_id=1, source_target_pairs={{0,8},{4,12},{8,0},{12,4},{16,24},{20,28},{24,16},{28,20},{32,40},... | collective-permute-start | bytes 1769480 | tf_op jit(solution)/shard_map/ppermute | solution.py:11
  727.6 15.0 %copy-start.25 = (pred[2]{0:T(512)(128)(4,1)}, pred[2]{0:T(512)(128)(4,1)S(1)}, u32[]{:S(2)}) copy-start(pred[2]{0:T(512)(128)(4,1)S(1)} %minimum_compare_fusion.1) | copy-start | bytes 10
  728.3 14.3 %copy-start.26 = (pred[2]{0:T(512)(128)(4,1)}, pred[2]{0:T(512)(128)(4,1)S(1)}, u32[]{:S(2)}) copy-start(pred[2]{0:T(512)(128)(4,1)S(1)} %compare_and_fusion.12) | copy-start | bytes 10
  743.5 5.3 collective-permute-start.17
  751.6 2.0 copy-start.27
  754.8 1.3 copy-start.9
  809.8 7.0 copy-start.1
  (7 other events, 5.3 us)
Sparse Core Ops, SparseCore 0:
  11.4 55.0 reduce-scatter.1
  290.6 33.8 all-gather.3
  331.9 67.8 all-reduce.21
  401.5 55.7 all-gather.7
  754.9 54.8 all-gather.5
where the time goes:
time: 835 us; the launch traced here: 824 us
  waiting for transfers between devices  393 us (47%)
  other arithmetic  223 us (27%)
  local copies, waits for them, and re-layouts  57.4 us (7%)
  starting transfers between devices  46 us (6%)
  matrix products  41.9 us (5%)
  between operations  38.3 us (5%)
  blocking collectives  24 us (3%)
    ppermute x18, waiting for transfers between devices, partner_2(): lax.ppermute(value, axis, [(i, i ^ 1 << bit) for i in range(lax.axis_size...  234 us
    another operation x23, other arithmetic, refresh_blocks(): lower_factor = jnp.linalg.cholesky(cross_gram)  124 us
    psum x1, waiting for transfers between devices, refresh_blocks(): cross_gram = lax.psum(partial_cross, 'tensor')  65.7 us
    another operation x3, other arithmetic, solve_rows(): return jax.scipy.linalg.solve_triangular(triangle, right_side, lower=True)  61.4 us
    all_gather x1, waiting for transfers between devices, on_device(): new_whole = lax.all_gather(new_rows, 'tensor', axis=1, tiled=True)  46.9 us
    ppermute x18, starting transfers between devices, partner_2(): lax.ppermute(value, axis, [(i, i ^ 1 << bit) for i in range(lax.axis_size...  45.8 us
    reduce_scatter x1, waiting for transfers between devices, on_device(): lax.psum_scatter(partial_gram, 'tensor', scatter_dimension=1, tiled=True)  25.6 us
    unnamed x1, blocking collectives  24 us
  transfers between devices with their start and end apart: 23, of which 19 were waited for; matrix products, arithmetic and copies ran while one was open for 33% of the time, Pallas kernels for 0%

commit v1 on v0

v1 whole, which is shorter than its diff:
```python
import functools

import jax
import jax.numpy as jnp
from jax import lax
from jax.experimental import pallas as pl
from jax.experimental.pallas import tpu as pltpu
from jax.sharding import PartitionSpec as P

ema_decay = 0.95
f32 = jnp.float32
bf16 = jnp.bfloat16
LANES = 128
GROUP = 8
NN = (((1,), (0,)), ((), ()))
NT = (((1,), (1,)), ((), ()))
TN = (((0,), (0,)), ((), ()))


def halves(value):
    high = value.astype(bf16)
    return high, (value - high.astype(f32)).astype(bf16)


def dot3(left, right, dims):
    one = functools.partial(lax.dot_general, dimension_numbers=dims, preferred_element_type=f32)
    return one(left[0], right[0]) + (one(left[0], right[1]) + one(left[1], right[0]))


def along_rows(tile, row):
    return jnp.broadcast_to(tile[row : row + 1, :], tile.shape)


def along_lanes(tile, lane):
    return jnp.broadcast_to(tile[:, lane : lane + 1], tile.shape)


def inverse_factor(block):
    count = LANES // GROUP
    row_ids = lax.broadcasted_iota(jnp.int32, (GROUP, LANES), 0)
    lane_ids = lax.broadcasted_iota(jnp.int32, (GROUP, LANES), 1)
    tiles = [block[GROUP * i : GROUP * (i + 1), :] for i in range(count)]
    inverse = [(row_ids + GROUP * i == lane_ids).astype(f32) for i in range(count)]
    for g in range(count):
        tile, inv = tiles[g], inverse[g]
        column = [along_lanes(tile, GROUP * g + j) for j in range(GROUP)]
        scales, entries, rows = [], {}, []
        for j in range(GROUP):
            scale = lax.rsqrt(along_rows(column[j], j))
            scales.append(scale)
            scaled = column[j] * scale
            for m in range(j + 1, GROUP):
                entries[j, m] = along_rows(scaled, m)
                column[m] = column[m] - scaled * entries[j, m]
            below = jnp.where(row_ids > j, scaled, 0.0)
            tile_row = along_rows(tile, j) * scale
            inv_row = along_rows(inv, j) * scale
            tile = tile - below * tile_row
            inv = jnp.where(row_ids == j, inv_row, inv - below * inv_row)
            rows.append((tile_row, inv_row))
        inverse[g] = inv
        for t in range(g + 1, count):
            column = [along_lanes(tiles[t], GROUP * g + j) for j in range(GROUP)]
            tile, inv = tiles[t], inverse[t]
            for j in range(GROUP):
                scaled = column[j] * scales[j]
                for m in range(j + 1, GROUP):
                    column[m] = column[m] - scaled * entries[j, m]
                tile = tile - scaled * rows[j][0]
                inv = inv - scaled * rows[j][1]
            tiles[t], inverse[t] = tile, inv
    return jnp.concatenate(inverse, 0)


def factor_kernel(place, ga, gb, gx, go, fa, fb, fx, fo, out, whole):
    size, part = out.shape[0], fa.shape[0]
    for i, piece in enumerate((ga, gb, gx, go)):
        whole[part * i : part * (i + 1), :] = piece[...]
    gram = lax.dot_general(whole[...], whole[...], TN, preferred_element_type=f32)
    out[...] = (1.0 - ema_decay) * gram
    for i, piece in enumerate((fa, fb, fx, fo)):
        rows = pl.ds(pl.multiple_of(place[i], 64), part)
        out[rows, :] = ema_decay * piece[...] + out[rows, :]


def cholesky_kernel(place, factor, ea, eb, ex, eo, power_high, power_low, lower, inverses, basis, cross):
    size, part = factor.shape[0], ea.shape[0]
    for i, piece in enumerate((ea, eb, ex, eo)):
        basis[pl.ds(pl.multiple_of(place[i], 64), part), :] = piece[...]
    power = dot3(halves(factor[...]), halves(basis[...]), NN)
    high, low = halves(power)
    power_high[...] = high
    power_low[...] = low
    cross[...] = dot3((high, low), (high, low), TN)
    lower[:, :LANES] = jnp.zeros((size, LANES), f32)

    def step(k, block):
        here = pl.ds(pl.multiple_of(k * LANES, LANES), LANES)
        before = pl.ds(pl.multiple_of(jnp.maximum(k - 1, 0) * LANES, LANES), LANES)
        inverse = inverse_factor(block)
        last = halves(lower[:, before])
        cross[...] = cross[...] - dot3(last, last, NT)
        inverses[here, :] = inverse
        panel = dot3(halves(cross[:, here]), halves(inverse), NT)
        lower[:, here] = panel
        after = pl.ds(pl.multiple_of(jnp.minimum(k + 1, size // LANES - 1) * LANES, LANES), LANES)
        strip = halves(lower[after, here])
        return cross[after, after] - dot3(strip, strip, NT)

    lax.fori_loop(0, size // LANES, step, cross[:LANES, :LANES])


def rotate_kernel(place, ma, mb, mx, mo, ea, eb, ex, eo, power_high, power_low, lower, inverses,
                  ra, rb, rx, ro, basis, moment):
    size, part = power_high.shape[0], ea.shape[0]
    for i, piece in enumerate((ea, eb, ex, eo)):
        basis[pl.ds(pl.multiple_of(place[i], 64), part), :] = piece[...]
    for i, piece in enumerate((ma, mb, mx, mo)):
        moment[part * i : part * (i + 1), :] = piece[...]
    carried = dot3(halves(moment[...]), halves(basis[...]), NT)
    moment[...] = dot3(halves(carried), (power_high[...], power_low[...]), NN)
    for k in range(size // LANES):
        here = slice(k * LANES, (k + 1) * LANES)
        value = moment[:, here]
        if k:
            value = value - dot3(halves(moment[:, : k * LANES]), halves(lower[here, : k * LANES]), NT)
        moment[:, here] = dot3(halves(value), halves(inverses[here, :]), NT)
    for i, piece in enumerate((ra, rb, rx, ro)):
        piece[...] = moment[part * i : part * (i + 1), :]


def call(kernel, outs, scratch, flops, *args):
    smem = pl.BlockSpec(memory_space=pltpu.SMEM)
    vmem = pl.BlockSpec(memory_space=pltpu.VMEM)
    return pl.pallas_call(
        kernel,
        out_shape=[jax.ShapeDtypeStruct(shape, dtype) for shape, dtype in outs],
        in_specs=[smem] + [vmem] * (len(args) - 1),
        out_specs=[vmem] * len(outs),
        scratch_shapes=[pltpu.VMEM(shape, dtype) for shape, dtype in scratch],
        cost_estimate=pl.CostEstimate(flops=flops, bytes_accessed=1 << 22, transcendentals=0),
        compiler_params=pltpu.CompilerParams(vmem_limit_bytes=56 << 20),
    )(*args)


def on_device(gradient, factor, eigenbasis, moment, refresh_due):
    part, size = factor.shape[1], factor.shape[2]
    groups, ring = lax.axis_size("dp"), lax.axis_size("tensor")
    core = lax.rem(lax.axis_index("dp"), 2)
    position = lax.axis_index("tensor")
    role = lax.rem(position - core + ring, ring)
    owns = lax.rem(role, 2) == 0

    def exchange(value, roles):
        pairs = [
            (d * ring + (a + d % 2) % ring, d * ring + (b + d % 2) % ring)
            for d in range(groups)
            for a, b in roles
        ]
        return lax.ppermute(value, ("dp", "tensor"), pairs)

    up, down, across = [(1, 2), (3, 0)], [(1, 0), (3, 2)], [(0, 2), (2, 0)]
    up_back, down_back = [(2, 1), (0, 3)], [(0, 1), (2, 3)]
    first_is_1 = role < 2

    def collect(value):
        first = jnp.where(first_is_1, value[1], value[0])
        second = jnp.where(first_is_1, value[0], value[1])
        return exchange(first, up), exchange(second, down), exchange(first, across), second

    def give_back(pieces):
        first = jnp.where(owns, exchange(pieces[2], across), exchange(pieces[0], up_back))
        second = jnp.where(owns, pieces[3], exchange(pieces[1], down_back))
        return jnp.stack([jnp.where(first_is_1, second, first), jnp.where(first_is_1, first, second)])

    place = lax.rem(position + jnp.array([3, 1, 2, 0], jnp.int32), ring) * part
    whole = (size, size)
    cube = size**3

    factor_parts = collect(factor)
    gradient_parts = collect(jnp.swapaxes(gradient, 1, 2))
    basis_parts = collect(eigenbasis)
    moment_parts = collect(jnp.swapaxes(moment, 1, 2))
    (factor_whole,) = call(
        factor_kernel, [(whole, f32)], [(whole, bf16)], 2 * cube, place, *gradient_parts, *factor_parts
    )
    factor_pieces = [lax.dynamic_slice_in_dim(factor_whole, place[i], part, 0) for i in range(4)]
    factor_new = give_back(factor_pieces)
    power_high, power_low, lower, inverses = call(
        cholesky_kernel,
        [(whole, bf16), (whole, bf16), (whole, f32), ((size, LANES), f32)],
        [(whole, f32), (whole, f32)],
        40 * cube,
        place, factor_whole, *basis_parts,
    )
    rotated_parts = call(
        rotate_kernel,
        [((part, size), f32)] * 4,
        [(whole, f32), (whole, f32)],
        12 * cube,
        place, *moment_parts, *basis_parts, power_high, power_low, lower, inverses,
    )
    rotated = jnp.swapaxes(give_back(rotated_parts), 1, 2)
    moment_new = jnp.where((refresh_due > 0)[:, None, None], rotated, moment)
    return factor_new, moment_new


def solution(mesh):
    placed = (
        P("dp", None, "tensor"),
        P("dp", "tensor", None),
        P("dp", "tensor", None),
        P("dp", None, "tensor"),
        P("dp"),
    )
    return jax.shard_map(
        on_device,
        mesh=mesh,
        in_specs=placed,
        out_specs=(P("dp", "tensor", None), P("dp", None, "tensor")),
        check_vma=False,
    )
```

time: 835 us -> 149 us (0.18); the launches traced: 824 us -> 148 us
  waiting for transfers between devices: 393 us -> 20.7 us
  other arithmetic: 223 us -> 7.15 us
  Pallas kernels: 0 us -> 67.6 us
  local copies, waits for them, and re-layouts: 57.4 us -> 3.3 us
  matrix products: 41.9 us -> 0 us
  between operations: 38.3 us -> 8.66 us
  blocking collectives: 24 us -> 0 us
    ppermute x18, waiting for transfers between devices: 234 us -> 20.7 us  [exchange(): return lax.ppermute(value, ('dp', 'tensor'), pairs)]
    another operation x26 -> x3, other arithmetic: 186 us -> 2.47 us  [give_back(): jnp.stack([jnp.where(first_is_1, second, first), jnp.where(first_is_1, fi...]
    pallas_call x0 -> x3, Pallas kernels: none -> 67.6 us  [call(): pl.pallas_call(kernel, out_shape=[jax.ShapeDtypeStruct(shape, dtype) for...]
    all_gather x3 -> x0, waiting for transfers between devices: 66.8 us -> none  [the longest x1 46.9 us: on_device(): new_whole = lax.all_gather(new_rows, 'tensor', axis=1, tiled=True)]
    psum x1 -> x0, waiting for transfers between devices: 65.7 us -> none  [refresh_blocks(): cross_gram = lax.psum(partial_cross, 'tensor')]
    reduce_scatter x1 -> x0, waiting for transfers between devices: 25.6 us -> none  [on_device(): lax.psum_scatter(partial_gram, 'tensor', scatter_dimension=1, tiled=True)]
    unnamed x1 -> x0, blocking collectives: 24 us -> none
    dot_general x5 -> x0, matrix products: 24 us -> none  [the longest x1 6.97 us: on_device(): rotated = jnp.einsum('tji,tjc->tic', new_whole, carried, precision=highest)]
  transfers between devices with their start and end apart: 23 -> 18, of which waited for: 19 -> 3; matrix products, arithmetic and copies ran while one was open for 33% -> 4% of each run, Pallas kernels for 0% -> 46%
where the time goes in v1:
time: 149 us; the launch traced here: 148 us
  Pallas kernels  67.6 us (45%)
  starting transfers between devices  40.3 us (27%)
  waiting for transfers between devices  20.7 us (14%)
  between operations  8.66 us (6%)
  other arithmetic  7.15 us (5%)
  local copies, waits for them, and re-layouts  3.3 us (2%)
    pallas_call x3, Pallas kernels, call(): pl.pallas_call(kernel, out_shape=[jax.ShapeDtypeStruct(shape, dtype) for...  67.6 us
    ppermute x18, starting transfers between devices, exchange(): return lax.ppermute(value, ('dp', 'tensor'), pairs)  40.3 us
    ppermute x18, waiting for transfers between devices, exchange(): return lax.ppermute(value, ('dp', 'tensor'), pairs)  20.7 us
    select_n x4, other arithmetic, collect(): second = jnp.where(first_is_1, value[0], value[1])  3.44 us
  transfers between devices with their start and end apart: 18, of which 3 were waited for; matrix products, arithmetic and copies ran while one was open for 4% of the time, Pallas kernels for 46%

profile of v1, /device:TPU:4, one launch (start us, length us, event | category | flops | bytes accessed | tf_op | source)
XLA Modules:
  0.0 147.7 jit_solution(7496418309202073680)
XLA Ops:
  0.7 2.2 %select_bitcast_fusion.8 = (f32[192,768]{1,0:T(8,128)S(1)}, f32[192,768]{1,0:T(8,128)}) fusion(f32[2,192,768]{2,1,0:T(8,128)} %param.7, pred[]{:T(512)S(6)} %lt.15), kind=kLoop, calls=%fused_computation.12 | loop fusion | flops 294912 | bytes 2359297 | tf_op jit(solution)/shard_map/jit(_where)/select_n | solution.py:168
  2.9 1.4 collective-permute-start.3
  4.3 1.3 collective-permute-start
  5.6 4.2 %collective-permute-start.2 = (bf16[192,768]{1,0:T(8,128)(2,1)S(1)}, bf16[192,768]{1,0:T(8,128)(2,1)S(1)}, u32[]{:S(2)}, u32[]{:S(2)}) collective-permute-start(bf16[192,768]{1,0:T(8,128)(2,1)S(1)} %get-tuple-element.32), channel_id=1, source_target_pairs={{0,2},{2,0},{5,7},{7,5},{8,10},{10,8},{13,15},{15,13},{16,18},{18,... | collective-permute-start | bytes 884744 | tf_op jit(solution)/shard_map/ppermute | solution.py:160
  9.8 3.2 %collective-permute-start.5 = (f32[192,768]{1,0:T(8,128)}, f32[192,768]{1,0:T(8,128)S(1)}, u32[]{:S(2)}, u32[]{:S(2)}) collective-permute-start(f32[192,768]{1,0:T(8,128)} %get-tuple-element.30), channel_id=1, source_target_pairs={{0,2},{2,0},{5,7},{7,5},{8,10},{10,8},{13,15},{15,13},{16,18},{18,... | collective-permute-start | bytes 1769480 | tf_op jit(solution)/shard_map/ppermute | solution.py:160
  13.0 0.0 copy-start.17
  13.0 0.0 copy-start
  13.0 1.4 collective-permute-start.1
  14.5 1.1 select_bitcast_fusion.2
  15.6 12.0 %collective-permute-done.ga = bf16[192,768]{1,0:T(8,128)(2,1)S(1)} collective-permute-done((bf16[192,768]{1,0:T(8,128)(2,1)S(1)}, bf16[192,768]{1,0:T(8,128)(2,1)S(1)}, u32[]{:S(2)}, u32[]{:S(2)}) %collective-permute-start) | collective-permute-done | bytes 294944 | tf_op jit(solution)/shard_map/ppermute | solution.py:160
  27.6 1.3 collective-permute-start.4
  28.9 0.0 collective-permute-done.1.gb
  28.9 1.3 collective-permute-start.12
  30.3 5.4 %collective-permute-start.14 = (f32[192,768]{1,0:T(8,128)}, f32[192,768]{1,0:T(8,128)}, u32[]{:S(2)}, u32[]{:S(2)}) collective-permute-start(f32[192,768]{1,0:T(8,128)} %get-tuple-element.26), channel_id=1, source_target_pairs={{0,2},{2,0},{5,7},{7,5},{8,10},{10,8},{13,15},{15,13},{16,18},{18,... | collective-permute-start | bytes 1769480 | tf_op jit(solution)/shard_map/ppermute | solution.py:160
  35.7 0.0 copy-start.4
  35.7 1.3 collective-permute-start.13
  37.0 0.6 fusion.3
  45.2 0.1 select_bitcast_fusion.4
  45.3 1.3 collective-permute-start.9
  46.6 0.0 collective-permute-done.5.fx
  46.6 0.0 copy-start.5
  46.6 2.0 %collective-permute-start.11 = (f32[192,768]{1,0:T(8,128)S(1)}, f32[192,768]{1,0:T(8,128)S(1)}, u32[]{:S(2)}, u32[]{:S(2)}) collective-permute-start(f32[192,768]{1,0:T(8,128)S(1)} %get-tuple-element.28), channel_id=1, source_target_pairs={{0,2},{2,0},{5,7},{7,5},{8,10},{10,8},{13,15},{15,13},{16,18},{18,... | collective-permute-start | bytes 1769480 | tf_op jit(solution)/shard_map/ppermute | solution.py:160
  48.6 4.9 %shard_map.77.factor = f32[768,768]{1,0:T(8,128)} custom-call(s32[4]{0:T(128)} %copy-done.12, bf16[192,768]{1,0:T(8,128)(2,1)} %copy-done.9, bf16[192,768]{1,0:T(8,128)(2,1)} %copy-done.11, bf16[192,768]{1,0:T(8,128)(2,1)} %copy-done.10, bf16[192,768]{1,0:T(8,128)(2,1)} %copy-done.2, f32[192,768]{1,0:T(8,128)} %copy-done.4, ...), custom_call_target="tpu_custom_call" | custom-call | flops 905969664 | bytes 4194304 | tf_op jit(solution)/shard_map/pallas_call | solution.py:135
  53.5 1.6 %constant_dynamic-slice_fusion.2 = (f32[192,768]{1,0:T(8,128)S(1)}, f32[192,768]{1,0:T(8,128)S(1)}, f32[192,768]{1,0:T(8,128)S(1)}) fusion(f32[768,768]{1,0:T(8,128)} %shard_map.77.factor, s32[]{:T(128)S(6)} %select_n.122, s32[]{:T(128)S(6)} %select_n.125, s32[]{:T(128)S(6)} %select_n.124), kind=kLoop, calls=%fused_computation.23 | loop fusion | bytes 3538956 | tf_op jit(solution)/shard_map/dynamic_slice | solution.py:187
  55.1 0.0 collective-permute-done.12.ea
  55.1 1.3 collective-permute-start.10
  56.4 0.0 collective-permute-done.13.eb
  56.4 5.4 %collective-permute-start.7 = (f32[192,768]{1,0:T(8,128)S(1)}, f32[192,768]{1,0:T(8,128)S(1)}, u32[]{:S(2)}, u32[]{:S(2)}) collective-permute-start(f32[192,768]{1,0:T(8,128)S(1)} %get-tuple-element.24), channel_id=1, source_target_pairs={{0,2},{2,0},{5,7},{7,5},{8,10},{10,8},{13,15},{15,13},{16,18},{18,... | collective-permute-start | bytes 1769480 | tf_op jit(solution)/shard_map/ppermute | solution.py:160
  61.8 0.0 collective-permute-done.14.ex
  61.8 2.1 %collective-permute-start.8 = (f32[192,768]{1,0:T(8,128)S(1)}, f32[192,768]{1,0:T(8,128)S(1)}, u32[]{:S(2)}, u32[]{:S(2)}) collective-permute-start(f32[192,768]{1,0:T(8,128)S(1)} %get-tuple-element.23), channel_id=1, source_target_pairs={{2,1},{0,3},{7,6},{5,4},{10,9},{8,11},{15,14},{13,12},{18,17},{16,... | collective-permute-start | bytes 1769480 | tf_op jit(solution)/shard_map/ppermute | solution.py:160
  63.9 43.7 %shard_map.78 = (bf16[768,768]{1,0:T(8,128)(2,1)}, bf16[768,768]{1,0:T(8,128)(2,1)}, f32[768,768]{1,0:T(8,128)}, f32[768,128]{1,0:T(8,128)}) custom-call(s32[4]{0:T(128)} %copy-done.12, f32[768,768]{1,0:T(8,128)} %shard_map.77.factor, f32[192,768]{1,0:T(8,128)} %collective-permute-done.12.ea, f32[192,768]{1,0:T(8,128)} %collective-permute-done.13.eb, ...), custom_call_target="tpu_custom_call" | custom-call | flops 18119393280 | bytes 4194304 | tf_op jit(solution)/shard_map/pallas_call | solution.py:135
  107.6 0.0 collective-permute-done.9.ma
  107.6 1.5 %collective-permute-start.6 = (f32[192,768]{1,0:T(8,128)S(1)}, f32[192,768]{1,0:T(8,128)S(1)}, u32[]{:S(2)}, u32[]{:S(2)}) collective-permute-start(f32[192,768]{1,0:T(8,128)S(1)} %get-tuple-element.22), channel_id=1, source_target_pairs={{0,1},{2,3},{5,6},{7,4},{8,9},{10,11},{13,14},{15,12},{16,17},{18,... | collective-permute-start | bytes 1769480 | tf_op jit(solution)/shard_map/ppermute | solution.py:160
  109.2 0.8 copy-done.15
  110.0 0.2 copy-done.14
  110.2 19.0 %shard_map.79 = (f32[192,768]{1,0:T(8,128)}, f32[192,768]{1,0:T(8,128)}, f32[192,768]{1,0:T(8,128)}, f32[192,768]{1,0:T(8,128)}) custom-call(s32[4]{0:T(128)} %copy-done.12, f32[192,768]{1,0:T(8,128)} %copy-done.13, f32[192,768]{1,0:T(8,128)} %copy-done.15, f32[192,768]{1,0:T(8,128)} %copy-done.14, f32[192,768]{1,0:T(8,128)} %copy-done.6, ...), custom_call_target="tpu_custom_call" | custom-call | flops 5435817984 | bytes 4194304 | tf_op jit(solution)/shard_map/pallas_call | solution.py:135
  129.2 1.3 collective-permute-start.15
  130.6 3.3 %collective-permute-start.16 = (f32[192,768]{1,0:T(8,128)}, f32[192,768]{1,0:T(8,128)S(1)}, u32[]{:S(2)}, u32[]{:S(2)}) collective-permute-start(f32[192,768]{1,0:T(8,128)} %get-tuple-element.16), channel_id=1, source_target_pairs={{0,2},{2,0},{5,7},{7,5},{8,10},{10,8},{13,15},{15,13},{16,18},{18,... | collective-permute-start | bytes 1769480 | tf_op jit(solution)/shard_map/ppermute | solution.py:160
  133.9 1.3 collective-permute-start.17
  135.3 0.0 collective-permute-done.8
  135.3 0.0 collective-permute-done.6
  135.3 1.2 select_bitcast_fusion.7
  136.5 1.1 pad_maximum_fusion
  137.6 0.6 collective-permute-done.15
  138.2 8.1 %collective-permute-done.16 = f32[192,768]{1,0:T(8,128)S(1)} collective-permute-done((f32[192,768]{1,0:T(8,128)}, f32[192,768]{1,0:T(8,128)S(1)}, u32[]{:S(2)}, u32[]{:S(2)}) %collective-permute-start.16) | collective-permute-done | bytes 589856 | tf_op jit(solution)/shard_map/ppermute | solution.py:160
  146.3 0.0 collective-permute-done.17
  146.3 0.2 select_bitcast_fusion.1
  146.5 1.2 fusion
  (39 shorter events, 0.1 us)
Async XLA Ops:
  0.6 3.6 %copy-start.7 = (bf16[2,768,192]{1,2,0:T(8,128)(2,1)S(1)}, bf16[2,768,192]{1,2,0:T(8,128)(2,1)}, u32[]{:S(2)}) copy-start(bf16[2,768,192]{1,2,0:T(8,128)(2,1)} %param.6) | copy-start | bytes 1769476
  2.8 24.8 %copy-start.1 = (f32[192,768]{1,0:T(8,128)}, f32[192,768]{1,0:T(8,128)S(1)}, u32[]{:S(2)}) copy-start(f32[192,768]{1,0:T(8,128)S(1)} %get-tuple-element.29.fo) | copy-start | bytes 1769476
  2.8 11.6 %copy-start.3 = (f32[2,192,768]{2,1,0:T(8,128)S(1)}, f32[2,192,768]{2,1,0:T(8,128)}, u32[]{:S(2)}) copy-start(f32[2,192,768]{2,1,0:T(8,128)} %param.8) | copy-start | bytes 3538948
  2.9 32.8 %collective-permute-start.3 = (f32[192,768]{1,0:T(8,128)}, f32[192,768]{1,0:T(8,128)S(1)}, u32[]{:S(2)}, u32[]{:S(2)}) collective-permute-start(f32[192,768]{1,0:T(8,128)} %get-tuple-element.30), channel_id=1, source_target_pairs={{1,2},{3,0},{6,7},{4,5},{9,10},{11,8},{14,15},{12,13},{17,18},{19,... | collective-permute-start | bytes 1769480 | tf_op jit(solution)/shard_map/ppermute | solution.py:160
  4.3 11.3 %copy-start.2 = (bf16[192,768]{1,0:T(8,128)(2,1)}, bf16[192,768]{1,0:T(8,128)(2,1)S(1)}, u32[]{:S(2)}) copy-start(bf16[192,768]{1,0:T(8,128)(2,1)S(1)} %get-tuple-element.31.go) | copy-start | bytes 884740
  4.3 23.3 %collective-permute-start = (bf16[192,768]{1,0:T(8,128)(2,1)S(1)}, bf16[192,768]{1,0:T(8,128)(2,1)S(1)}, u32[]{:S(2)}, u32[]{:S(2)}) collective-permute-start(bf16[192,768]{1,0:T(8,128)(2,1)S(1)} %get-tuple-element.32), channel_id=1, source_target_pairs={{1,2},{3,0},{6,7},{4,5},{9,10},{11,8},{14,15},{12,13},{17,18},{19,... | collective-permute-start | bytes 884744 | tf_op jit(solution)/shard_map/ppermute | solution.py:160
  5.6 24.6 %collective-permute-start.2 = (bf16[192,768]{1,0:T(8,128)(2,1)S(1)}, bf16[192,768]{1,0:T(8,128)(2,1)S(1)}, u32[]{:S(2)}, u32[]{:S(2)}) collective-permute-start(bf16[192,768]{1,0:T(8,128)(2,1)S(1)} %get-tuple-element.32), channel_id=1, source_target_pairs={{0,2},{2,0},{5,7},{7,5},{8,10},{10,8},{13,15},{15,13},{16,18},{18,... | collective-permute-start | bytes 884744 | tf_op jit(solution)/shard_map/ppermute | solution.py:160
  9.8 36.8 %collective-permute-start.5 = (f32[192,768]{1,0:T(8,128)}, f32[192,768]{1,0:T(8,128)S(1)}, u32[]{:S(2)}, u32[]{:S(2)}) collective-permute-start(f32[192,768]{1,0:T(8,128)} %get-tuple-element.30), channel_id=1, source_target_pairs={{0,2},{2,0},{5,7},{7,5},{8,10},{10,8},{13,15},{15,13},{16,18},{18,... | collective-permute-start | bytes 1769480 | tf_op jit(solution)/shard_map/ppermute | solution.py:160
  13.0 15.9 %copy-start.17 = (s32[4]{0:T(128)S(1)}, s32[4]{0:T(128)}, u32[]{:S(2)}) copy-start(s32[4]{0:T(128)} %constant.33.clone) | copy-start | bytes 52
  13.0 32.1 %copy-start = (f32[2,768,192]{1,2,0:T(8,128)S(1)}, f32[2,768,192]{1,2,0:T(8,128)}, u32[]{:S(2)}) copy-start(f32[2,768,192]{1,2,0:T(8,128)} %param.9) | copy-start | bytes 3538948
  13.0 15.9 %collective-permute-start.1 = (bf16[192,768]{1,0:T(8,128)(2,1)S(1)}, bf16[192,768]{1,0:T(8,128)(2,1)S(1)}, u32[]{:S(2)}, u32[]{:S(2)}) collective-permute-start(bf16[192,768]{1,0:T(8,128)(2,1)S(1)} %get-tuple-element.31.go), channel_id=1, source_target_pairs={{1,0},{3,2},{6,5},{4,7},{9,8},{11,10},{14,13},{12,15},{17,16},{19,... | collective-permute-start | bytes 884744 | tf_op jit(solution)/shard_map/ppermute | solution.py:160
  27.6 17.6 %copy-start.9 = (bf16[192,768]{1,0:T(8,128)(2,1)}, bf16[192,768]{1,0:T(8,128)(2,1)S(1)}, u32[]{:S(2)}) copy-start(bf16[192,768]{1,0:T(8,128)(2,1)S(1)} %collective-permute-done.ga) | copy-start | bytes 884740
  27.6 17.7 %collective-permute-start.4 = (f32[192,768]{1,0:T(8,128)S(1)}, f32[192,768]{1,0:T(8,128)}, u32[]{:S(2)}, u32[]{:S(2)}) collective-permute-start(f32[192,768]{1,0:T(8,128)S(1)} %get-tuple-element.29.fo), channel_id=1, source_target_pairs={{1,0},{3,2},{6,5},{4,7},{9,8},{11,10},{14,13},{12,15},{17,16},{19,... | collective-permute-start | bytes 1769480 | tf_op jit(solution)/shard_map/ppermute | solution.py:160
  28.9 19.7 %copy-start.12 = (s32[4]{0:T(128)}, s32[4]{0:T(128)S(1)}, u32[]{:S(2)}) copy-start(s32[4]{0:T(128)S(1)} %fusion.2.place) | copy-start | bytes 52
  28.9 6.7 %copy-start.11 = (bf16[192,768]{1,0:T(8,128)(2,1)}, bf16[192,768]{1,0:T(8,128)(2,1)S(1)}, u32[]{:S(2)}) copy-start(bf16[192,768]{1,0:T(8,128)(2,1)S(1)} %collective-permute-done.1.gb) | copy-start | bytes 884740
  28.9 26.1 %collective-permute-start.12 = (f32[192,768]{1,0:T(8,128)}, f32[192,768]{1,0:T(8,128)}, u32[]{:S(2)}, u32[]{:S(2)}) collective-permute-start(f32[192,768]{1,0:T(8,128)} %get-tuple-element.26), channel_id=1, source_target_pairs={{1,2},{3,0},{6,7},{4,5},{9,10},{11,8},{14,15},{12,13},{17,18},{19,... | collective-permute-start | bytes 1769480 | tf_op jit(solution)/shard_map/ppermute | solution.py:160
  30.3 5.4 %copy-start.10 = (bf16[192,768]{1,0:T(8,128)(2,1)}, bf16[192,768]{1,0:T(8,128)(2,1)S(1)}, u32[]{:S(2)}) copy-start(bf16[192,768]{1,0:T(8,128)(2,1)S(1)} %collective-permute-done.2.gx) | copy-start | bytes 884740
  30.3 31.5 %collective-permute-start.14 = (f32[192,768]{1,0:T(8,128)}, f32[192,768]{1,0:T(8,128)}, u32[]{:S(2)}, u32[]{:S(2)}) collective-permute-start(f32[192,768]{1,0:T(8,128)} %get-tuple-element.26), channel_id=1, source_target_pairs={{0,2},{2,0},{5,7},{7,5},{8,10},{10,8},{13,15},{15,13},{16,18},{18,... | collective-permute-start | bytes 1769480 | tf_op jit(solution)/shard_map/ppermute | solution.py:160
  35.7 9.6 %copy-start.4 = (f32[192,768]{1,0:T(8,128)}, f32[192,768]{1,0:T(8,128)S(1)}, u32[]{:S(2)}) copy-start(f32[192,768]{1,0:T(8,128)S(1)} %collective-permute-done.3.fa) | copy-start | bytes 1769476
  35.7 20.7 %collective-permute-start.13 = (f32[192,768]{1,0:T(8,128)}, f32[192,768]{1,0:T(8,128)}, u32[]{:S(2)}, u32[]{:S(2)}) collective-permute-start(f32[192,768]{1,0:T(8,128)} %get-tuple-element.25.eo), channel_id=1, source_target_pairs={{1,0},{3,2},{6,5},{4,7},{9,8},{11,10},{14,13},{12,15},{17,16},{19,... | collective-permute-start | bytes 1769480 | tf_op jit(solution)/shard_map/ppermute | solution.py:160
  45.3 9.8 %copy-start.6 = (f32[192,768]{1,0:T(8,128)}, f32[192,768]{1,0:T(8,128)S(1)}, u32[]{:S(2)}) copy-start(f32[192,768]{1,0:T(8,128)S(1)} %get-tuple-element.27.mo) | copy-start | bytes 1769476
  45.3 62.3 %collective-permute-start.9 = (f32[192,768]{1,0:T(8,128)S(1)}, f32[192,768]{1,0:T(8,128)S(1)}, u32[]{:S(2)}, u32[]{:S(2)}) collective-permute-start(f32[192,768]{1,0:T(8,128)S(1)} %get-tuple-element.28), channel_id=1, source_target_pairs={{1,2},{3,0},{6,7},{4,5},{9,10},{11,8},{14,15},{12,13},{17,18},{19,... | collective-permute-start | bytes 1769480 | tf_op jit(solution)/shard_map/ppermute | solution.py:160
  46.6 2.0 %copy-start.5 = (f32[192,768]{1,0:T(8,128)}, f32[192,768]{1,0:T(8,128)S(1)}, u32[]{:S(2)}) copy-start(f32[192,768]{1,0:T(8,128)S(1)} %collective-permute-done.5.fx) | copy-start | bytes 1769476
  46.6 62.6 %collective-permute-start.11 = (f32[192,768]{1,0:T(8,128)S(1)}, f32[192,768]{1,0:T(8,128)S(1)}, u32[]{:S(2)}, u32[]{:S(2)}) collective-permute-start(f32[192,768]{1,0:T(8,128)S(1)} %get-tuple-element.28), channel_id=1, source_target_pairs={{0,2},{2,0},{5,7},{7,5},{8,10},{10,8},{13,15},{15,13},{16,18},{18,... | collective-permute-start | bytes 1769480 | tf_op jit(solution)/shard_map/ppermute | solution.py:160
  55.1 54.1 %collective-permute-start.10 = (f32[192,768]{1,0:T(8,128)S(1)}, f32[192,768]{1,0:T(8,128)S(1)}, u32[]{:S(2)}, u32[]{:S(2)}) collective-permute-start(f32[192,768]{1,0:T(8,128)S(1)} %get-tuple-element.27.mo), channel_id=1, source_target_pairs={{1,0},{3,2},{6,5},{4,7},{9,8},{11,10},{14,13},{12,15},{17,16},{19,... | collective-permute-start | bytes 1769480 | tf_op jit(solution)/shard_map/ppermute | solution.py:160
  56.4 77.5 %collective-permute-start.7 = (f32[192,768]{1,0:T(8,128)S(1)}, f32[192,768]{1,0:T(8,128)S(1)}, u32[]{:S(2)}, u32[]{:S(2)}) collective-permute-start(f32[192,768]{1,0:T(8,128)S(1)} %get-tuple-element.24), channel_id=1, source_target_pairs={{0,2},{2,0},{5,7},{7,5},{8,10},{10,8},{13,15},{15,13},{16,18},{18,... | collective-permute-start | bytes 1769480 | tf_op jit(solution)/shard_map/ppermute | solution.py:160
  61.8 73.5 %collective-permute-start.8 = (f32[192,768]{1,0:T(8,128)S(1)}, f32[192,768]{1,0:T(8,128)S(1)}, u32[]{:S(2)}, u32[]{:S(2)}) collective-permute-start(f32[192,768]{1,0:T(8,128)S(1)} %get-tuple-element.23), channel_id=1, source_target_pairs={{2,1},{0,3},{7,6},{5,4},{10,9},{8,11},{15,14},{13,12},{18,17},{16,... | collective-permute-start | bytes 1769480 | tf_op jit(solution)/shard_map/ppermute | solution.py:160
  107.6 1.6 %copy-start.13 = (f32[192,768]{1,0:T(8,128)}, f32[192,768]{1,0:T(8,128)S(1)}, u32[]{:S(2)}) copy-start(f32[192,768]{1,0:T(8,128)S(1)} %collective-permute-done.9.ma) | copy-start | bytes 1769476
  107.6 27.7 %collective-permute-start.6 = (f32[192,768]{1,0:T(8,128)S(1)}, f32[192,768]{1,0:T(8,128)S(1)}, u32[]{:S(2)}, u32[]{:S(2)}) collective-permute-start(f32[192,768]{1,0:T(8,128)S(1)} %get-tuple-element.22), channel_id=1, source_target_pairs={{0,1},{2,3},{5,6},{7,4},{8,9},{10,11},{13,14},{15,12},{16,17},{18,... | collective-permute-start | bytes 1769480 | tf_op jit(solution)/shard_map/ppermute | solution.py:160
  109.2 0.8 copy-start.15
  109.2 1.0 copy-start.14
  110.2 25.0 %copy-start.16 = (s32[2]{0:T(128)S(1)}, s32[2]{0:T(128)}, u32[]{:S(2)}) copy-start(s32[2]{0:T(128)} %param.10) | copy-start | bytes 28
  129.2 9.0 %collective-permute-start.15 = (f32[192,768]{1,0:T(8,128)}, f32[192,768]{1,0:T(8,128)S(1)}, u32[]{:S(2)}, u32[]{:S(2)}) collective-permute-start(f32[192,768]{1,0:T(8,128)} %get-tuple-element.15), channel_id=1, source_target_pairs={{0,1},{2,3},{5,6},{7,4},{8,9},{10,11},{13,14},{15,12},{16,17},{18,... | collective-permute-start | bytes 1769480 | tf_op jit(solution)/shard_map/ppermute | solution.py:160
  130.6 15.8 %collective-permute-start.16 = (f32[192,768]{1,0:T(8,128)}, f32[192,768]{1,0:T(8,128)S(1)}, u32[]{:S(2)}, u32[]{:S(2)}) collective-permute-start(f32[192,768]{1,0:T(8,128)} %get-tuple-element.16), channel_id=1, source_target_pairs={{0,2},{2,0},{5,7},{7,5},{8,10},{10,8},{13,15},{15,13},{16,18},{18,... | collective-permute-start | bytes 1769480 | tf_op jit(solution)/shard_map/ppermute | solution.py:160
  133.9 12.4 %collective-permute-start.17 = (f32[192,768]{1,0:T(8,128)}, f32[192,768]{1,0:T(8,128)S(1)}, u32[]{:S(2)}, u32[]{:S(2)}) collective-permute-start(f32[192,768]{1,0:T(8,128)} %get-tuple-element.17), channel_id=1, source_target_pairs={{2,1},{0,3},{7,6},{5,4},{10,9},{8,11},{15,14},{13,12},{18,17},{16,... | collective-permute-start | bytes 1769480 | tf_op jit(solution)/shard_map/ppermute | solution.py:160
  136.5 9.8 %copy-start.8 = (f32[192,768]{1,0:T(8,128)S(1)}, f32[192,768]{1,0:T(8,128)}, u32[]{:S(2)}) copy-start(f32[192,768]{1,0:T(8,128)} %get-tuple-element.14) | copy-start | bytes 1769476

commit v2 on v1

v2 whole, which is shorter than its diff:
```python
import functools

import jax
import jax.numpy as jnp
from jax import lax
from jax.experimental import pallas as pl
from jax.experimental.pallas import tpu as pltpu
from jax.sharding import PartitionSpec as P

ema_decay = 0.95
f32 = jnp.float32
bf16 = jnp.bfloat16
LANES = 128
GROUP = 8
NN = (((1,), (0,)), ((), ()))
NT = (((1,), (1,)), ((), ()))
TN = (((0,), (0,)), ((), ()))


def halves(value):
    high = value.astype(bf16)
    return high, (value - high.astype(f32)).astype(bf16)


def dot3(left, right, dims):
    one = functools.partial(lax.dot_general, dimension_numbers=dims, preferred_element_type=f32)
    return one(left[0], right[0]) + (one(left[0], right[1]) + one(left[1], right[0]))


def along_rows(tile, row):
    return jnp.broadcast_to(tile[row : row + 1, :], tile.shape)


def along_lanes(tile, lane):
    return jnp.broadcast_to(tile[:, lane : lane + 1], tile.shape)


def inverse_factor(block, reach=3):
    count = LANES // GROUP
    row_ids = lax.broadcasted_iota(jnp.int32, (GROUP, LANES), 0)
    lane_ids = lax.broadcasted_iota(jnp.int32, (GROUP, LANES), 1)
    tiles = [block[GROUP * i : GROUP * (i + 1), :] for i in range(count)]
    inverse = [(row_ids + GROUP * i == lane_ids).astype(f32) for i in range(count)]
    column = [along_lanes(tiles[0], j) for j in range(GROUP)]
    waiting = []
    for g in range(count):
        tile, inv = tiles[g], inverse[g]
        if waiting:
            waiting.pop(0)()
        near = range(g + 1, min(count, g + reach + 1))
        spread = {t: [along_lanes(tiles[t], GROUP * g + j) for j in range(GROUP)] for t in near}
        if near:
            following = [along_lanes(tiles[g + 1], GROUP * (g + 1) + j) for j in range(GROUP)]
        pivots = jnp.zeros((GROUP, LANES), f32)
        entries, scales, rows = {}, [], []
        for j in range(GROUP):
            pivot = along_rows(column[j], j)
            scale = 1.0 / pivot
            scales.append(scale)
            pivots = jnp.where(row_ids == j, pivot, pivots)
            for m in range(j + 1, GROUP):
                entries[j, m] = along_rows(column[j], m) * scale
                column[m] = column[m] - column[j] * entries[j, m]
            tile_row, inv_row = along_rows(tile, j) * scale, along_rows(inv, j) * scale
            rows.append((tile_row, inv_row))
            below = jnp.where(row_ids > j, column[j], 0.0)
            tile, inv = tile - below * tile_row, inv - below * inv_row
        root = lax.rsqrt(pivots)
        inverse[g] = inv * root
        for t in near:
            col = spread[t]
            tile_t, inv_t = tiles[t], inverse[t]
            for j in range(GROUP):
                for m in range(j + 1, GROUP):
                    col[m] = col[m] - col[j] * entries[j, m]
                if t == g + 1:
                    for m in range(GROUP):
                        following[m] = following[m] - col[j] * (along_rows(col[j], m) * scales[j])
                tile_t = tile_t - col[j] * rows[j][0]
                inv_t = inv_t - col[j] * rows[j][1]
            tiles[t], inverse[t] = tile_t, inv_t
        if near:
            column = following
        while waiting:
            waiting.pop(0)()
        far = g + reach + 1
        if far < count:
            high, low = tile_halves(tile * root)
            inv_high, inv_low = tile_halves(inv * root)
            left = jnp.concatenate([high, high, low], 0).astype(bf16)
            right = jnp.concatenate(
                [jnp.concatenate([high, low, high], 0), jnp.concatenate([inv_high, inv_low, inv_high], 0)], 1
            ).astype(bf16)
            change = lax.dot_general(left, right, TN, preferred_element_type=f32)

            def update(t, change=change):
                tiles[t] = tiles[t] - change[GROUP * t : GROUP * (t + 1), :LANES]
                inverse[t] = inverse[t] - change[GROUP * t : GROUP * (t + 1), LANES:]

            waiting = [functools.partial(update, t) for t in range(far, count)]
    return jnp.concatenate(inverse, 0)


def tile_halves(tile):
    high = tile.astype(bf16).astype(f32)
    return high, tile - high


def eliminate(table, columns, block, beside):
    count = columns // LANES
    for k in range(count):
        here, after = slice(k * LANES, (k + 1) * LANES), (k + 1) * LANES
        inverse = halves(inverse_factor(block))
        if k in beside:
            beside[k]()
        panel = dot3(halves(table[after:, here]), inverse, NT)
        table[after:, here] = panel
        if k + 1 < count:
            high, low = halves(panel)
            strip = (high[:LANES], low[:LANES])
            block = table[after : after + LANES, after : after + LANES] - dot3(strip, strip, NT)
            ahead = columns - after
            table[after:, after:columns] = table[after:, after:columns] - dot3(
                (high, low), (high[:ahead], low[:ahead]), NT
            )


def power_kernel(place, ga, gb, gx, go, pa, pb, px, po, ra, rb, rx, ro, rest, whole, factor, basis, table):
    size, part = factor.shape[0], ra.shape[0]
    half = size // 2
    for i, piece in enumerate((ga, gb, gx, go)):
        whole[part * i : part * (i + 1), :] = piece[...]
    factor[...] = (1.0 - ema_decay) * lax.dot_general(whole[...], whole[...], TN, preferred_element_type=f32)
    for i, (piece, back) in enumerate(((pa, ra), (pb, rb), (px, rx), (po, ro))):
        rows = pl.ds(pl.multiple_of(place[i], 64), part)
        basis[rows, :] = piece[:part, :]
        new = ema_decay * piece[part:, :] + factor[rows, :]
        factor[rows, :] = new
        back[...] = new
    base = halves(basis[...])
    power = halves(dot3(halves(factor[...]), base, NN))
    table[:size, :] = dot3(power, power, TN)

    def spread_basis():
        table[size:, :] = dot3(base, power, TN)

    block = table[:LANES, :LANES]
    eliminate_part(table, size, block, 3, spread_basis)
    rest[:half, :] = table[half:size, half:]
    rest[half : half + size, :] = table[size:, half:]
    rest[half + size :, :] = table[size:, :half]


def eliminate_part(table, size, block, steps, first):
    for k in range(steps):
        here, after = slice(k * LANES, (k + 1) * LANES), (k + 1) * LANES
        inverse = halves(inverse_factor(block))
        if k == 0:
            first()
        panel = dot3(halves(table[after:, here]), inverse, NT)
        table[after:, here] = panel
        high, low = halves(panel)
        ahead = size - after
        if k + 1 < steps:
            strip = (high[:LANES], low[:LANES])
            block = table[after : after + LANES, after : after + LANES] - dot3(strip, strip, NT)
        table[after:, after:size] = table[after:, after:size] - dot3((high, low), (high[:ahead], low[:ahead]), NT)


def rotate_kernel(rest, ma, mb, mx, mo, ra, rb, rx, ro, table, moment, done):
    size, part = moment.shape[0], ra.shape[0]
    half = size // 2
    table[...] = rest[: half + size, :]
    for i, piece in enumerate((ma, mb, mx, mo)):
        moment[part * i : part * (i + 1), :] = piece[...]
    turned = halves(moment[...])

    def early(k):
        here = slice(k * LANES, (k + 1) * LANES)
        done[:, here] = dot3(turned, halves(rest[half + size :, here]), NN)

    eliminate(table, half, table[:LANES, :LANES], {k: functools.partial(early, k) for k in range(half // LANES)})
    done[:, half:] = dot3(turned, halves(table[half:, :]), NN)
    for i, piece in enumerate((ra, rb, rx, ro)):
        piece[...] = done[part * i : part * (i + 1), :]


def call(kernel, outs, scratch, flops, *args, place=None):
    smem = pl.BlockSpec(memory_space=pltpu.SMEM)
    vmem = pl.BlockSpec(memory_space=pltpu.VMEM)
    lead = () if place is None else (place,)
    return pl.pallas_call(
        kernel,
        out_shape=[jax.ShapeDtypeStruct(shape, dtype) for shape, dtype in outs],
        in_specs=[smem] * len(lead) + [vmem] * len(args),
        out_specs=[vmem] * len(outs),
        scratch_shapes=[pltpu.VMEM(shape, dtype) for shape, dtype in scratch],
        cost_estimate=pl.CostEstimate(flops=flops, bytes_accessed=1 << 22, transcendentals=0),
        compiler_params=pltpu.CompilerParams(vmem_limit_bytes=56 << 20),
    )(*lead, *args)


def power_call(place, gradient_parts, pair_parts):
    part, size = gradient_parts[0].shape
    whole = (size, size)
    outs = [((part, size), f32)] * 4 + [((size // 2 + 2 * size, size // 2), f32)]
    scratch = [(whole, bf16), (whole, f32), (whole, f32), ((2 * size, size), f32)]
    return call(power_kernel, outs, scratch, 30 * size**3, *gradient_parts, *pair_parts, place=place)


def rotate_call(rest, moment_parts):
    part, size = moment_parts[0].shape
    whole = (size, size)
    outs = [((part, size), f32)] * 4
    scratch = [((size // 2 + size, size // 2), f32), (whole, f32), (whole, f32)]
    return call(rotate_kernel, outs, scratch, 20 * size**3, rest, *moment_parts)


def on_device(gradient, factor, eigenbasis, moment, refresh_due):
    part, size = factor.shape[1], factor.shape[2]
    groups, ring = lax.axis_size("dp"), lax.axis_size("tensor")
    core = lax.rem(lax.axis_index("dp"), 2)
    position = lax.axis_index("tensor")
    role = lax.rem(position - core + ring, ring)
    owns = lax.rem(role, 2) == 0

    def exchange(value, roles):
        pairs = [
            (d * ring + (a + d % 2) % ring, d * ring + (b + d % 2) % ring)
            for d in range(groups)
            for a, b in roles
        ]
        return lax.ppermute(value, ("dp", "tensor"), pairs)

    up, down, across = [(1, 2), (3, 0)], [(1, 0), (3, 2)], [(0, 2), (2, 0)]
    up_back, down_back = [(2, 1), (0, 3)], [(0, 1), (2, 3)]
    first_is_1 = role < 2

    def choose(value):
        return jnp.where(first_is_1, value[1], value[0]), jnp.where(first_is_1, value[0], value[1])

    def send(first, second):
        return exchange(first, up), exchange(second, down), exchange(first, across), second

    def collect(value):
        return send(*choose(value))

    def give_back(pieces):
        first = jnp.where(owns, exchange(pieces[2], across), exchange(pieces[0], up_back))
        second = jnp.where(owns, pieces[3], exchange(pieces[1], down_back))
        return jnp.stack([jnp.where(first_is_1, second, first), jnp.where(first_is_1, first, second)])

    place = lax.rem(position + jnp.array([3, 1, 2, 0], jnp.int32), ring) * part

    pair_parts = collect(jnp.concatenate([eigenbasis, factor], 1))
    gradient_parts = collect(jnp.swapaxes(gradient, 1, 2))
    turned = choose(jnp.swapaxes(moment, 1, 2))
    turned, pair_parts = lax.optimization_barrier((turned, pair_parts))
    moment_parts = send(*turned)
    *factor_parts, rest = power_call(place, gradient_parts, pair_parts)
    factor_new = give_back(factor_parts)
    rotated_parts = rotate_call(rest, moment_parts)
    rotated = jnp.swapaxes(give_back(rotated_parts), 1, 2)
    moment_new = jnp.where((refresh_due > 0)[:, None, None], rotated, moment)
    return factor_new, moment_new


def solution(mesh):
    placed = (
        P("dp", None, "tensor"),
        P("dp", "tensor", None),
        P("dp", "tensor", None),
        P("dp", None, "tensor"),
        P("dp"),
    )
    return jax.shard_map(
        on_device,
        mesh=mesh,
        in_specs=placed,
        out_specs=(P("dp", "tensor", None), P("dp", None, "tensor")),
        check_vma=False,
    )
```

time: 149 us -> 126 us (0.85)
  Pallas kernels: 67.6 us -> 49 us
  waiting for transfers between devices: 20.7 us -> 29.2 us
  between operations: 8.66 us -> 0.98 us
  starting transfers between devices: 40.3 us -> 36.1 us
  other arithmetic: 7.15 us -> 5.27 us
    pallas_call x3 -> x2, Pallas kernels: 67.6 us -> 49 us  [call(): pl.pallas_call(kernel, out_shape=[jax.ShapeDtypeStruct(shape, dtype) for...]
    ppermute x18 -> x15, waiting for transfers between devices: 20.7 us -> 29.2 us  [exchange(): return lax.ppermute(value, ('dp', 'tensor'), pairs)]
    ppermute x18 -> x15, starting transfers between devices: 40.3 us -> 36.1 us  [exchange(): return lax.ppermute(value, ('dp', 'tensor'), pairs)]
    dynamic_slice x1 -> x0, local copies, waits for them, and re-layouts: 1.59 us -> none  [on_device(): lax.dynamic_slice_in_dim(factor_whole, place[i], part, 0)]
    unnamed x36 -> x27, local copies, waits for them, and re-layouts: 1.06 us -> 2.62 us
    select_n x4 -> x3, other arithmetic: 3.44 us -> 2.14 us  [choose(): jnp.where(first_is_1, value[0], value[1])]
  transfers between devices with their start and end apart: 18 -> 15, of which waited for: 3 -> 4; matrix products, arithmetic and copies ran while one was open for 4% -> 2% of each run, Pallas kernels for 46% -> 40%
where the time goes in v2:
time: 126 us; the launch traced here: 123 us
  Pallas kernels  49 us (39%)
  starting transfers between devices  36.1 us (29%)
  waiting for transfers between devices  29.2 us (23%)
  other arithmetic  5.27 us (4%)
  local copies, waits for them, and re-layouts  2.7 us (2%)
    pallas_call x2, Pallas kernels, call(): pl.pallas_call(kernel, out_shape=[jax.ShapeDtypeStruct(shape, dtype) for...  49 us
    ppermute x15, starting transfers between devices, exchange(): return lax.ppermute(value, ('dp', 'tensor'), pairs)  36.1 us
    ppermute x15, waiting for transfers between devices, exchange(): return lax.ppermute(value, ('dp', 'tensor'), pairs)  29.2 us
    unnamed x27, local copies, waits for them, and re-layouts  2.62 us
  transfers between devices with their start and end apart: 15, of which 4 were waited for; matrix products, arithmetic and copies ran while one was open for 2% of the time, Pallas kernels for 40%

profile of v2, /device:TPU:4, one launch (start us, length us, event | category | flops | bytes accessed | tf_op | source)
XLA Modules:
  0.0 123.2 jit_solution(6619958514828596723)
XLA Ops:
  0.6 0.0 copy-start.2
  0.6 1.4 %constant_dynamic-update-slice_fusion.1 = f32[2,384,768]{2,1,0:T(8,128)S(1)} fusion(f32[2,192,768]{2,1,0:T(8,128)} %param.8), kind=kLoop, calls=%fused_computation.18 | loop fusion | bytes 2359296
  2.1 0.2 copy-done.2
  2.3 0.1 constant_dynamic-update-slice_fusion
  2.3 0.0 copy-start.4
  2.4 1.2 select_bitcast_fusion
  3.5 1.5 %collective-permute-start.3 = (f32[384,768]{1,0:T(8,128)}, f32[384,768]{1,0:T(8,128)S(1)}, u32[]{:S(2)}, u32[]{:S(2)}) collective-permute-start(f32[384,768]{1,0:T(8,128)} %get-tuple-element.37), channel_id=1, source_target_pairs={{1,2},{3,0},{6,7},{4,5},{9,10},{11,8},{14,15},{12,13},{17,18},{19,... | collective-permute-start | bytes 3538952 | tf_op jit(solution)/shard_map/ppermute | solution.py:233
  5.1 1.3 %collective-permute-start.4 = (f32[384,768]{1,0:T(8,128)S(1)}, f32[384,768]{1,0:T(8,128)}, u32[]{:S(2)}, u32[]{:S(2)}) collective-permute-start(f32[384,768]{1,0:T(8,128)S(1)} %get-tuple-element.20.po), channel_id=1, source_target_pairs={{1,0},{3,2},{6,5},{4,7},{9,8},{11,10},{14,13},{12,15},{17,16},{19,... | collective-permute-start | bytes 3538952 | tf_op jit(solution)/shard_map/ppermute | solution.py:233
  6.4 4.2 %collective-permute-start.5 = (f32[384,768]{1,0:T(8,128)}, f32[384,768]{1,0:T(8,128)}, u32[]{:S(2)}, u32[]{:S(2)}) collective-permute-start(f32[384,768]{1,0:T(8,128)} %get-tuple-element.37), channel_id=1, source_target_pairs={{0,2},{2,0},{5,7},{7,5},{8,10},{10,8},{13,15},{15,13},{16,18},{18,... | collective-permute-start | bytes 3538952 | tf_op jit(solution)/shard_map/ppermute | solution.py:233
  10.6 0.9 select_bitcast_fusion.8
  11.4 1.3 %collective-permute-start = (bf16[192,768]{1,0:T(8,128)(2,1)}, bf16[192,768]{1,0:T(8,128)(2,1)}, u32[]{:S(2)}, u32[]{:S(2)}) collective-permute-start(bf16[192,768]{1,0:T(8,128)(2,1)} %get-tuple-element.41), channel_id=1, source_target_pairs={{1,2},{3,0},{6,7},{4,5},{9,10},{11,8},{14,15},{12,13},{17,18},{19,... | collective-permute-start | bytes 884744 | tf_op jit(solution)/shard_map/ppermute | solution.py:233
  12.7 3.2 %collective-permute-start.2 = (bf16[192,768]{1,0:T(8,128)(2,1)}, bf16[192,768]{1,0:T(8,128)(2,1)}, u32[]{:S(2)}, u32[]{:S(2)}) collective-permute-start(bf16[192,768]{1,0:T(8,128)(2,1)} %get-tuple-element.41), channel_id=1, source_target_pairs={{0,2},{2,0},{5,7},{7,5},{8,10},{10,8},{13,15},{15,13},{16,18},{18,... | collective-permute-start | bytes 884744 | tf_op jit(solution)/shard_map/ppermute | solution.py:233
  15.9 14.6 %collective-permute-done.3.pa = f32[384,768]{1,0:T(8,128)S(1)} collective-permute-done((f32[384,768]{1,0:T(8,128)}, f32[384,768]{1,0:T(8,128)S(1)}, u32[]{:S(2)}, u32[]{:S(2)}) %collective-permute-start.3) | collective-permute-done | bytes 1179680 | tf_op jit(solution)/shard_map/ppermute | solution.py:233
  30.6 1.3 %collective-permute-start.1 = (bf16[192,768]{1,0:T(8,128)(2,1)}, bf16[192,768]{1,0:T(8,128)(2,1)}, u32[]{:S(2)}, u32[]{:S(2)}) collective-permute-start(bf16[192,768]{1,0:T(8,128)(2,1)} %get-tuple-element.40.go), channel_id=1, source_target_pairs={{1,0},{3,2},{6,5},{4,7},{9,8},{11,10},{14,13},{12,15},{17,16},{19,... | collective-permute-start | bytes 884744 | tf_op jit(solution)/shard_map/ppermute | solution.py:233
  31.9 0.5 fusion.2.place
  32.4 0.1 select_bitcast_fusion.6
  32.5 4.8 %collective-permute-done.4.pb = f32[384,768]{1,0:T(8,128)} collective-permute-done((f32[384,768]{1,0:T(8,128)S(1)}, f32[384,768]{1,0:T(8,128)}, u32[]{:S(2)}, u32[]{:S(2)}) %collective-permute-start.4) | collective-permute-done | bytes 1179680 | tf_op jit(solution)/shard_map/ppermute | solution.py:233
  37.3 0.0 collective-permute-done.5.px
  37.3 4.2 %collective-permute-start.11 = (f32[192,768]{1,0:T(8,128)S(1)}, f32[192,768]{1,0:T(8,128)S(1)}, u32[]{:S(2)}, u32[]{:S(2)}) collective-permute-start(f32[192,768]{1,0:T(8,128)S(1)} %get-tuple-element.26), channel_id=1, source_target_pairs={{0,2},{2,0},{5,7},{7,5},{8,10},{10,8},{13,15},{15,13},{16,18},{18,... | collective-permute-start | bytes 1769480 | tf_op jit(solution)/shard_map/ppermute | solution.py:233
  41.6 1.3 %collective-permute-start.9 = (f32[192,768]{1,0:T(8,128)S(1)}, f32[192,768]{1,0:T(8,128)S(1)}, u32[]{:S(2)}, u32[]{:S(2)}) collective-permute-start(f32[192,768]{1,0:T(8,128)S(1)} %get-tuple-element.26), channel_id=1, source_target_pairs={{1,2},{3,0},{6,7},{4,5},{9,10},{11,8},{14,15},{12,13},{17,18},{19,... | collective-permute-start | bytes 1769480 | tf_op jit(solution)/shard_map/ppermute | solution.py:233
  42.9 0.0 collective-permute-done.ga
  42.9 1.3 %collective-permute-start.10 = (f32[192,768]{1,0:T(8,128)S(1)}, f32[192,768]{1,0:T(8,128)S(1)}, u32[]{:S(2)}, u32[]{:S(2)}) collective-permute-start(f32[192,768]{1,0:T(8,128)S(1)} %get-tuple-element.27.mo), channel_id=1, source_target_pairs={{1,0},{3,2},{6,5},{4,7},{9,8},{11,10},{14,13},{12,15},{17,16},{19,... | collective-permute-start | bytes 1769480 | tf_op jit(solution)/shard_map/ppermute | solution.py:233
  44.2 0.0 collective-permute-done.1.gb
  44.2 0.0 collective-permute-done.2.gx
  44.2 30.5 %shard_map.77 = (f32[192,768]{1,0:T(8,128)}, f32[192,768]{1,0:T(8,128)}, f32[192,768]{1,0:T(8,128)}, f32[192,768]{1,0:T(8,128)}, f32[1920,384]{1,0:T(8,128)}) custom-call(s32[4]{0:T(128)} %fusion.2.place, bf16[192,768]{1,0:T(8,128)(2,1)} %collective-permute-done.ga, bf16[192,768]{1,0:T(8,128)(2,1)} %collective-permute-done.1.gb, ...), custom_call_target="tpu_custom_call" | custom-call | flops 13589544960 | bytes 4194304 | tf_op jit(solution)/shard_map/pallas_call | solution.py:192
  74.7 5.0 %collective-permute-start.6 = (f32[192,768]{1,0:T(8,128)}, f32[192,768]{1,0:T(8,128)S(1)}, u32[]{:S(2)}, u32[]{:S(2)}) collective-permute-start(f32[192,768]{1,0:T(8,128)} %get-tuple-element.22), channel_id=1, source_target_pairs={{0,1},{2,3},{5,6},{7,4},{8,9},{10,11},{13,14},{15,12},{16,17},{18,... | collective-permute-start | bytes 1769480 | tf_op jit(solution)/shard_map/ppermute | solution.py:233
  79.7 3.3 %collective-permute-start.7 = (f32[192,768]{1,0:T(8,128)}, f32[192,768]{1,0:T(8,128)S(1)}, u32[]{:S(2)}, u32[]{:S(2)}) collective-permute-start(f32[192,768]{1,0:T(8,128)} %get-tuple-element.23), channel_id=1, source_target_pairs={{0,2},{2,0},{5,7},{7,5},{8,10},{10,8},{13,15},{15,13},{16,18},{18,... | collective-permute-start | bytes 1769480 | tf_op jit(solution)/shard_map/ppermute | solution.py:233
  82.9 0.0 collective-permute-done.10.mb
  83.0 1.5 %collective-permute-start.8 = (f32[192,768]{1,0:T(8,128)}, f32[192,768]{1,0:T(8,128)S(1)}, u32[]{:S(2)}, u32[]{:S(2)}) collective-permute-start(f32[192,768]{1,0:T(8,128)} %get-tuple-element.24), channel_id=1, source_target_pairs={{2,1},{0,3},{7,6},{5,4},{10,9},{8,11},{15,14},{13,12},{18,17},{16,... | collective-permute-start | bytes 1769480 | tf_op jit(solution)/shard_map/ppermute | solution.py:233
  84.5 0.0 collective-permute-done.11.mx
  84.5 0.0 collective-permute-done.9.ma
  84.5 0.0 copy-start.9
  84.6 0.8 copy-done.8
  85.3 0.2 copy-done.9
  85.5 18.5 %shard_map.78 = (f32[192,768]{1,0:T(8,128)}, f32[192,768]{1,0:T(8,128)}, f32[192,768]{1,0:T(8,128)}, f32[192,768]{1,0:T(8,128)}) custom-call(f32[1920,384]{1,0:T(8,128)} %get-tuple-element.25.rest, f32[192,768]{1,0:T(8,128)} %copy-done.9, f32[192,768]{1,0:T(8,128)} %copy-done.10, f32[192,768]{1,0:T(8,128)} %copy-done.8, f32[192,768]{1,0:T(8,128)} %copy-done.3), custom_call_target="tpu_custom_call" | custom-call | flops 9059696640 | bytes 4194304 | tf_op jit(solution)/shard_map/pallas_call | solution.py:192
  104.0 1.3 %collective-permute-start.12 = (f32[192,768]{1,0:T(8,128)}, f32[192,768]{1,0:T(8,128)S(1)}, u32[]{:S(2)}, u32[]{:S(2)}) collective-permute-start(f32[192,768]{1,0:T(8,128)} %get-tuple-element.29), channel_id=1, source_target_pairs={{0,1},{2,3},{5,6},{7,4},{8,9},{10,11},{13,14},{15,12},{16,17},{18,... | collective-permute-start | bytes 1769480 | tf_op jit(solution)/shard_map/ppermute | solution.py:233
  105.3 4.1 %collective-permute-start.13 = (f32[192,768]{1,0:T(8,128)}, f32[192,768]{1,0:T(8,128)S(1)}, u32[]{:S(2)}, u32[]{:S(2)}) collective-permute-start(f32[192,768]{1,0:T(8,128)} %get-tuple-element.30), channel_id=1, source_target_pairs={{0,2},{2,0},{5,7},{7,5},{8,10},{10,8},{13,15},{15,13},{16,18},{18,... | collective-permute-start | bytes 1769480 | tf_op jit(solution)/shard_map/ppermute | solution.py:233
  109.4 0.0 collective-permute-done.6
  109.4 1.3 %collective-permute-start.14 = (f32[192,768]{1,0:T(8,128)}, f32[192,768]{1,0:T(8,128)S(1)}, u32[]{:S(2)}, u32[]{:S(2)}) collective-permute-start(f32[192,768]{1,0:T(8,128)} %get-tuple-element.31), channel_id=1, source_target_pairs={{2,1},{0,3},{7,6},{5,4},{10,9},{8,11},{15,14},{13,12},{18,17},{16,... | collective-permute-start | bytes 1769480 | tf_op jit(solution)/shard_map/ppermute | solution.py:233
  110.8 0.0 collective-permute-done.7
  110.8 0.0 collective-permute-done.8
  110.8 0.1 select_bitcast_fusion.5
  111.0 1.1 pad_maximum_fusion
  112.1 0.9 collective-permute-done.12
  113.0 8.8 %collective-permute-done.13 = f32[192,768]{1,0:T(8,128)S(1)} collective-permute-done((f32[192,768]{1,0:T(8,128)}, f32[192,768]{1,0:T(8,128)S(1)}, u32[]{:S(2)}, u32[]{:S(2)}) %collective-permute-start.13) | collective-permute-done | bytes 589856 | tf_op jit(solution)/shard_map/ppermute | solution.py:233
  121.8 0.0 collective-permute-done.14
  121.8 0.1 select_bitcast_fusion.3
  122.0 1.2 fusion
  (21 shorter events, 0.0 us)
Async XLA Ops:
  0.6 1.6 %copy-start.2 = (f32[2,192,768]{2,1,0:T(8,128)S(1)}, f32[2,192,768]{2,1,0:T(8,128)}, u32[]{:S(2)}) copy-start(f32[2,192,768]{2,1,0:T(8,128)} %param.7) | copy-start | bytes 3538948
  2.3 8.2 %copy-start.4 = (bf16[2,768,192]{1,2,0:T(8,128)(2,1)S(1)}, bf16[2,768,192]{1,2,0:T(8,128)(2,1)}, u32[]{:S(2)}) copy-start(bf16[2,768,192]{1,2,0:T(8,128)(2,1)} %param.6) | copy-start | bytes 1769476
  3.5 28.9 %copy-start.1 = (f32[384,768]{1,0:T(8,128)}, f32[384,768]{1,0:T(8,128)S(1)}, u32[]{:S(2)}) copy-start(f32[384,768]{1,0:T(8,128)S(1)} %get-tuple-element.20.po) | copy-start | bytes 3538948
  3.5 28.3 %copy-start.12 = (s32[4]{0:T(128)S(1)}, s32[4]{0:T(128)}, u32[]{:S(2)}) copy-start(s32[4]{0:T(128)} %constant.31.clone) | copy-start | bytes 52
  3.5 28.8 %copy-start = (f32[2,768,192]{1,2,0:T(8,128)S(1)}, f32[2,768,192]{1,2,0:T(8,128)}, u32[]{:S(2)}) copy-start(f32[2,768,192]{1,2,0:T(8,128)} %param.9) | copy-start | bytes 3538948
  3.5 27.0 %collective-permute-start.3 = (f32[384,768]{1,0:T(8,128)}, f32[384,768]{1,0:T(8,128)S(1)}, u32[]{:S(2)}, u32[]{:S(2)}) collective-permute-start(f32[384,768]{1,0:T(8,128)} %get-tuple-element.37), channel_id=1, source_target_pairs={{1,2},{3,0},{6,7},{4,5},{9,10},{11,8},{14,15},{12,13},{17,18},{19,... | collective-permute-start | bytes 3538952 | tf_op jit(solution)/shard_map/ppermute | solution.py:233
  5.1 32.2 %collective-permute-start.4 = (f32[384,768]{1,0:T(8,128)S(1)}, f32[384,768]{1,0:T(8,128)}, u32[]{:S(2)}, u32[]{:S(2)}) collective-permute-start(f32[384,768]{1,0:T(8,128)S(1)} %get-tuple-element.20.po), channel_id=1, source_target_pairs={{1,0},{3,2},{6,5},{4,7},{9,8},{11,10},{14,13},{12,15},{17,16},{19,... | collective-permute-start | bytes 3538952 | tf_op jit(solution)/shard_map/ppermute | solution.py:233
  6.4 30.9 %collective-permute-start.5 = (f32[384,768]{1,0:T(8,128)}, f32[384,768]{1,0:T(8,128)}, u32[]{:S(2)}, u32[]{:S(2)}) collective-permute-start(f32[384,768]{1,0:T(8,128)} %get-tuple-element.37), channel_id=1, source_target_pairs={{0,2},{2,0},{5,7},{7,5},{8,10},{10,8},{13,15},{15,13},{16,18},{18,... | collective-permute-start | bytes 3538952 | tf_op jit(solution)/shard_map/ppermute | solution.py:233
  11.4 31.4 %collective-permute-start = (bf16[192,768]{1,0:T(8,128)(2,1)}, bf16[192,768]{1,0:T(8,128)(2,1)}, u32[]{:S(2)}, u32[]{:S(2)}) collective-permute-start(bf16[192,768]{1,0:T(8,128)(2,1)} %get-tuple-element.41), channel_id=1, source_target_pairs={{1,2},{3,0},{6,7},{4,5},{9,10},{11,8},{14,15},{12,13},{17,18},{19,... | collective-permute-start | bytes 884744 | tf_op jit(solution)/shard_map/ppermute | solution.py:233
  12.7 31.5 %collective-permute-start.2 = (bf16[192,768]{1,0:T(8,128)(2,1)}, bf16[192,768]{1,0:T(8,128)(2,1)}, u32[]{:S(2)}, u32[]{:S(2)}) collective-permute-start(bf16[192,768]{1,0:T(8,128)(2,1)} %get-tuple-element.41), channel_id=1, source_target_pairs={{0,2},{2,0},{5,7},{7,5},{8,10},{10,8},{13,15},{15,13},{16,18},{18,... | collective-permute-start | bytes 884744 | tf_op jit(solution)/shard_map/ppermute | solution.py:233
  30.6 1.8 %copy-start.7 = (f32[384,768]{1,0:T(8,128)}, f32[384,768]{1,0:T(8,128)S(1)}, u32[]{:S(2)}) copy-start(f32[384,768]{1,0:T(8,128)S(1)} %collective-permute-done.3.pa) | copy-start | bytes 3538948
  30.6 13.6 %collective-permute-start.1 = (bf16[192,768]{1,0:T(8,128)(2,1)}, bf16[192,768]{1,0:T(8,128)(2,1)}, u32[]{:S(2)}, u32[]{:S(2)}) collective-permute-start(bf16[192,768]{1,0:T(8,128)(2,1)} %get-tuple-element.40.go), channel_id=1, source_target_pairs={{1,0},{3,2},{6,5},{4,7},{9,8},{11,10},{14,13},{12,15},{17,16},{19,... | collective-permute-start | bytes 884744 | tf_op jit(solution)/shard_map/ppermute | solution.py:233
  32.5 42.2 %copy-start.3 = (f32[192,768]{1,0:T(8,128)}, f32[192,768]{1,0:T(8,128)S(1)}, u32[]{:S(2)}) copy-start(f32[192,768]{1,0:T(8,128)S(1)} %get-tuple-element.27.mo) | copy-start | bytes 1769476
  37.3 47.2 %collective-permute-start.11 = (f32[192,768]{1,0:T(8,128)S(1)}, f32[192,768]{1,0:T(8,128)S(1)}, u32[]{:S(2)}, u32[]{:S(2)}) collective-permute-start(f32[192,768]{1,0:T(8,128)S(1)} %get-tuple-element.26), channel_id=1, source_target_pairs={{0,2},{2,0},{5,7},{7,5},{8,10},{10,8},{13,15},{15,13},{16,18},{18,... | collective-permute-start | bytes 1769480 | tf_op jit(solution)/shard_map/ppermute | solution.py:233
  41.6 43.0 %collective-permute-start.9 = (f32[192,768]{1,0:T(8,128)S(1)}, f32[192,768]{1,0:T(8,128)S(1)}, u32[]{:S(2)}, u32[]{:S(2)}) collective-permute-start(f32[192,768]{1,0:T(8,128)S(1)} %get-tuple-element.26), channel_id=1, source_target_pairs={{1,2},{3,0},{6,7},{4,5},{9,10},{11,8},{14,15},{12,13},{17,18},{19,... | collective-permute-start | bytes 1769480 | tf_op jit(solution)/shard_map/ppermute | solution.py:233
  42.9 40.1 %collective-permute-start.10 = (f32[192,768]{1,0:T(8,128)S(1)}, f32[192,768]{1,0:T(8,128)S(1)}, u32[]{:S(2)}, u32[]{:S(2)}) collective-permute-start(f32[192,768]{1,0:T(8,128)S(1)} %get-tuple-element.27.mo), channel_id=1, source_target_pairs={{1,0},{3,2},{6,5},{4,7},{9,8},{11,10},{14,13},{12,15},{17,16},{19,... | collective-permute-start | bytes 1769480 | tf_op jit(solution)/shard_map/ppermute | solution.py:233
  74.7 34.7 %collective-permute-start.6 = (f32[192,768]{1,0:T(8,128)}, f32[192,768]{1,0:T(8,128)S(1)}, u32[]{:S(2)}, u32[]{:S(2)}) collective-permute-start(f32[192,768]{1,0:T(8,128)} %get-tuple-element.22), channel_id=1, source_target_pairs={{0,1},{2,3},{5,6},{7,4},{8,9},{10,11},{13,14},{15,12},{16,17},{18,... | collective-permute-start | bytes 1769480 | tf_op jit(solution)/shard_map/ppermute | solution.py:233
  79.7 31.1 %collective-permute-start.7 = (f32[192,768]{1,0:T(8,128)}, f32[192,768]{1,0:T(8,128)S(1)}, u32[]{:S(2)}, u32[]{:S(2)}) collective-permute-start(f32[192,768]{1,0:T(8,128)} %get-tuple-element.23), channel_id=1, source_target_pairs={{0,2},{2,0},{5,7},{7,5},{8,10},{10,8},{13,15},{15,13},{16,18},{18,... | collective-permute-start | bytes 1769480 | tf_op jit(solution)/shard_map/ppermute | solution.py:233
  82.9 1.6 %copy-start.10 = (f32[192,768]{1,0:T(8,128)}, f32[192,768]{1,0:T(8,128)S(1)}, u32[]{:S(2)}) copy-start(f32[192,768]{1,0:T(8,128)S(1)} %collective-permute-done.10.mb) | copy-start | bytes 1769476
  83.0 27.8 %collective-permute-start.8 = (f32[192,768]{1,0:T(8,128)}, f32[192,768]{1,0:T(8,128)S(1)}, u32[]{:S(2)}, u32[]{:S(2)}) collective-permute-start(f32[192,768]{1,0:T(8,128)} %get-tuple-element.24), channel_id=1, source_target_pairs={{2,1},{0,3},{7,6},{5,4},{10,9},{8,11},{15,14},{13,12},{18,17},{16,... | collective-permute-start | bytes 1769480 | tf_op jit(solution)/shard_map/ppermute | solution.py:233
  84.5 0.8 copy-start.8
  84.5 1.0 copy-start.9
  85.5 25.2 %copy-start.11 = (s32[2]{0:T(128)S(1)}, s32[2]{0:T(128)}, u32[]{:S(2)}) copy-start(s32[2]{0:T(128)} %param.10) | copy-start | bytes 28
  85.5 25.3 %copy-start.5 = (f32[192,768]{1,0:T(8,128)S(1)}, f32[192,768]{1,0:T(8,128)}, u32[]{:S(2)}) copy-start(f32[192,768]{1,0:T(8,128)} %get-tuple-element.21) | copy-start | bytes 1769476
  104.0 9.0 %collective-permute-start.12 = (f32[192,768]{1,0:T(8,128)}, f32[192,768]{1,0:T(8,128)S(1)}, u32[]{:S(2)}, u32[]{:S(2)}) collective-permute-start(f32[192,768]{1,0:T(8,128)} %get-tuple-element.29), channel_id=1, source_target_pairs={{0,1},{2,3},{5,6},{7,4},{8,9},{10,11},{13,14},{15,12},{16,17},{18,... | collective-permute-start | bytes 1769480 | tf_op jit(solution)/shard_map/ppermute | solution.py:233
  105.3 16.5 %collective-permute-start.13 = (f32[192,768]{1,0:T(8,128)}, f32[192,768]{1,0:T(8,128)S(1)}, u32[]{:S(2)}, u32[]{:S(2)}) collective-permute-start(f32[192,768]{1,0:T(8,128)} %get-tuple-element.30), channel_id=1, source_target_pairs={{0,2},{2,0},{5,7},{7,5},{8,10},{10,8},{13,15},{15,13},{16,18},{18,... | collective-permute-start | bytes 1769480 | tf_op jit(solution)/shard_map/ppermute | solution.py:233
  109.4 12.4 %collective-permute-start.14 = (f32[192,768]{1,0:T(8,128)}, f32[192,768]{1,0:T(8,128)S(1)}, u32[]{:S(2)}, u32[]{:S(2)}) collective-permute-start(f32[192,768]{1,0:T(8,128)} %get-tuple-element.31), channel_id=1, source_target_pairs={{2,1},{0,3},{7,6},{5,4},{10,9},{8,11},{15,14},{13,12},{18,17},{16,... | collective-permute-start | bytes 1769480 | tf_op jit(solution)/shard_map/ppermute | solution.py:233
  111.0 10.9 %copy-start.6 = (f32[192,768]{1,0:T(8,128)S(1)}, f32[192,768]{1,0:T(8,128)}, u32[]{:S(2)}) copy-start(f32[192,768]{1,0:T(8,128)} %get-tuple-element.28) | copy-start | bytes 1769476

commit v3 on v2

--- a/solution.py
+++ b/solution.py
@@ -35,7 +35,8 @@
     return jnp.broadcast_to(tile[:, lane : lane + 1], tile.shape)
 
 
-def inverse_factor(block, reach=3):
+def inverse_factor(block, beside=(), reach=3):
+    beside = list(beside)
     count = LANES // GROUP
     row_ids = lax.broadcasted_iota(jnp.int32, (GROUP, LANES), 0)
     lane_ids = lax.broadcasted_iota(jnp.int32, (GROUP, LANES), 1)
@@ -44,6 +45,8 @@
     column = [along_lanes(tiles[0], j) for j in range(GROUP)]
     waiting = []
     for g in range(count):
+        for _ in range(-(-len(beside) // (count - g))):
+            beside.pop(0)()
         tile, inv = tiles[g], inverse[g]
         if waiting:
             waiting.pop(0)()
@@ -56,10 +59,11 @@
         for j in range(GROUP):
             pivot = along_rows(column[j], j)
             scale = 1.0 / pivot
+            pivots = jnp.where(row_ids == j, pivot, pivots)
+            scaled = column[j] * scale
             scales.append(scale)
-            pivots = jnp.where(row_ids == j, pivot, pivots)
             for m in range(j + 1, GROUP):
-                entries[j, m] = along_rows(column[j], m) * scale
+                entries[j, m] = along_rows(scaled, m)
                 column[m] = column[m] - column[j] * entries[j, m]
             tile_row, inv_row = along_rows(tile, j) * scale, along_rows(inv, j) * scale
             rows.append((tile_row, inv_row))
@@ -74,8 +78,9 @@
                 for m in range(j + 1, GROUP):
                     col[m] = col[m] - col[j] * entries[j, m]
                 if t == g + 1:
+                    scaled = col[j] * scales[j]
                     for m in range(GROUP):
-                        following[m] = following[m] - col[j] * (along_rows(col[j], m) * scales[j])
+                        following[m] = following[m] - col[j] * along_rows(scaled, m)
                 tile_t = tile_t - col[j] * rows[j][0]
                 inv_t = inv_t - col[j] * rows[j][1]
             tiles[t], inverse[t] = tile_t, inv_t
@@ -106,81 +111,149 @@
     return high, tile - high
 
 
-def eliminate(table, columns, block, beside):
-    count = columns // LANES
-    for k in range(count):
-        here, after = slice(k * LANES, (k + 1) * LANES), (k + 1) * LANES
-        inverse = halves(inverse_factor(block))
-        if k in beside:
-            beside[k]()
-        panel = dot3(halves(table[after:, here]), inverse, NT)
-        table[after:, here] = panel
-        if k + 1 < count:
-            high, low = halves(panel)
-            strip = (high[:LANES], low[:LANES])
-            block = table[after : after + LANES, after : after + LANES] - dot3(strip, strip, NT)
-            ahead = columns - after
-            table[after:, after:columns] = table[after:, after:columns] - dot3(
-                (high, low), (high[:ahead], low[:ahead]), NT
-            )
-
-
-def power_kernel(place, ga, gb, gx, go, pa, pb, px, po, ra, rb, rx, ro, rest, whole, factor, basis, table):
-    size, part = factor.shape[0], ra.shape[0]
-    half = size // 2
+def joined(left, right, dims):
+    return lax.dot_general(
+        jnp.concatenate([left[0], left[0], left[1]], dims[0][0][0]),
+        jnp.concatenate([right[0], right[1], right[0]], dims[0][1][0]),
+        dims,
+        preferred_element_type=f32,
+    )
+
+
+class Pair:
+    def __init__(self, high, low):
+        self.high, self.low = high, low
+
+    def __getitem__(self, where):
+        return self.high[where], self.low[where]
+
+    def __setitem__(self, where, value):
+        self.high[where], self.low[where] = halves(value)
+
+
+def block_of(k):
+    return slice(k * LANES, (k + 1) * LANES)
+
+
+def chunks(start, stop, step=2 * LANES):
+    return [slice(i, min(i + step, stop)) for i in range(start, stop, step)]
+
+
+def panel_and_next(table, lower, inverse, k, size, base=0):
+    after = (k + 1) * LANES
+    panel = joined(halves(table[after - base :, block_of(k)]), halves(inverse), NT)
+    lower[after:, block_of(k)] = panel
+    high, low = halves(panel[:LANES])
+    return table[after - base : after - base + LANES, block_of(k + 1)] - joined((high, low), (high, low), NT)
+
+
+def trailing(table, lower, k, size, base=0):
+    def piece(cols):
+        rows = slice(cols.start - base, None)
+        table[rows, cols] = table[rows, cols] - joined(
+            lower[cols.start :, block_of(k)], lower[cols, block_of(k)], NT
+        )
+
+    return [functools.partial(piece, cols) for cols in chunks((k + 1) * LANES, size)]
+
+
+def solved_row(solved, inverse, k):
+    def piece(cols):
+        solved[block_of(k), cols] = joined(halves(inverse), halves(solved[block_of(k), cols]), NN)
+
+    return [functools.partial(piece, cols) for cols in chunks(0, solved.shape[1], 3 * LANES)]
+
+
+def rows_update(solved, lower, rows, done):
+    def piece(cols):
+        solved[rows, cols] = solved[rows, cols] - joined(
+            lower[rows, done], halves(solved[done, cols]), NN
+        )
+
+    return [functools.partial(piece, cols) for cols in chunks(0, solved.shape[1])]
+
+
+def gram_kernel(place, ga, gb, gx, go, ra, rb, rx, ro, whole, gram):
+    part = ga.shape[0]
     for i, piece in enumerate((ga, gb, gx, go)):
         whole[part * i : part * (i + 1), :] = piece[...]
-    factor[...] = (1.0 - ema_decay) * lax.dot_general(whole[...], whole[...], TN, preferred_element_type=f32)
-    for i, (piece, back) in enumerate(((pa, ra), (pb, rb), (px, rx), (po, ro))):
+    gram[...] = lax.dot_general(whole[...], whole[...], TN, preferred_element_type=f32)
+    for i, piece in enumerate((ra, rb, rx, ro)):
+        piece[...] = gram[pl.ds(pl.multiple_of(place[i], 64), part), :]
+
+
+def power_kernel(place, ga, gb, gx, go, pa, pb, px, po, rest, solved, last_inverse,
+                 factor, basis_high, basis_low, turned_high, turned_low, table, lower_high, lower_low):
+    size, part = factor.shape[0], ga.shape[0]
+    half = size // 2
+    basis, turned, lower = Pair(basis_high, basis_low), Pair(turned_high, turned_low), Pair(lower_high, lower_low)
+    for i, (gram, piece) in enumerate(((ga, pa), (gb, pb), (gx, px), (go, po))):
         rows = pl.ds(pl.multiple_of(place[i], 64), part)
         basis[rows, :] = piece[:part, :]
-        new = ema_decay * piece[part:, :] + factor[rows, :]
-        factor[rows, :] = new
-        back[...] = new
-    base = halves(basis[...])
-    power = halves(dot3(halves(factor[...]), base, NN))
-    table[:size, :] = dot3(power, power, TN)
-
-    def spread_basis():
-        table[size:, :] = dot3(base, power, TN)
-
-    block = table[:LANES, :LANES]
-    eliminate_part(table, size, block, 3, spread_basis)
-    rest[:half, :] = table[half:size, half:]
-    rest[half : half + size, :] = table[size:, half:]
-    rest[half + size :, :] = table[size:, :half]
-
-
-def eliminate_part(table, size, block, steps, first):
-    for k in range(steps):
-        here, after = slice(k * LANES, (k + 1) * LANES), (k + 1) * LANES
-        inverse = halves(inverse_factor(block))
-        if k == 0:
-            first()
-        panel = dot3(halves(table[after:, here]), inverse, NT)
-        table[after:, here] = panel
-        high, low = halves(panel)
-        ahead = size - after
-        if k + 1 < steps:
-            strip = (high[:LANES], low[:LANES])
-            block = table[after : after + LANES, after : after + LANES] - dot3(strip, strip, NT)
-        table[after:, after:size] = table[after:, after:size] - dot3((high, low), (high[:ahead], low[:ahead]), NT)
-
-
-def rotate_kernel(rest, ma, mb, mx, mo, ra, rb, rx, ro, table, moment, done):
-    size, part = moment.shape[0], ra.shape[0]
+        factor[rows, :] = ema_decay * piece[part:, :] + (1.0 - ema_decay) * gram[...]
+    turned[...] = dot3(basis[...], halves(factor[...]), TN)
+
+    def cross(rows, cols):
+        table[rows, cols] = dot3(turned[rows, :], turned[cols, :], NT)
+
+    def start(rows, cols):
+        solved[rows, cols] = dot3(turned[rows, :], basis[:, cols], NN)
+
+    whole = chunks(0, size)
+    part_of = functools.partial
+    first = turned[:LANES, :]
+    block = dot3(first, first, NT)
+    work = [part_of(cross, rows, cols) for cols in whole for rows in whole if rows.start >= cols.start]
+    work += [part_of(start, whole[0], cols) for cols in whole]
+    inverse = [inverse_factor(block, work)]
+    block = panel_and_next(table, lower, inverse[0], 0, size)
+    work = trailing(table, lower, 0, size) + solved_row(solved, inverse[0], 0)
+    work += [part_of(start, whole[1], cols) for cols in whole]
+    inverse.append(inverse_factor(block, work))
+    block = panel_and_next(table, lower, inverse[1], 1, size)
+    work = trailing(table, lower, 1, size) + [part_of(start, whole[2], cols) for cols in whole]
+    work += rows_update(solved, lower, block_of(1), block_of(0)) + solved_row(solved, inverse[1], 1)
+    work += rows_update(solved, lower, slice(2 * LANES, size), slice(0, 2 * LANES))
+    inverse.append(inverse_factor(block, work))
+    last_inverse[...] = inverse[2]
+    rest[:, :LANES] = joined(halves(table[half:, 2 * LANES : half]), halves(inverse[2]), NT)
+    rest[:, LANES:] = table[half:, half:]
+
+
+def rotate_kernel(rest, solved_in, inverse_2, ma, mb, mx, mo, ra, rb, rx, ro,
+                  table, solved, lower_high, lower_low, moment_high, moment_low, done):
+    size, part = solved.shape[0], ra.shape[0]
     half = size // 2
-    table[...] = rest[: half + size, :]
+    lower, moment = Pair(lower_high, lower_low), Pair(moment_high, moment_low)
+    table[:, half:] = rest[:, LANES:]
+    solved[...] = solved_in[...]
+    lower[half:, 2 * LANES : half] = rest[:, :LANES]
     for i, piece in enumerate((ma, mb, mx, mo)):
         moment[part * i : part * (i + 1), :] = piece[...]
-    turned = halves(moment[...])
-
-    def early(k):
-        here = slice(k * LANES, (k + 1) * LANES)
-        done[:, here] = dot3(turned, halves(rest[half + size :, here]), NN)
-
-    eliminate(table, half, table[:LANES, :LANES], {k: functools.partial(early, k) for k in range(half // LANES)})
-    done[:, half:] = dot3(turned, halves(table[half:, :]), NN)
+    strip = lower[half : half + LANES, block_of(2)]
+    block = table[:LANES, block_of(3)] - joined(strip, strip, NT)
+
+    def product(cols, rows):
+        done[rows, cols] = dot3(moment[rows, :], halves(solved[cols, :]), NT)
+
+    def products(cols):
+        return [functools.partial(product, cols, rows) for rows in chunks(0, size)]
+
+    def left(k):
+        return slice((k + 1) * LANES, size)
+
+    work = trailing(table, lower, 2, size, half) + solved_row(solved, inverse_2[...], 2)
+    work += rows_update(solved, lower, left(2), block_of(2)) + products(slice(0, half))
+    inverse = inverse_factor(block, work)
+    block = panel_and_next(table, lower, inverse, 3, size, half)
+    work = trailing(table, lower, 3, size, half) + solved_row(solved, inverse, 3)
+    work += rows_update(solved, lower, left(3), block_of(3)) + products(block_of(3))
+    inverse = inverse_factor(block, work)
+    block = panel_and_next(table, lower, inverse, 4, size, half)
+    work = solved_row(solved, inverse, 4) + rows_update(solved, lower, left(4), block_of(4)) + products(block_of(4))
+    inverse = inverse_factor(block, work)
+    for piece in solved_row(solved, inverse, 5) + products(block_of(5)):
+        piece()
     for i, piece in enumerate((ra, rb, rx, ro)):
         piece[...] = done[part * i : part * (i + 1), :]
 
@@ -200,20 +273,27 @@
     )(*lead, *args)
 
 
-def power_call(place, gradient_parts, pair_parts):
+def gram_call(place, gradient_parts):
     part, size = gradient_parts[0].shape
     whole = (size, size)
-    outs = [((part, size), f32)] * 4 + [((size // 2 + 2 * size, size // 2), f32)]
-    scratch = [(whole, bf16), (whole, f32), (whole, f32), ((2 * size, size), f32)]
-    return call(power_kernel, outs, scratch, 30 * size**3, *gradient_parts, *pair_parts, place=place)
-
-
-def rotate_call(rest, moment_parts):
+    return call(gram_kernel, [((part, size), f32)] * 4, [(whole, bf16), (whole, f32)], 2 * size**3,
+                *gradient_parts, place=place)
+
+
+def power_call(place, gram_parts, pair_parts):
+    part, size = gram_parts[0].shape
+    whole = (size, size)
+    outs = [((size // 2, size // 2 + LANES), f32), (whole, f32), ((LANES, LANES), f32)]
+    scratch = [(whole, f32)] + [(whole, bf16)] * 4 + [(whole, f32)] + [(whole, bf16)] * 2
+    return call(power_kernel, outs, scratch, 20 * size**3, *gram_parts, *pair_parts, place=place)
+
+
+def rotate_call(rest, solved, inverse, moment_parts):
     part, size = moment_parts[0].shape
     whole = (size, size)
     outs = [((part, size), f32)] * 4
-    scratch = [((size // 2 + size, size // 2), f32), (whole, f32), (whole, f32)]
-    return call(rotate_kernel, outs, scratch, 20 * size**3, rest, *moment_parts)
+    scratch = [((size // 2, size), f32), (whole, f32)] + [(whole, bf16)] * 4 + [(whole, f32)]
+    return call(rotate_kernel, outs, scratch, 20 * size**3, rest, solved, inverse, *moment_parts)
 
 
 def on_device(gradient, factor, eigenbasis, moment, refresh_due):
@@ -252,14 +332,17 @@
 
     place = lax.rem(position + jnp.array([3, 1, 2, 0], jnp.int32), ring) * part
 
+    gradient_parts = collect(jnp.swapaxes(gradient, 1, 2))
     pair_parts = collect(jnp.concatenate([eigenbasis, factor], 1))
-    gradient_parts = collect(jnp.swapaxes(gradient, 1, 2))
     turned = choose(jnp.swapaxes(moment, 1, 2))
-    turned, pair_parts = lax.optimization_barrier((turned, pair_parts))
+    turned, gradient_parts = lax.optimization_barrier((turned, gradient_parts))
     moment_parts = send(*turned)
-    *factor_parts, rest = power_call(place, gradient_parts, pair_parts)
-    factor_new = give_back(factor_parts)
-    rotated_parts = rotate_call(rest, moment_parts)
+    gram_parts = gram_call(place, gradient_parts)
+    gram_rows = give_back(gram_parts)
+    rest, solved, inverse = power_call(place, gram_parts, pair_parts)
+    rotated_parts = rotate_call(rest, solved, inverse, moment_parts)
+    rotated_parts, gram_rows = lax.optimization_barrier((rotated_parts, gram_rows))
+    factor_new = ema_decay * factor + (1.0 - ema_decay) * gram_rows
     rotated = jnp.swapaxes(give_back(rotated_parts), 1, 2)
     moment_new = jnp.where((refresh_due > 0)[:, None, None], rotated, moment)
     return factor_new, moment_new

time: 126 us -> 142 us (1.13)
  the two profiles are of different devices: /device:TPU:4 before, /device:TPU:1 now
where the time goes in v3:
time: 142 us; the launch traced here: 141 us
  starting transfers between devices  65.3 us (46%)
  Pallas kernels  41.8 us (29%)
  waiting for transfers between devices  21.9 us (15%)
  other arithmetic  8.06 us (6%)
  local copies, waits for them, and re-layouts  3.11 us (2%)
    ppermute x15, starting transfers between devices, exchange(): return lax.ppermute(value, ('dp', 'tensor'), pairs)  65.3 us
    pallas_call x3, Pallas kernels, call(): pl.pallas_call(kernel, out_shape=[jax.ShapeDtypeStruct(shape, dtype) for...  41.8 us
    ppermute x15, waiting for transfers between devices, exchange(): return lax.ppermute(value, ('dp', 'tensor'), pairs)  21.9 us
    select_n x3, other arithmetic, choose(): jnp.where(first_is_1, value[0], value[1])  3.45 us
    unnamed x31, local copies, waits for them, and re-layouts  3.04 us
  transfers between devices with their start and end apart: 15, of which 4 were waited for; matrix products, arithmetic and copies ran while one was open for 4% of the time, Pallas kernels for 15%

profile of v3, /device:TPU:1, one launch (start us, length us, event | category | flops | bytes accessed | tf_op | source)
XLA Modules:
  0.0 141.2 jit_solution(17763009843070741096)
XLA Ops:
  0.6 0.0 copy-start.14
  0.7 1.2 select_bitcast_fusion.8
  1.9 4.0 %collective-permute-start = (bf16[192,768]{1,0:T(8,128)(2,1)S(1)}, bf16[192,768]{1,0:T(8,128)(2,1)S(1)}, u32[]{:S(2)}, u32[]{:S(2)}) collective-permute-start(bf16[192,768]{1,0:T(8,128)(2,1)S(1)} %get-tuple-element.55), channel_id=1, source_target_pairs={{1,2},{3,0},{6,7},{4,5},{9,10},{11,8},{14,15},{12,13},{17,18},{19,... | collective-permute-start | bytes 884744 | tf_op jit(solution)/shard_map/ppermute | solution.py:313
  5.8 0.7 collective-permute-start.2
  6.5 4.9 %collective-permute-start.1 = (bf16[192,768]{1,0:T(8,128)(2,1)S(1)}, bf16[192,768]{1,0:T(8,128)(2,1)S(1)}, u32[]{:S(2)}, u32[]{:S(2)}) collective-permute-start(bf16[192,768]{1,0:T(8,128)(2,1)S(1)} %get-tuple-element.27.go), channel_id=1, source_target_pairs={{1,0},{3,2},{6,5},{4,7},{9,8},{11,10},{14,13},{12,15},{17,16},{19,... | collective-permute-start | bytes 884744 | tf_op jit(solution)/shard_map/ppermute | solution.py:313
  11.5 0.5 fusion.2.place
  12.0 1.1 select_bitcast_fusion.6
  13.1 2.4 %collective-permute-done.1.gb = bf16[192,768]{1,0:T(8,128)(2,1)S(1)} collective-permute-done((bf16[192,768]{1,0:T(8,128)(2,1)S(1)}, bf16[192,768]{1,0:T(8,128)(2,1)S(1)}, u32[]{:S(2)}, u32[]{:S(2)}) %collective-permute-start.1) | collective-permute-done | bytes 294944 | tf_op jit(solution)/shard_map/ppermute | solution.py:313
  15.5 0.0 collective-permute-done.2.gx
  15.5 0.7 copy-done.12
  16.2 0.1 copy-done.11
  16.3 3.9 %shard_map.77 = (f32[192,768]{1,0:T(8,128)}, f32[192,768]{1,0:T(8,128)}, f32[192,768]{1,0:T(8,128)}, f32[192,768]{1,0:T(8,128)}) custom-call(s32[4]{0:T(128)} %fusion.2.place, bf16[192,768]{1,0:T(8,128)(2,1)} %copy-done.10, bf16[192,768]{1,0:T(8,128)(2,1)} %copy-done.12, bf16[192,768]{1,0:T(8,128)(2,1)} %copy-done.11, bf16[192,768]{1,0:T(8,128)(2,1)} %copy-done.6), custom_call_target="tpu_custom_call" | custom-call | flops 905969664 | bytes 4194304 | tf_op jit(solution)/shard_map/pallas_call | solution.py:265
  20.2 1.4 collective-permute-start.9
  21.7 0.1 constant_dynamic-update-slice_fusion.1
  21.8 0.1 constant_dynamic-update-slice_fusion
  21.9 1.2 select_bitcast_fusion
  23.0 5.7 %collective-permute-start.3 = (f32[384,768]{1,0:T(8,128)}, f32[384,768]{1,0:T(8,128)}, u32[]{:S(2)}, u32[]{:S(2)}) collective-permute-start(f32[384,768]{1,0:T(8,128)} %get-tuple-element.51), channel_id=1, source_target_pairs={{1,2},{3,0},{6,7},{4,5},{9,10},{11,8},{14,15},{12,13},{17,18},{19,... | collective-permute-start | bytes 3538952 | tf_op jit(solution)/shard_map/ppermute | solution.py:313
  28.8 2.6 %collective-permute-start.4 = (f32[384,768]{1,0:T(8,128)S(1)}, f32[384,768]{1,0:T(8,128)}, u32[]{:S(2)}, u32[]{:S(2)}) collective-permute-start(f32[384,768]{1,0:T(8,128)S(1)} %get-tuple-element.50.po), channel_id=1, source_target_pairs={{1,0},{3,2},{6,5},{4,7},{9,8},{11,10},{14,13},{12,15},{17,16},{19,... | collective-permute-start | bytes 3538952 | tf_op jit(solution)/shard_map/ppermute | solution.py:313
  31.3 1.7 %collective-permute-start.5 = (f32[384,768]{1,0:T(8,128)}, f32[384,768]{1,0:T(8,128)}, u32[]{:S(2)}, u32[]{:S(2)}) collective-permute-start(f32[384,768]{1,0:T(8,128)} %get-tuple-element.51), channel_id=1, source_target_pairs={{0,2},{2,0},{5,7},{7,5},{8,10},{10,8},{13,15},{15,13},{16,18},{18,... | collective-permute-start | bytes 3538952 | tf_op jit(solution)/shard_map/ppermute | solution.py:313
  33.0 1.5 %collective-permute-start.10 = (f32[192,768]{1,0:T(8,128)}, f32[192,768]{1,0:T(8,128)}, u32[]{:S(2)}, u32[]{:S(2)}) collective-permute-start(f32[192,768]{1,0:T(8,128)} %get-tuple-element.30.gx), channel_id=1, source_target_pairs={{0,2},{2,0},{5,7},{7,5},{8,10},{10,8},{13,15},{15,13},{16,18},{18,... | collective-permute-start | bytes 1769480 | tf_op jit(solution)/shard_map/ppermute | solution.py:313
  34.5 0.0 collective-permute-done.9
  34.6 1.3 collective-permute-start.11
  35.9 0.0 collective-permute-done.10
  35.9 32.3 %collective-permute-start.6 = (f32[192,768]{1,0:T(8,128)}, f32[192,768]{1,0:T(8,128)S(1)}, u32[]{:S(2)}, u32[]{:S(2)}) collective-permute-start(f32[192,768]{1,0:T(8,128)} %get-tuple-element.35), channel_id=1, source_target_pairs={{1,2},{3,0},{6,7},{4,5},{9,10},{11,8},{14,15},{12,13},{17,18},{19,... | collective-permute-start | bytes 1769480 | tf_op jit(solution)/shard_map/ppermute | solution.py:313
  68.2 3.2 %collective-permute-done.11 = f32[192,768]{1,0:T(8,128)} collective-permute-done((f32[192,768]{1,0:T(8,128)}, f32[192,768]{1,0:T(8,128)}, u32[]{:S(2)}, u32[]{:S(2)}) %collective-permute-start.11) | collective-permute-done | bytes 589856 | tf_op jit(solution)/shard_map/ppermute | solution.py:313
  71.4 0.7 collective-permute-start.8
  72.1 1.4 select_bitcast_fusion.5
  73.5 0.1 pad_maximum_fusion
  73.6 0.0 collective-permute-done.3.pa
  73.6 1.0 copy-done.4
  74.5 5.3 %collective-permute-start.7 = (f32[192,768]{1,0:T(8,128)S(1)}, f32[192,768]{1,0:T(8,128)S(1)}, u32[]{:S(2)}, u32[]{:S(2)}) collective-permute-start(f32[192,768]{1,0:T(8,128)S(1)} %copy-done.4), channel_id=1, source_target_pairs={{1,0},{3,2},{6,5},{4,7},{9,8},{11,10},{14,13},{12,15},{17,16},{19,... | collective-permute-start | bytes 1769480 | tf_op jit(solution)/shard_map/ppermute | solution.py:313
  79.8 0.0 collective-permute-done.4.pb
  79.8 0.0 collective-permute-done.5.px
  79.8 21.8 %shard_map.78 = (f32[384,512]{1,0:T(8,128)}, f32[768,768]{1,0:T(8,128)}, f32[128,128]{1,0:T(8,128)}) custom-call(s32[4]{0:T(128)} %fusion.2.place, f32[192,768]{1,0:T(8,128)} %get-tuple-element.28.ga, f32[192,768]{1,0:T(8,128)} %get-tuple-element.29.gb, f32[192,768]{1,0:T(8,128)} %get-tuple-element.30.gx, f32[192,768]{1,0:T(8,128)} %get-tuple-element.31.go, ...), custom_call_target="tpu_custom_call" | custom-call | flops 9059696640 | bytes 4194304 | tf_op jit(solution)/shard_map/pallas_call | solution.py:265
  101.6 0.0 collective-permute-done.6.ma
  101.6 0.0 collective-permute-done.7.mb
  101.7 0.8 copy-done.7
  102.4 0.2 copy-done.9
  102.6 0.2 copy-done.8
  102.8 16.1 %shard_map.79 = (f32[192,768]{1,0:T(8,128)}, f32[192,768]{1,0:T(8,128)}, f32[192,768]{1,0:T(8,128)}, f32[192,768]{1,0:T(8,128)}) custom-call(f32[384,512]{1,0:T(8,128)} %get-tuple-element.32.rest, f32[768,768]{1,0:T(8,128)} %get-tuple-element.33.solved_in, f32[128,128]{1,0:T(8,128)} %get-tuple-element.34.inverse_2, f32[192,768]{1,0:T(8,128)} %copy-done.7, ...), custom_call_target="tpu_custom_call" | custom-call | flops 9059696640 | bytes 4194304 | tf_op jit(solution)/shard_map/pallas_call | solution.py:265
  118.9 1.3 collective-permute-start.12
  120.2 0.7 collective-permute-start.13
  120.9 1.3 collective-permute-start.14
  122.2 1.2 multiply_add_fusion
  123.4 13.8 %collective-permute-done.12 = f32[192,768]{1,0:T(8,128)S(1)} collective-permute-done((f32[192,768]{1,0:T(8,128)}, f32[192,768]{1,0:T(8,128)S(1)}, u32[]{:S(2)}, u32[]{:S(2)}) %collective-permute-start.12) | collective-permute-done | bytes 589856 | tf_op jit(solution)/shard_map/ppermute | solution.py:313
  137.2 2.6 %collective-permute-done.14 = f32[192,768]{1,0:T(8,128)S(1)} collective-permute-done((f32[192,768]{1,0:T(8,128)}, f32[192,768]{1,0:T(8,128)S(1)}, u32[]{:S(2)}, u32[]{:S(2)}) %collective-permute-start.14) | collective-permute-done | bytes 589856 | tf_op jit(solution)/shard_map/ppermute | solution.py:313
  139.8 0.1 select_bitcast_fusion.3
  140.0 1.2 fusion
  (27 shorter events, 0.1 us)
Async XLA Ops:
  0.6 10.8 %copy-start.14 = (s32[4]{0:T(128)S(1)}, s32[4]{0:T(128)}, u32[]{:S(2)}) copy-start(s32[4]{0:T(128)} %constant.35.clone) | copy-start | bytes 52
  0.6 11.4 %copy-start.1 = (f32[2,768,192]{1,2,0:T(8,128)S(1)}, f32[2,768,192]{1,2,0:T(8,128)}, u32[]{:S(2)}) copy-start(f32[2,768,192]{1,2,0:T(8,128)} %param.9) | copy-start | bytes 3538948
  1.9 11.2 %copy-start.6 = (bf16[192,768]{1,0:T(8,128)(2,1)}, bf16[192,768]{1,0:T(8,128)(2,1)S(1)}, u32[]{:S(2)}) copy-start(bf16[192,768]{1,0:T(8,128)(2,1)S(1)} %get-tuple-element.27.go) | copy-start | bytes 884740
  1.9 11.2 %collective-permute-start = (bf16[192,768]{1,0:T(8,128)(2,1)S(1)}, bf16[192,768]{1,0:T(8,128)(2,1)S(1)}, u32[]{:S(2)}, u32[]{:S(2)}) collective-permute-start(bf16[192,768]{1,0:T(8,128)(2,1)S(1)} %get-tuple-element.55), channel_id=1, source_target_pairs={{1,2},{3,0},{6,7},{4,5},{9,10},{11,8},{14,15},{12,13},{17,18},{19,... | collective-permute-start | bytes 884744 | tf_op jit(solution)/shard_map/ppermute | solution.py:313
  5.8 9.7 %collective-permute-start.2 = (bf16[192,768]{1,0:T(8,128)(2,1)S(1)}, bf16[192,768]{1,0:T(8,128)(2,1)S(1)}, u32[]{:S(2)}, u32[]{:S(2)}) collective-permute-start(bf16[192,768]{1,0:T(8,128)(2,1)S(1)} %get-tuple-element.55), channel_id=1, source_target_pairs={{0,2},{2,0},{5,7},{7,5},{8,10},{10,8},{13,15},{15,13},{16,18},{18,... | collective-permute-start | bytes 884744 | tf_op jit(solution)/shard_map/ppermute | solution.py:313
  6.5 9.0 %collective-permute-start.1 = (bf16[192,768]{1,0:T(8,128)(2,1)S(1)}, bf16[192,768]{1,0:T(8,128)(2,1)S(1)}, u32[]{:S(2)}, u32[]{:S(2)}) collective-permute-start(bf16[192,768]{1,0:T(8,128)(2,1)S(1)} %get-tuple-element.27.go), channel_id=1, source_target_pairs={{1,0},{3,2},{6,5},{4,7},{9,8},{11,10},{14,13},{12,15},{17,16},{19,... | collective-permute-start | bytes 884744 | tf_op jit(solution)/shard_map/ppermute | solution.py:313
  13.1 2.4 %copy-start.10 = (bf16[192,768]{1,0:T(8,128)(2,1)}, bf16[192,768]{1,0:T(8,128)(2,1)S(1)}, u32[]{:S(2)}) copy-start(bf16[192,768]{1,0:T(8,128)(2,1)S(1)} %collective-permute-done.ga) | copy-start | bytes 884740
  15.5 0.7 copy-start.12
  15.5 0.8 copy-start.11
  16.3 5.4 %copy-start.3 = (f32[2,192,768]{2,1,0:T(8,128)S(1)}, f32[2,192,768]{2,1,0:T(8,128)}, u32[]{:S(2)}) copy-start(f32[2,192,768]{2,1,0:T(8,128)} %param.8) | copy-start | bytes 3538948
  20.2 1.5 %copy-start = (f32[2,192,768]{2,1,0:T(8,128)S(1)}, f32[2,192,768]{2,1,0:T(8,128)}, u32[]{:S(2)}) copy-start(f32[2,192,768]{2,1,0:T(8,128)} %param.7) | copy-start | bytes 3538948
  20.2 14.3 %collective-permute-start.9 = (f32[192,768]{1,0:T(8,128)}, f32[192,768]{1,0:T(8,128)}, u32[]{:S(2)}, u32[]{:S(2)}) collective-permute-start(f32[192,768]{1,0:T(8,128)} %get-tuple-element.29.gb), channel_id=1, source_target_pairs={{0,1},{2,3},{5,6},{7,4},{8,9},{10,11},{13,14},{15,12},{16,17},{18,... | collective-permute-start | bytes 1769480 | tf_op jit(solution)/shard_map/ppermute | solution.py:313
  23.0 50.4 %copy-start.2 = (f32[384,768]{1,0:T(8,128)}, f32[384,768]{1,0:T(8,128)S(1)}, u32[]{:S(2)}) copy-start(f32[384,768]{1,0:T(8,128)S(1)} %get-tuple-element.50.po) | copy-start | bytes 3538948
  23.0 50.5 %collective-permute-start.3 = (f32[384,768]{1,0:T(8,128)}, f32[384,768]{1,0:T(8,128)}, u32[]{:S(2)}, u32[]{:S(2)}) collective-permute-start(f32[384,768]{1,0:T(8,128)} %get-tuple-element.51), channel_id=1, source_target_pairs={{1,2},{3,0},{6,7},{4,5},{9,10},{11,8},{14,15},{12,13},{17,18},{19,... | collective-permute-start | bytes 3538952 | tf_op jit(solution)/shard_map/ppermute | solution.py:313
  28.8 51.0 %collective-permute-start.4 = (f32[384,768]{1,0:T(8,128)S(1)}, f32[384,768]{1,0:T(8,128)}, u32[]{:S(2)}, u32[]{:S(2)}) collective-permute-start(f32[384,768]{1,0:T(8,128)S(1)} %get-tuple-element.50.po), channel_id=1, source_target_pairs={{1,0},{3,2},{6,5},{4,7},{9,8},{11,10},{14,13},{12,15},{17,16},{19,... | collective-permute-start | bytes 3538952 | tf_op jit(solution)/shard_map/ppermute | solution.py:313
  31.3 48.5 %collective-permute-start.5 = (f32[384,768]{1,0:T(8,128)}, f32[384,768]{1,0:T(8,128)}, u32[]{:S(2)}, u32[]{:S(2)}) collective-permute-start(f32[384,768]{1,0:T(8,128)} %get-tuple-element.51), channel_id=1, source_target_pairs={{0,2},{2,0},{5,7},{7,5},{8,10},{10,8},{13,15},{15,13},{16,18},{18,... | collective-permute-start | bytes 3538952 | tf_op jit(solution)/shard_map/ppermute | solution.py:313
  33.0 2.8 %collective-permute-start.10 = (f32[192,768]{1,0:T(8,128)}, f32[192,768]{1,0:T(8,128)}, u32[]{:S(2)}, u32[]{:S(2)}) collective-permute-start(f32[192,768]{1,0:T(8,128)} %get-tuple-element.30.gx), channel_id=1, source_target_pairs={{0,2},{2,0},{5,7},{7,5},{8,10},{10,8},{13,15},{15,13},{16,18},{18,... | collective-permute-start | bytes 1769480 | tf_op jit(solution)/shard_map/ppermute | solution.py:313
  34.6 36.8 %collective-permute-start.11 = (f32[192,768]{1,0:T(8,128)}, f32[192,768]{1,0:T(8,128)}, u32[]{:S(2)}, u32[]{:S(2)}) collective-permute-start(f32[192,768]{1,0:T(8,128)} %get-tuple-element.28.ga), channel_id=1, source_target_pairs={{2,1},{0,3},{7,6},{5,4},{10,9},{8,11},{15,14},{13,12},{18,17},{16,... | collective-permute-start | bytes 1769480 | tf_op jit(solution)/shard_map/ppermute | solution.py:313
  35.9 65.8 %collective-permute-start.6 = (f32[192,768]{1,0:T(8,128)}, f32[192,768]{1,0:T(8,128)S(1)}, u32[]{:S(2)}, u32[]{:S(2)}) collective-permute-start(f32[192,768]{1,0:T(8,128)} %get-tuple-element.35), channel_id=1, source_target_pairs={{1,2},{3,0},{6,7},{4,5},{9,10},{11,8},{14,15},{12,13},{17,18},{19,... | collective-permute-start | bytes 1769480 | tf_op jit(solution)/shard_map/ppermute | solution.py:313
  71.4 30.3 %collective-permute-start.8 = (f32[192,768]{1,0:T(8,128)}, f32[192,768]{1,0:T(8,128)S(1)}, u32[]{:S(2)}, u32[]{:S(2)}) collective-permute-start(f32[192,768]{1,0:T(8,128)} %get-tuple-element.35), channel_id=1, source_target_pairs={{0,2},{2,0},{5,7},{7,5},{8,10},{10,8},{13,15},{15,13},{16,18},{18,... | collective-permute-start | bytes 1769480 | tf_op jit(solution)/shard_map/ppermute | solution.py:313
  73.5 1.1 copy-start.4
  74.5 27.1 %collective-permute-start.7 = (f32[192,768]{1,0:T(8,128)S(1)}, f32[192,768]{1,0:T(8,128)S(1)}, u32[]{:S(2)}, u32[]{:S(2)}) collective-permute-start(f32[192,768]{1,0:T(8,128)S(1)} %copy-done.4), channel_id=1, source_target_pairs={{1,0},{3,2},{6,5},{4,7},{9,8},{11,10},{14,13},{12,15},{17,16},{19,... | collective-permute-start | bytes 1769480 | tf_op jit(solution)/shard_map/ppermute | solution.py:313
  101.6 0.8 copy-start.7
  101.6 1.0 copy-start.9
  101.7 1.2 copy-start.8
  102.8 19.3 %copy-start.13 = (s32[2]{0:T(128)S(1)}, s32[2]{0:T(128)}, u32[]{:S(2)}) copy-start(s32[2]{0:T(128)} %param.10) | copy-start | bytes 28
  118.9 18.4 %collective-permute-start.12 = (f32[192,768]{1,0:T(8,128)}, f32[192,768]{1,0:T(8,128)S(1)}, u32[]{:S(2)}, u32[]{:S(2)}) collective-permute-start(f32[192,768]{1,0:T(8,128)} %get-tuple-element.43), channel_id=1, source_target_pairs={{0,1},{2,3},{5,6},{7,4},{8,9},{10,11},{13,14},{15,12},{16,17},{18,... | collective-permute-start | bytes 1769480 | tf_op jit(solution)/shard_map/ppermute | solution.py:313
  120.2 17.1 %collective-permute-start.13 = (f32[192,768]{1,0:T(8,128)}, f32[192,768]{1,0:T(8,128)S(1)}, u32[]{:S(2)}, u32[]{:S(2)}) collective-permute-start(f32[192,768]{1,0:T(8,128)} %get-tuple-element.44), channel_id=1, source_target_pairs={{0,2},{2,0},{5,7},{7,5},{8,10},{10,8},{13,15},{15,13},{16,18},{18,... | collective-permute-start | bytes 1769480 | tf_op jit(solution)/shard_map/ppermute | solution.py:313
  120.9 18.9 %collective-permute-start.14 = (f32[192,768]{1,0:T(8,128)}, f32[192,768]{1,0:T(8,128)S(1)}, u32[]{:S(2)}, u32[]{:S(2)}) collective-permute-start(f32[192,768]{1,0:T(8,128)} %get-tuple-element.45), channel_id=1, source_target_pairs={{2,1},{0,3},{7,6},{5,4},{10,9},{8,11},{15,14},{13,12},{18,17},{16,... | collective-permute-start | bytes 1769480 | tf_op jit(solution)/shard_map/ppermute | solution.py:313
  122.2 17.6 %copy-start.5 = (f32[192,768]{1,0:T(8,128)S(1)}, f32[192,768]{1,0:T(8,128)}, u32[]{:S(2)}) copy-start(f32[192,768]{1,0:T(8,128)} %get-tuple-element.42) | copy-start | bytes 1769476

commit v4 on v3

--- a/solution.py
+++ b/solution.py
@@ -268,7 +268,7 @@
         in_specs=[smem] * len(lead) + [vmem] * len(args),
         out_specs=[vmem] * len(outs),
         scratch_shapes=[pltpu.VMEM(shape, dtype) for shape, dtype in scratch],
-        cost_estimate=pl.CostEstimate(flops=flops, bytes_accessed=1 << 22, transcendentals=0),
+        cost_estimate=pl.CostEstimate(flops=flops, bytes_accessed=1024, transcendentals=0),
         compiler_params=pltpu.CompilerParams(vmem_limit_bytes=56 << 20),
     )(*lead, *args)
 
@@ -276,7 +276,7 @@
 def gram_call(place, gradient_parts):
     part, size = gradient_parts[0].shape
     whole = (size, size)
-    return call(gram_kernel, [((part, size), f32)] * 4, [(whole, bf16), (whole, f32)], 2 * size**3,
+    return call(gram_kernel, [((part, size), f32)] * 4, [(whole, bf16), (whole, f32)], 1,
                 *gradient_parts, place=place)
 
 
@@ -322,26 +322,43 @@
     def send(first, second):
         return exchange(first, up), exchange(second, down), exchange(first, across), second
 
-    def collect(value):
-        return send(*choose(value))
+    def arrange(first, second):
+        return jnp.stack([jnp.where(first_is_1, second, first), jnp.where(first_is_1, first, second)])
 
     def give_back(pieces):
         first = jnp.where(owns, exchange(pieces[2], across), exchange(pieces[0], up_back))
         second = jnp.where(owns, pieces[3], exchange(pieces[1], down_back))
-        return jnp.stack([jnp.where(first_is_1, second, first), jnp.where(first_is_1, first, second)])
+        return arrange(first, second)
 
     place = lax.rem(position + jnp.array([3, 1, 2, 0], jnp.int32), ring) * part
 
-    gradient_parts = collect(jnp.swapaxes(gradient, 1, 2))
-    pair_parts = collect(jnp.concatenate([eigenbasis, factor], 1))
-    turned = choose(jnp.swapaxes(moment, 1, 2))
-    turned, gradient_parts = lax.optimization_barrier((turned, gradient_parts))
-    moment_parts = send(*turned)
+    gradient_first, gradient_second = choose(jnp.swapaxes(gradient, 1, 2))
+    pair_first, pair_second = choose(jnp.concatenate([eigenbasis, factor], 1))
+    moment_first, moment_second = choose(jnp.swapaxes(moment, 1, 2))
+    pair_up, pair_down = exchange(pair_first, up), exchange(pair_second, down)
+    gradient_parts = send(gradient_first, gradient_second)
+    pair_first, pair_up, pair_down, gradient_parts, moment_first, moment_second = lax.optimization_barrier(
+        (pair_first, pair_up, pair_down, gradient_parts, moment_first, moment_second)
+    )
+    pair_parts = (pair_up, pair_down, exchange(pair_first, across), pair_second)
     gram_parts = gram_call(place, gradient_parts)
-    gram_rows = give_back(gram_parts)
-    rest, solved, inverse = power_call(place, gram_parts, pair_parts)
-    rotated_parts = rotate_call(rest, solved, inverse, moment_parts)
-    rotated_parts, gram_rows = lax.optimization_barrier((rotated_parts, gram_rows))
+    to_next = jnp.where(owns, gram_parts[1], moment_first)
+    to_last = jnp.where(owns, gram_parts[0], moment_second)
+    from_last = exchange(to_next, [(a, (a + 1) % ring) for a in range(ring)])
+    from_next = exchange(to_last, [(a, (a - 1) % ring) for a in range(ring)])
+    from_across = exchange(jnp.concatenate([moment_first, gram_parts[2]], 0), across)
+    powered = power_call(place, gram_parts, pair_parts)
+    powered, from_last, from_next, from_across = lax.optimization_barrier(
+        (powered, from_last, from_next, from_across)
+    )
+    moment_parts = (from_last, from_next, from_across[:part], moment_second)
+    rotated_parts = rotate_call(*powered, moment_parts)
+    rotated_parts, from_last, from_next, from_across = lax.optimization_barrier(
+        (rotated_parts, from_last, from_next, from_across)
+    )
+    gram_rows = arrange(
+        jnp.where(owns, from_across[part:], from_next), jnp.where(owns, gram_parts[3], from_last)
+    )
     factor_new = ema_decay * factor + (1.0 - ema_decay) * gram_rows
     rotated = jnp.swapaxes(give_back(rotated_parts), 1, 2)
     moment_new = jnp.where((refresh_due > 0)[:, None, None], rotated, moment)

time: 142 us -> 118 us (0.83)
  starting transfers between devices: 65.3 us -> 23.7 us
  waiting for transfers between devices: 21.9 us -> 39 us
    ppermute x15 -> x12, starting transfers between devices: 65.3 us -> 23.7 us  [exchange(): return lax.ppermute(value, ('dp', 'tensor'), pairs)]
    ppermute x15 -> x12, waiting for transfers between devices: 21.9 us -> 39 us  [exchange(): return lax.ppermute(value, ('dp', 'tensor'), pairs)]
    select_n x3, other arithmetic: 3.45 us -> 1.29 us  [choose(): jnp.where(first_is_1, value[0], value[1])]
    unnamed x31 -> x39, local copies, waits for them, and re-layouts: 3.04 us -> 3.49 us
  transfers between devices with their start and end apart: 15 -> 12, of which waited for: 4 -> 5; matrix products, arithmetic and copies ran while one was open for 4% -> 5% of each run, Pallas kernels for 15% -> 22%
where the time goes in v4:
time: 118 us
  Pallas kernels  41.7 us (35%)
  waiting for transfers between devices  39 us (33%)
  starting transfers between devices  23.7 us (20%)
  other arithmetic  7.97 us (7%)
  local copies, waits for them, and re-layouts  4.48 us (4%)
    pallas_call x3, Pallas kernels, call(): pl.pallas_call(kernel, out_shape=[jax.ShapeDtypeStruct(shape, dtype) for...  41.7 us
    ppermute x12, waiting for transfers between devices, exchange(): return lax.ppermute(value, ('dp', 'tensor'), pairs)  39 us
    ppermute x12, starting transfers between devices, exchange(): return lax.ppermute(value, ('dp', 'tensor'), pairs)  23.7 us
    unnamed x39, local copies, waits for them, and re-layouts  3.49 us
  transfers between devices with their start and end apart: 12, of which 5 were waited for; matrix products, arithmetic and copies ran while one was open for 5% of the time, Pallas kernels for 22%

profile of v4, /device:TPU:1, one launch (start us, length us, event | category | flops | bytes accessed | tf_op | source)
XLA Modules:
  0.0 117.8 jit_solution(2630900469321352066)
XLA Ops:
  0.6 1.4 %constant_dynamic-update-slice_fusion.1 = f32[2,384,768]{2,1,0:T(8,128)S(1)} fusion(f32[2,192,768]{2,1,0:T(8,128)} %param.8), kind=kLoop, calls=%fused_computation.22 | loop fusion | bytes 2359296
  2.1 0.2 copy-done
  2.3 0.1 constant_dynamic-update-slice_fusion
  2.3 0.0 copy-start.5
  2.4 1.2 select_bitcast_fusion
  3.5 4.3 %collective-permute-start = (f32[384,768]{1,0:T(8,128)}, f32[384,768]{1,0:T(8,128)S(1)}, u32[]{:S(2)}, u32[]{:S(2)}) collective-permute-start(f32[384,768]{1,0:T(8,128)} %get-tuple-element.45), channel_id=1, source_target_pairs={{1,2},{3,0},{6,7},{4,5},{9,10},{11,8},{14,15},{12,13},{17,18},{19,... | collective-permute-start | bytes 3538952 | tf_op jit(solution)/shard_map/ppermute | solution.py:313
  7.8 2.6 %collective-permute-start.1 = (f32[384,768]{1,0:T(8,128)S(1)}, f32[384,768]{1,0:T(8,128)S(1)}, u32[]{:S(2)}, u32[]{:S(2)}) collective-permute-start(f32[384,768]{1,0:T(8,128)S(1)} %get-tuple-element.72.po), channel_id=1, source_target_pairs={{1,0},{3,2},{6,5},{4,7},{9,8},{11,10},{14,13},{12,15},{17,16},{19,... | collective-permute-start | bytes 3538952 | tf_op jit(solution)/shard_map/ppermute | solution.py:313
  10.4 1.3 %collective-permute-start.2 = (bf16[192,768]{1,0:T(8,128)(2,1)S(1)}, bf16[192,768]{1,0:T(8,128)(2,1)S(1)}, u32[]{:S(2)}, u32[]{:S(2)}) collective-permute-start(bf16[192,768]{1,0:T(8,128)(2,1)S(1)} %get-tuple-element.77), channel_id=1, source_target_pairs={{1,2},{3,0},{6,7},{4,5},{9,10},{11,8},{14,15},{12,13},{17,18},{19,... | collective-permute-start | bytes 884744 | tf_op jit(solution)/shard_map/ppermute | solution.py:313
  11.8 1.3 %collective-permute-start.3 = (bf16[192,768]{1,0:T(8,128)(2,1)S(1)}, bf16[192,768]{1,0:T(8,128)(2,1)S(1)}, u32[]{:S(2)}, u32[]{:S(2)}) collective-permute-start(bf16[192,768]{1,0:T(8,128)(2,1)S(1)} %get-tuple-element.38.go), channel_id=1, source_target_pairs={{1,0},{3,2},{6,5},{4,7},{9,8},{11,10},{14,13},{12,15},{17,16},{19,... | collective-permute-start | bytes 884744 | tf_op jit(solution)/shard_map/ppermute | solution.py:313
  13.1 0.7 collective-permute-start.4
  13.8 0.0 copy-start.18
  13.8 0.0 copy-start.17
  13.8 0.1 select_bitcast_fusion.6
  13.9 13.5 %collective-permute-done.2.ga = bf16[192,768]{1,0:T(8,128)(2,1)S(1)} collective-permute-done((bf16[192,768]{1,0:T(8,128)(2,1)S(1)}, bf16[192,768]{1,0:T(8,128)(2,1)S(1)}, u32[]{:S(2)}, u32[]{:S(2)}) %collective-permute-start.2) | collective-permute-done | bytes 294944 | tf_op jit(solution)/shard_map/ppermute | solution.py:313
  27.4 2.4 %collective-permute-done.3.gb = bf16[192,768]{1,0:T(8,128)(2,1)S(1)} collective-permute-done((bf16[192,768]{1,0:T(8,128)(2,1)S(1)}, bf16[192,768]{1,0:T(8,128)(2,1)S(1)}, u32[]{:S(2)}, u32[]{:S(2)}) %collective-permute-start.3) | collective-permute-done | bytes 294944 | tf_op jit(solution)/shard_map/ppermute | solution.py:313
  29.8 0.0 collective-permute-done.4.gx
  29.8 0.0 collective-permute-done.pa
  29.8 0.0 copy-start.15
  29.8 0.0 collective-permute-done.1.pb
  29.8 0.7 copy-done.13
  30.5 0.1 copy-done.14
  30.6 0.3 copy-done.15
  31.0 0.4 copy-done.16
  31.3 1.7 %collective-permute-start.5 = (f32[384,768]{1,0:T(8,128)}, f32[384,768]{1,0:T(8,128)}, u32[]{:S(2)}, u32[]{:S(2)}) collective-permute-start(f32[384,768]{1,0:T(8,128)} %get-tuple-element.45), channel_id=1, source_target_pairs={{0,2},{2,0},{5,7},{7,5},{8,10},{10,8},{13,15},{15,13},{16,18},{18,... | collective-permute-start | bytes 3538952 | tf_op jit(solution)/shard_map/ppermute | solution.py:313
  33.1 0.5 fusion.3.place
  33.6 3.8 %shard_map.77 = (f32[192,768]{1,0:T(8,128)}, f32[192,768]{1,0:T(8,128)}, f32[192,768]{1,0:T(8,128)}, f32[192,768]{1,0:T(8,128)}) custom-call(s32[4]{0:T(128)} %fusion.3.place, bf16[192,768]{1,0:T(8,128)(2,1)} %copy-done.12, bf16[192,768]{1,0:T(8,128)(2,1)} %copy-done.13, bf16[192,768]{1,0:T(8,128)(2,1)} %copy-done.14, bf16[192,768]{1,0:T(8,128)(2,1)} %copy-done.4), custom_call_target="tpu_custom_call" | custom-call | flops 1 | bytes 1024 | tf_op jit(solution)/shard_map/pallas_call | solution.py:265
  37.4 1.2 %pad_maximum_fusion = f32[384,768]{1,0:T(8,128)S(1)} fusion(f32[192,768]{1,0:T(8,128)} %get-tuple-element.42.gx, f32[192,768]{1,0:T(8,128)S(1)} %get-tuple-element.49), kind=kLoop, calls=%fused_computation | loop fusion | flops 294912 | bytes 2359296 | tf_op jit(solution)/shard_map/concatenate | solution.py:349
  38.6 0.9 collective-permute-start.8
  39.5 0.9 broadcast_select_fusion.4
  40.4 5.7 %collective-permute-start.6 = (f32[192,768]{1,0:T(8,128)}, f32[192,768]{1,0:T(8,128)S(1)}, u32[]{:S(2)}, u32[]{:S(2)}) collective-permute-start(f32[192,768]{1,0:T(8,128)} %broadcast_select_fusion.4), channel_id=1, source_target_pairs={{0,1},{1,2},{2,3},{3,0},{5,6},{6,7},{7,4},{4,5},{8,9},{9,10},{10,1... | collective-permute-start | bytes 1769480 | tf_op jit(solution)/shard_map/ppermute | solution.py:313
  46.1 0.1 broadcast_select_fusion.3
  46.2 2.0 %collective-permute-start.7 = (f32[192,768]{1,0:T(8,128)S(1)}, f32[192,768]{1,0:T(8,128)S(1)}, u32[]{:S(2)}, u32[]{:S(2)}) collective-permute-start(f32[192,768]{1,0:T(8,128)S(1)} %broadcast_select_fusion.3), channel_id=1, source_target_pairs={{0,3},{1,0},{2,1},{3,2},{5,4},{6,5},{7,6},{4,7},{8,11},{9,8},{10,9... | collective-permute-start | bytes 1769480 | tf_op jit(solution)/shard_map/ppermute | solution.py:313
  48.2 21.8 %shard_map.78 = (f32[384,512]{1,0:T(8,128)}, f32[768,768]{1,0:T(8,128)}, f32[128,128]{1,0:T(8,128)}) custom-call(s32[4]{0:T(128)} %fusion.3.place, f32[192,768]{1,0:T(8,128)} %get-tuple-element.40.ga, f32[192,768]{1,0:T(8,128)} %get-tuple-element.41.gb, f32[192,768]{1,0:T(8,128)} %get-tuple-element.42.gx, f32[192,768]{1,0:T(8,128)} %get-tuple-element.39.go, ...), custom_call_target="tpu_custom_call" | custom-call | flops 9059696640 | bytes 1024 | tf_op jit(solution)/shard_map/pallas_call | solution.py:265
  70.0 7.9 %collective-permute-done.6.ma = f32[192,768]{1,0:T(8,128)S(1)} collective-permute-done((f32[192,768]{1,0:T(8,128)}, f32[192,768]{1,0:T(8,128)S(1)}, u32[]{:S(2)}, u32[]{:S(2)}) %collective-permute-start.6) | collective-permute-done | bytes 589856 | tf_op jit(solution)/shard_map/ppermute | solution.py:313
  77.9 0.0 collective-permute-done.7.mb
  77.9 0.9 slice.36.mx
  78.8 0.1 copy-done.7
  78.9 0.2 copy-done.8
  79.1 16.1 %shard_map.79 = (f32[192,768]{1,0:T(8,128)}, f32[192,768]{1,0:T(8,128)}, f32[192,768]{1,0:T(8,128)}, f32[192,768]{1,0:T(8,128)}) custom-call(f32[384,512]{1,0:T(8,128)} %get-tuple-element.51.rest, f32[768,768]{1,0:T(8,128)} %get-tuple-element.52.solved_in, f32[128,128]{1,0:T(8,128)} %get-tuple-element.53.inverse_2, f32[192,768]{1,0:T(8,128)} %copy-done.7, ...), custom_call_target="tpu_custom_call" | custom-call | flops 9059696640 | bytes 1024 | tf_op jit(solution)/shard_map/pallas_call | solution.py:265
  95.2 1.3 %collective-permute-start.9 = (f32[192,768]{1,0:T(8,128)}, f32[192,768]{1,0:T(8,128)S(1)}, u32[]{:S(2)}, u32[]{:S(2)}) collective-permute-start(f32[192,768]{1,0:T(8,128)} %get-tuple-element.65), channel_id=1, source_target_pairs={{0,1},{2,3},{5,6},{7,4},{8,9},{10,11},{13,14},{15,12},{16,17},{18,... | collective-permute-start | bytes 1769480 | tf_op jit(solution)/shard_map/ppermute | solution.py:313
  96.5 0.7 collective-permute-start.10
  97.2 1.3 %collective-permute-start.11 = (f32[192,768]{1,0:T(8,128)}, f32[192,768]{1,0:T(8,128)S(1)}, u32[]{:S(2)}, u32[]{:S(2)}) collective-permute-start(f32[192,768]{1,0:T(8,128)} %get-tuple-element.67), channel_id=1, source_target_pairs={{2,1},{0,3},{7,6},{5,4},{10,9},{8,11},{15,14},{13,12},{18,17},{16,... | collective-permute-start | bytes 1769480 | tf_op jit(solution)/shard_map/ppermute | solution.py:313
  98.5 1.4 %select_bitcast_fusion.5 = (f32[1,192,768]{2,1,0:T(8,128)S(1)}, f32[1,192,768]{2,1,0:T(8,128)S(1)}) fusion(pred[]{:T(512)S(6)} %lt.3, f32[192,768]{1,0:T(8,128)S(1)} %copy-done.6, f32[192,768]{1,0:T(8,128)} %copy-done.7, pred[]{:T(512)S(6)} %eq.3, f32[192,768]{1,0:T(8,128)} %copy-done.8, f32[384,768]{1,0:T(8,128)S(1)} %collective-permute-done.8), kind=kLoop, calls=%fused_computation.10 | loop fusion | flops 589824 | bytes 3538946 | tf_op jit(solution)/shard_map/stack | solution.py:326
  100.0 1.2 %fusion = f32[2,192,768]{2,1,0:T(8,128)} fusion(f32[1,192,768]{2,1,0:T(8,128)S(1)} %get-tuple-element.69, f32[1,192,768]{2,1,0:T(8,128)S(1)} %get-tuple-element.68, f32[2,192,768]{2,1,0:T(8,128)S(1)} %copy-done), kind=kLoop, calls=%fused_computation.2 | loop fusion | flops 1179648 | bytes 3538944 | tf_op jit(solution)/shard_map/add | solution.py:362
  101.2 6.1 %collective-permute-done.9 = f32[192,768]{1,0:T(8,128)S(1)} collective-permute-done((f32[192,768]{1,0:T(8,128)}, f32[192,768]{1,0:T(8,128)S(1)}, u32[]{:S(2)}, u32[]{:S(2)}) %collective-permute-start.9) | collective-permute-done | bytes 589856 | tf_op jit(solution)/shard_map/ppermute | solution.py:313
  107.3 9.2 %collective-permute-done.11 = f32[192,768]{1,0:T(8,128)S(1)} collective-permute-done((f32[192,768]{1,0:T(8,128)}, f32[192,768]{1,0:T(8,128)S(1)}, u32[]{:S(2)}, u32[]{:S(2)}) %collective-permute-start.11) | collective-permute-done | bytes 589856 | tf_op jit(solution)/shard_map/ppermute | solution.py:313
  116.5 0.1 select_bitcast_fusion.3
  116.6 1.2 %fusion.1 = f32[2,768,192]{1,2,0:T(8,128)} fusion(f32[2,768,192]{1,2,0:T(8,128)S(1)} %copy-done.1, f32[1,192,768]{2,1,0:T(8,128)S(1)} %get-tuple-element.71, f32[1,192,768]{2,1,0:T(8,128)S(1)} %get-tuple-element.70, pred[2]{0:T(512)(128)(4,1)S(1)} %broadcast_compare_fusion), kind=kLoop, calls=%fused_computation.4 | loop fusion | flops 589824 | bytes 3538946 | tf_op jit(solution)/shard_map/jit(_where)/select_n | solution.py:364
  (32 shorter events, 0.1 us)
Async XLA Ops:
  0.6 1.6 %copy-start = (f32[2,192,768]{2,1,0:T(8,128)S(1)}, f32[2,192,768]{2,1,0:T(8,128)}, u32[]{:S(2)}) copy-start(f32[2,192,768]{2,1,0:T(8,128)} %param.7) | copy-start | bytes 3538948
  2.3 8.0 %copy-start.5 = (bf16[2,768,192]{1,2,0:T(8,128)(2,1)S(1)}, bf16[2,768,192]{1,2,0:T(8,128)(2,1)}, u32[]{:S(2)}) copy-start(bf16[2,768,192]{1,2,0:T(8,128)(2,1)} %param.6) | copy-start | bytes 1769476
  3.5 10.4 %copy-start.3 = (f32[384,768]{1,0:T(8,128)}, f32[384,768]{1,0:T(8,128)S(1)}, u32[]{:S(2)}) copy-start(f32[384,768]{1,0:T(8,128)S(1)} %get-tuple-element.72.po) | copy-start | bytes 3538948
  3.5 10.2 %copy-start.1 = (f32[2,768,192]{1,2,0:T(8,128)S(1)}, f32[2,768,192]{1,2,0:T(8,128)}, u32[]{:S(2)}) copy-start(f32[2,768,192]{1,2,0:T(8,128)} %param.9) | copy-start | bytes 3538948
  3.5 26.2 %collective-permute-start = (f32[384,768]{1,0:T(8,128)}, f32[384,768]{1,0:T(8,128)S(1)}, u32[]{:S(2)}, u32[]{:S(2)}) collective-permute-start(f32[384,768]{1,0:T(8,128)} %get-tuple-element.45), channel_id=1, source_target_pairs={{1,2},{3,0},{6,7},{4,5},{9,10},{11,8},{14,15},{12,13},{17,18},{19,... | collective-permute-start | bytes 3538952 | tf_op jit(solution)/shard_map/ppermute | solution.py:313
  7.8 22.0 %collective-permute-start.1 = (f32[384,768]{1,0:T(8,128)S(1)}, f32[384,768]{1,0:T(8,128)S(1)}, u32[]{:S(2)}, u32[]{:S(2)}) collective-permute-start(f32[384,768]{1,0:T(8,128)S(1)} %get-tuple-element.72.po), channel_id=1, source_target_pairs={{1,0},{3,2},{6,5},{4,7},{9,8},{11,10},{14,13},{12,15},{17,16},{19,... | collective-permute-start | bytes 3538952 | tf_op jit(solution)/shard_map/ppermute | solution.py:313
  10.4 3.5 %copy-start.4 = (bf16[192,768]{1,0:T(8,128)(2,1)}, bf16[192,768]{1,0:T(8,128)(2,1)S(1)}, u32[]{:S(2)}) copy-start(bf16[192,768]{1,0:T(8,128)(2,1)S(1)} %get-tuple-element.38.go) | copy-start | bytes 884740
  10.4 16.9 %collective-permute-start.2 = (bf16[192,768]{1,0:T(8,128)(2,1)S(1)}, bf16[192,768]{1,0:T(8,128)(2,1)S(1)}, u32[]{:S(2)}, u32[]{:S(2)}) collective-permute-start(bf16[192,768]{1,0:T(8,128)(2,1)S(1)} %get-tuple-element.77), channel_id=1, source_target_pairs={{1,2},{3,0},{6,7},{4,5},{9,10},{11,8},{14,15},{12,13},{17,18},{19,... | collective-permute-start | bytes 884744 | tf_op jit(solution)/shard_map/ppermute | solution.py:313
  11.8 18.0 %collective-permute-start.3 = (bf16[192,768]{1,0:T(8,128)(2,1)S(1)}, bf16[192,768]{1,0:T(8,128)(2,1)S(1)}, u32[]{:S(2)}, u32[]{:S(2)}) collective-permute-start(bf16[192,768]{1,0:T(8,128)(2,1)S(1)} %get-tuple-element.38.go), channel_id=1, source_target_pairs={{1,0},{3,2},{6,5},{4,7},{9,8},{11,10},{14,13},{12,15},{17,16},{19,... | collective-permute-start | bytes 884744 | tf_op jit(solution)/shard_map/ppermute | solution.py:313
  13.1 16.7 %collective-permute-start.4 = (bf16[192,768]{1,0:T(8,128)(2,1)S(1)}, bf16[192,768]{1,0:T(8,128)(2,1)S(1)}, u32[]{:S(2)}, u32[]{:S(2)}) collective-permute-start(bf16[192,768]{1,0:T(8,128)(2,1)S(1)} %get-tuple-element.77), channel_id=1, source_target_pairs={{0,2},{2,0},{5,7},{7,5},{8,10},{10,8},{13,15},{15,13},{16,18},{18,... | collective-permute-start | bytes 884744 | tf_op jit(solution)/shard_map/ppermute | solution.py:313
  13.8 19.3 %copy-start.18 = (s32[4]{0:T(128)S(1)}, s32[4]{0:T(128)}, u32[]{:S(2)}) copy-start(s32[4]{0:T(128)} %constant.35.clone) | copy-start | bytes 52
  13.8 19.8 %copy-start.17 = (s32[2]{0:T(128)S(1)}, s32[2]{0:T(128)}, u32[]{:S(2)}) copy-start(s32[2]{0:T(128)} %param.10) | copy-start | bytes 28
  13.9 32.2 %copy-start.2 = (f32[192,768]{1,0:T(8,128)}, f32[192,768]{1,0:T(8,128)S(1)}, u32[]{:S(2)}) copy-start(f32[192,768]{1,0:T(8,128)S(1)} %get-tuple-element.50.mo) | copy-start | bytes 1769476
  27.4 2.4 %copy-start.12 = (bf16[192,768]{1,0:T(8,128)(2,1)}, bf16[192,768]{1,0:T(8,128)(2,1)S(1)}, u32[]{:S(2)}) copy-start(bf16[192,768]{1,0:T(8,128)(2,1)S(1)} %collective-permute-done.2.ga) | copy-start | bytes 884740
  29.8 0.7 copy-start.13
  29.8 0.9 copy-start.14
  29.8 1.2 %copy-start.15 = (f32[384,768]{1,0:T(8,128)}, f32[384,768]{1,0:T(8,128)S(1)}, u32[]{:S(2)}) copy-start(f32[384,768]{1,0:T(8,128)S(1)} %collective-permute-done.pa) | copy-start | bytes 3538948
  29.8 1.5 %copy-start.16 = (f32[384,768]{1,0:T(8,128)}, f32[384,768]{1,0:T(8,128)S(1)}, u32[]{:S(2)}) copy-start(f32[384,768]{1,0:T(8,128)S(1)} %collective-permute-done.1.pb) | copy-start | bytes 3538948
  31.3 16.9 %collective-permute-start.5 = (f32[384,768]{1,0:T(8,128)}, f32[384,768]{1,0:T(8,128)}, u32[]{:S(2)}, u32[]{:S(2)}) collective-permute-start(f32[384,768]{1,0:T(8,128)} %get-tuple-element.45), channel_id=1, source_target_pairs={{0,2},{2,0},{5,7},{7,5},{8,10},{10,8},{13,15},{15,13},{16,18},{18,... | collective-permute-start | bytes 3538952 | tf_op jit(solution)/shard_map/ppermute | solution.py:313
  37.4 2.1 %copy-start.11 = (f32[192,768]{1,0:T(8,128)S(1)}, f32[192,768]{1,0:T(8,128)}, u32[]{:S(2)}) copy-start(f32[192,768]{1,0:T(8,128)} %get-tuple-element.41.gb) | copy-start | bytes 1769476
  38.6 7.5 %copy-start.10 = (f32[192,768]{1,0:T(8,128)S(1)}, f32[192,768]{1,0:T(8,128)}, u32[]{:S(2)}) copy-start(f32[192,768]{1,0:T(8,128)} %get-tuple-element.40.ga) | copy-start | bytes 1769476
  38.6 39.3 %collective-permute-start.8 = (f32[384,768]{1,0:T(8,128)S(1)}, f32[384,768]{1,0:T(8,128)S(1)}, u32[]{:S(2)}, u32[]{:S(2)}) collective-permute-start(f32[384,768]{1,0:T(8,128)S(1)} %pad_maximum_fusion), channel_id=1, source_target_pairs={{0,2},{2,0},{5,7},{7,5},{8,10},{10,8},{13,15},{15,13},{16,18},{18,... | collective-permute-start | bytes 3538952 | tf_op jit(solution)/shard_map/ppermute | solution.py:313
  40.4 37.5 %collective-permute-start.6 = (f32[192,768]{1,0:T(8,128)}, f32[192,768]{1,0:T(8,128)S(1)}, u32[]{:S(2)}, u32[]{:S(2)}) collective-permute-start(f32[192,768]{1,0:T(8,128)} %broadcast_select_fusion.4), channel_id=1, source_target_pairs={{0,1},{1,2},{2,3},{3,0},{5,6},{6,7},{7,4},{4,5},{8,9},{9,10},{10,1... | collective-permute-start | bytes 1769480 | tf_op jit(solution)/shard_map/ppermute | solution.py:313
  46.2 31.7 %collective-permute-start.7 = (f32[192,768]{1,0:T(8,128)S(1)}, f32[192,768]{1,0:T(8,128)S(1)}, u32[]{:S(2)}, u32[]{:S(2)}) collective-permute-start(f32[192,768]{1,0:T(8,128)S(1)} %broadcast_select_fusion.3), channel_id=1, source_target_pairs={{0,3},{1,0},{2,1},{3,2},{5,4},{6,5},{7,6},{4,7},{8,11},{9,8},{10,9... | collective-permute-start | bytes 1769480 | tf_op jit(solution)/shard_map/ppermute | solution.py:313
  77.9 1.0 copy-start.7
  77.9 1.2 %copy-start.8 = (f32[192,768]{1,0:T(8,128)}, f32[192,768]{1,0:T(8,128)S(1)}, u32[]{:S(2)}) copy-start(f32[192,768]{1,0:T(8,128)S(1)} %collective-permute-done.7.mb) | copy-start | bytes 1769476
  79.1 19.4 %copy-start.6 = (f32[192,768]{1,0:T(8,128)S(1)}, f32[192,768]{1,0:T(8,128)}, u32[]{:S(2)}) copy-start(f32[192,768]{1,0:T(8,128)} %get-tuple-element.39.go) | copy-start | bytes 1769476
  95.2 12.0 %collective-permute-start.9 = (f32[192,768]{1,0:T(8,128)}, f32[192,768]{1,0:T(8,128)S(1)}, u32[]{:S(2)}, u32[]{:S(2)}) collective-permute-start(f32[192,768]{1,0:T(8,128)} %get-tuple-element.65), channel_id=1, source_target_pairs={{0,1},{2,3},{5,6},{7,4},{8,9},{10,11},{13,14},{15,12},{16,17},{18,... | collective-permute-start | bytes 1769480 | tf_op jit(solution)/shard_map/ppermute | solution.py:313
  96.5 10.8 %collective-permute-start.10 = (f32[192,768]{1,0:T(8,128)}, f32[192,768]{1,0:T(8,128)S(1)}, u32[]{:S(2)}, u32[]{:S(2)}) collective-permute-start(f32[192,768]{1,0:T(8,128)} %get-tuple-element.66), channel_id=1, source_target_pairs={{0,2},{2,0},{5,7},{7,5},{8,10},{10,8},{13,15},{15,13},{16,18},{18,... | collective-permute-start | bytes 1769480 | tf_op jit(solution)/shard_map/ppermute | solution.py:313
  97.2 19.2 %collective-permute-start.11 = (f32[192,768]{1,0:T(8,128)}, f32[192,768]{1,0:T(8,128)S(1)}, u32[]{:S(2)}, u32[]{:S(2)}) collective-permute-start(f32[192,768]{1,0:T(8,128)} %get-tuple-element.67), channel_id=1, source_target_pairs={{2,1},{0,3},{7,6},{5,4},{10,9},{8,11},{15,14},{13,12},{18,17},{16,... | collective-permute-start | bytes 1769480 | tf_op jit(solution)/shard_map/ppermute | solution.py:313
  99.9 16.5 %copy-start.9 = (f32[192,768]{1,0:T(8,128)S(1)}, f32[192,768]{1,0:T(8,128)}, u32[]{:S(2)}) copy-start(f32[192,768]{1,0:T(8,128)} %get-tuple-element.64) | copy-start | bytes 1769476

commit v5 on v4

--- a/solution.py
+++ b/solution.py
@@ -173,24 +173,65 @@
     return [functools.partial(piece, cols) for cols in chunks(0, solved.shape[1])]
 
 
-def gram_kernel(place, ga, gb, gx, go, ra, rb, rx, ro, whole, gram):
-    part = ga.shape[0]
-    for i, piece in enumerate((ga, gb, gx, go)):
-        whole[part * i : part * (i + 1), :] = piece[...]
+def fetch(moves, sems):
+    copies = [pltpu.make_async_copy(source, target, sems.at[i]) for i, (source, target) in enumerate(moves)]
+    for copy in copies:
+        copy.start()
+    return copies
+
+
+def wait_all(copies):
+    for copy in copies:
+        copy.wait()
+
+
+def pack_kernel(choice, basis, factor, gradient, first, second, raw, packed, sems, more_sems, out_sems):
+    part = basis.shape[1]
+    tops = [slice(0, 2 * part), slice(2 * part, 5 * part)]
+    sources = [(n, i) for n in range(2) for i in range(2)]
+    loads = fetch([((basis, factor)[i].at[choice[n]], raw.at[n, i]) for n, i in sources], sems)
+    straight = fetch([(gradient.at[choice[n]], packed.at[n, 4 * part :]) for n in range(2)], more_sems)
+    stores = []
+    for m, (n, i) in enumerate(sources):
+        loads[m].wait()
+        packed[n, 2 * part * i : 2 * part * i + part, :], packed[n, 2 * part * i + part : 2 * part * (i + 1), :] = (
+            halves(raw[n, i])
+        )
+        if i:
+            straight[n].wait()
+        stores.append(
+            pltpu.make_async_copy(packed.at[n, tops[i]], (first, second)[n].at[tops[i]], out_sems.at[m])
+        )
+        stores[-1].start()
+    wait_all(stores)
+
+
+def gram_kernel(place, ga, gb, gx, go, ra, rb, rx, ro, whole, gram, sems):
+    part = ra.shape[0]
+    pieces = [piece.at[4 * part :] for piece in (ga, gb)] + [gx, go.at[4 * part :]]
+    wait_all(fetch([(piece, whole.at[part * i : part * (i + 1)]) for i, piece in enumerate(pieces)], sems))
     gram[...] = lax.dot_general(whole[...], whole[...], TN, preferred_element_type=f32)
     for i, piece in enumerate((ra, rb, rx, ro)):
         piece[...] = gram[pl.ds(pl.multiple_of(place[i], 64), part), :]
 
 
 def power_kernel(place, ga, gb, gx, go, pa, pb, px, po, rest, solved, last_inverse,
-                 factor, basis_high, basis_low, turned_high, turned_low, table, lower_high, lower_low):
-    size, part = factor.shape[0], ga.shape[0]
+                 factor, basis_high, basis_low, turned_high, turned_low, table, lower_high, lower_low,
+                 old_high, old_low, sems):
+    size = factor.shape[0]
+    part = size // 4
     half = size // 2
     basis, turned, lower = Pair(basis_high, basis_low), Pair(turned_high, turned_low), Pair(lower_high, lower_low)
+    moves = []
     for i, (gram, piece) in enumerate(((ga, pa), (gb, pb), (gx, px), (go, po))):
         rows = pl.ds(pl.multiple_of(place[i], 64), part)
-        basis[rows, :] = piece[:part, :]
-        factor[rows, :] = ema_decay * piece[part:, :] + (1.0 - ema_decay) * gram[...]
+        moves.append((gram, factor.at[rows]))
+        for n, target in enumerate((basis_high, basis_low, old_high, old_low)):
+            moves.append((piece.at[part * n : part * (n + 1)], target.at[rows]))
+    wait_all(fetch(moves, sems))
+    factor[...] = (1.0 - ema_decay) * factor[...] + ema_decay * (
+        old_high[...].astype(f32) + old_low[...].astype(f32)
+    )
     turned[...] = dot3(basis[...], halves(factor[...]), TN)
 
     def cross(rows, cols):
@@ -220,16 +261,17 @@
     rest[:, LANES:] = table[half:, half:]
 
 
-def rotate_kernel(rest, solved_in, inverse_2, ma, mb, mx, mo, ra, rb, rx, ro,
-                  table, solved, lower_high, lower_low, moment_high, moment_low, done):
+def rotate_kernel(rest, inverse_2, solved_in, ma, mb, mx, mo, ra, rb, rx, ro,
+                  table, solved, lower_high, lower_low, moment_high, moment_low, done, raw, sems):
     size, part = solved.shape[0], ra.shape[0]
     half = size // 2
     lower, moment = Pair(lower_high, lower_low), Pair(moment_high, moment_low)
+    moves = [(solved_in, solved)]
+    for i, piece in enumerate((ma, mb, mx, mo)):
+        moves.append((piece, raw.at[part * i : part * (i + 1)]))
+    copies = fetch(moves, sems)
     table[:, half:] = rest[:, LANES:]
-    solved[...] = solved_in[...]
     lower[half:, 2 * LANES : half] = rest[:, :LANES]
-    for i, piece in enumerate((ma, mb, mx, mo)):
-        moment[part * i : part * (i + 1), :] = piece[...]
     strip = lower[half : half + LANES, block_of(2)]
     block = table[:LANES, block_of(3)] - joined(strip, strip, NT)
 
@@ -242,8 +284,12 @@
     def left(k):
         return slice((k + 1) * LANES, size)
 
-    work = trailing(table, lower, 2, size, half) + solved_row(solved, inverse_2[...], 2)
-    work += rows_update(solved, lower, left(2), block_of(2)) + products(slice(0, half))
+    def split_moment():
+        wait_all(copies[1:])
+        moment[...] = raw[...]
+
+    work = trailing(table, lower, 2, size, half) + [copies[0].wait] + solved_row(solved, inverse_2[...], 2)
+    work += rows_update(solved, lower, left(2), block_of(2)) + [split_moment] + products(slice(0, half))
     inverse = inverse_factor(block, work)
     block = panel_and_next(table, lower, inverse, 3, size, half)
     work = trailing(table, lower, 3, size, half) + solved_row(solved, inverse, 3)
@@ -258,42 +304,66 @@
         piece[...] = done[part * i : part * (i + 1), :]
 
 
-def call(kernel, outs, scratch, flops, *args, place=None):
+def call(kernel, outs, scratch, flops, remote, *args, place=None):
     smem = pl.BlockSpec(memory_space=pltpu.SMEM)
     vmem = pl.BlockSpec(memory_space=pltpu.VMEM)
     lead = () if place is None else (place,)
+    specs = [smem] * len(lead) + [vmem] * len(args) + [pl.BlockSpec(memory_space=pl.ANY)] * len(remote)
     return pl.pallas_call(
         kernel,
         out_shape=[jax.ShapeDtypeStruct(shape, dtype) for shape, dtype in outs],
-        in_specs=[smem] * len(lead) + [vmem] * len(args),
+        in_specs=specs,
         out_specs=[vmem] * len(outs),
-        scratch_shapes=[pltpu.VMEM(shape, dtype) for shape, dtype in scratch],
+        scratch_shapes=[pltpu.VMEM(shape, dtype) for shape, dtype in scratch]
+        + ([pltpu.SemaphoreType.DMA((20,))] if remote else []),
         cost_estimate=pl.CostEstimate(flops=flops, bytes_accessed=1024, transcendentals=0),
         compiler_params=pltpu.CompilerParams(vmem_limit_bytes=56 << 20),
-    )(*lead, *args)
-
-
-def gram_call(place, gradient_parts):
-    part, size = gradient_parts[0].shape
+    )(*lead, *args, *remote)
+
+
+def pack_call(choice, basis, factor, gradient):
+    part, size = basis.shape[1:]
+    stay = pl.BlockSpec(memory_space=pl.ANY)
+    return pl.pallas_call(
+        pack_kernel,
+        out_shape=[jax.ShapeDtypeStruct((5 * part, size), bf16)] * 2,
+        in_specs=[pl.BlockSpec(memory_space=pltpu.SMEM)] + [stay] * 3,
+        out_specs=[stay] * 2,
+        scratch_shapes=[
+            pltpu.VMEM((2, 2, part, size), f32),
+            pltpu.VMEM((2, 5 * part, size), bf16),
+            pltpu.SemaphoreType.DMA((4,)),
+            pltpu.SemaphoreType.DMA((2,)),
+            pltpu.SemaphoreType.DMA((4,)),
+        ],
+        cost_estimate=pl.CostEstimate(flops=1, bytes_accessed=1024, transcendentals=0),
+        compiler_params=pltpu.CompilerParams(vmem_limit_bytes=56 << 20),
+    )(choice, basis, factor, gradient)
+
+
+def gram_call(place, parts, across, part):
+    size = across.shape[1]
     whole = (size, size)
+    up, down, own = parts
     return call(gram_kernel, [((part, size), f32)] * 4, [(whole, bf16), (whole, f32)], 1,
-                *gradient_parts, place=place)
-
-
-def power_call(place, gram_parts, pair_parts):
+                [up, down, across, own], place=place)
+
+
+def power_call(place, gram_parts, parts, across):
     part, size = gram_parts[0].shape
     whole = (size, size)
+    up, down, own = parts
     outs = [((size // 2, size // 2 + LANES), f32), (whole, f32), ((LANES, LANES), f32)]
-    scratch = [(whole, f32)] + [(whole, bf16)] * 4 + [(whole, f32)] + [(whole, bf16)] * 2
-    return call(power_kernel, outs, scratch, 20 * size**3, *gram_parts, *pair_parts, place=place)
-
-
-def rotate_call(rest, solved, inverse, moment_parts):
-    part, size = moment_parts[0].shape
+    scratch = [(whole, f32)] + [(whole, bf16)] * 4 + [(whole, f32)] + [(whole, bf16)] * 4
+    return call(power_kernel, outs, scratch, 20 * size**3, [*gram_parts, up, down, across, own], place=place)
+
+
+def rotate_call(rest, solved, inverse, up, down, across, own):
+    part, size = own.shape
     whole = (size, size)
     outs = [((part, size), f32)] * 4
-    scratch = [((size // 2, size), f32), (whole, f32)] + [(whole, bf16)] * 4 + [(whole, f32)]
-    return call(rotate_kernel, outs, scratch, 20 * size**3, rest, solved, inverse, *moment_parts)
+    scratch = [((size // 2, size), f32), (whole, f32)] + [(whole, bf16)] * 4 + [(whole, f32)] * 2
+    return call(rotate_kernel, outs, scratch, 20 * size**3, [solved, up, down, across, own], rest, inverse)
 
 
 def on_device(gradient, factor, eigenbasis, moment, refresh_due):
@@ -319,9 +389,6 @@
     def choose(value):
         return jnp.where(first_is_1, value[1], value[0]), jnp.where(first_is_1, value[0], value[1])
 
-    def send(first, second):
-        return exchange(first, up), exchange(second, down), exchange(first, across), second
-
     def arrange(first, second):
         return jnp.stack([jnp.where(first_is_1, second, first), jnp.where(first_is_1, first, second)])
 
@@ -332,32 +399,31 @@
 
     place = lax.rem(position + jnp.array([3, 1, 2, 0], jnp.int32), ring) * part
 
-    gradient_first, gradient_second = choose(jnp.swapaxes(gradient, 1, 2))
-    pair_first, pair_second = choose(jnp.concatenate([eigenbasis, factor], 1))
+    one = first_is_1.astype(jnp.int32)
+    first, second = pack_call(jnp.stack([one, 1 - one]), eigenbasis, factor, jnp.swapaxes(gradient, 1, 2))
     moment_first, moment_second = choose(jnp.swapaxes(moment, 1, 2))
-    pair_up, pair_down = exchange(pair_first, up), exchange(pair_second, down)
-    gradient_parts = send(gradient_first, gradient_second)
-    pair_first, pair_up, pair_down, gradient_parts, moment_first, moment_second = lax.optimization_barrier(
-        (pair_first, pair_up, pair_down, gradient_parts, moment_first, moment_second)
-    )
-    pair_parts = (pair_up, pair_down, exchange(pair_first, across), pair_second)
-    gram_parts = gram_call(place, gradient_parts)
+    parts = [exchange(first, up), exchange(second, down), second]
+    gradient_across = exchange(first[4 * part :], across)
+    pair_across = exchange(first[: 4 * part], across)
+    parts, gradient_across, moment_first, moment_second = lax.optimization_barrier(
+        (parts, gradient_across, moment_first, moment_second)
+    )
+    gram_parts = gram_call(place, parts, gradient_across, part)
     to_next = jnp.where(owns, gram_parts[1], moment_first)
     to_last = jnp.where(owns, gram_parts[0], moment_second)
     from_last = exchange(to_next, [(a, (a + 1) % ring) for a in range(ring)])
     from_next = exchange(to_last, [(a, (a - 1) % ring) for a in range(ring)])
-    from_across = exchange(jnp.concatenate([moment_first, gram_parts[2]], 0), across)
-    powered = power_call(place, gram_parts, pair_parts)
-    powered, from_last, from_next, from_across = lax.optimization_barrier(
-        (powered, from_last, from_next, from_across)
-    )
-    moment_parts = (from_last, from_next, from_across[:part], moment_second)
-    rotated_parts = rotate_call(*powered, moment_parts)
-    rotated_parts, from_last, from_next, from_across = lax.optimization_barrier(
-        (rotated_parts, from_last, from_next, from_across)
+    moment_across, gram_across = exchange(moment_first, across), exchange(gram_parts[2], across)
+    powered = power_call(place, gram_parts, parts, pair_across)
+    powered, from_last, from_next, moment_across = lax.optimization_barrier(
+        (powered, from_last, from_next, moment_across)
+    )
+    rotated_parts = rotate_call(*powered, from_last, from_next, moment_across, moment_second)
+    rotated_parts, from_last, from_next, gram_across = lax.optimization_barrier(
+        (rotated_parts, from_last, from_next, gram_across)
     )
     gram_rows = arrange(
-        jnp.where(owns, from_across[part:], from_next), jnp.where(owns, gram_parts[3], from_last)
+        jnp.where(owns, gram_across, from_next), jnp.where(owns, gram_parts[3], from_last)
     )
     factor_new = ema_decay * factor + (1.0 - ema_decay) * gram_rows
     rotated = jnp.swapaxes(give_back(rotated_parts), 1, 2)

time: 118 us -> 119 us (level)
  the two profiles are of different devices: /device:TPU:1 before, /device:TPU:4 now
where the time goes in v5:
time: 119 us; the launch traced here: 118 us
  Pallas kernels  45.9 us (39%)
  waiting for transfers between devices  35.4 us (30%)
  starting transfers between devices  25.6 us (22%)
  other arithmetic  5.33 us (4%)
  local copies, waits for them, and re-layouts  4.38 us (4%)
    pallas_call x3, Pallas kernels, call(): pl.pallas_call(kernel, out_shape=[jax.ShapeDtypeStruct(shape, dtype) for...  42.4 us
    ppermute x11, waiting for transfers between devices, exchange(): return lax.ppermute(value, ('dp', 'tensor'), pairs)  35.4 us
    ppermute x11, starting transfers between devices, exchange(): return lax.ppermute(value, ('dp', 'tensor'), pairs)  25.6 us
    pallas_call x1, Pallas kernels, pack_call(): pl.pallas_call(pack_kernel, out_shape=[jax.ShapeDtypeStruct((5 * part, si...  3.47 us
  transfers between devices with their start and end apart: 11, of which 5 were waited for; matrix products, arithmetic and copies ran while one was open for 6% of the time, Pallas kernels for 36%

profile of v5, /device:TPU:4, one launch (start us, length us, event | category | flops | bytes accessed | tf_op | source)
XLA Modules:
  0.0 117.6 jit_solution(12262119826843591155)
XLA Ops:
  0.6 0.6 pad_add_fusion.choice
  1.3 3.5 %shard_map.77 = (bf16[960,768]{1,0:T(8,128)(2,1)}, bf16[960,768]{1,0:T(8,128)(2,1)}) custom-call(s32[2]{0:T(128)} %pad_add_fusion.choice, f32[2,192,768]{2,1,0:T(8,128)} %basis.1, f32[2,192,768]{2,1,0:T(8,128)} %factor.1, bf16[2,192,768]{2,1,0:T(8,128)(2,1)} %bitcast.21), custom_call_target="tpu_custom_call" | custom-call | flops 1 | bytes 1024 | tf_op jit(solution)/shard_map/pallas_call | solution.py:327
  4.8 1.3 %collective-permute-start = (bf16[960,768]{1,0:T(8,128)(2,1)}, bf16[960,768]{1,0:T(8,128)(2,1)S(1)}, u32[]{:S(2)}, u32[]{:S(2)}) collective-permute-start(bf16[960,768]{1,0:T(8,128)(2,1)} %get-tuple-element.34), channel_id=1, source_target_pairs={{1,2},{3,0},{6,7},{4,5},{9,10},{11,8},{14,15},{12,13},{17,18},{19,... | collective-permute-start | bytes 4423688 | tf_op jit(solution)/shard_map/ppermute | solution.py:383
  6.1 1.3 %collective-permute-start.1 = (bf16[960,768]{1,0:T(8,128)(2,1)}, bf16[960,768]{1,0:T(8,128)(2,1)}, u32[]{:S(2)}, u32[]{:S(2)}) collective-permute-start(bf16[960,768]{1,0:T(8,128)(2,1)} %get-tuple-element.39.go.po), channel_id=1, source_target_pairs={{1,0},{3,2},{6,5},{4,7},{9,8},{11,10},{14,13},{12,15},{17,16},{19,... | collective-permute-start | bytes 4423688 | tf_op jit(solution)/shard_map/ppermute | solution.py:383
  7.4 1.0 slice.14
  8.4 0.0 copy-start.12
  8.4 0.0 copy-start.11
  8.4 0.0 copy-start.1
  8.4 4.3 %collective-permute-start.2 = (bf16[192,768]{1,0:T(8,128)(2,1)S(1)}, bf16[192,768]{1,0:T(8,128)(2,1)S(1)}, u32[]{:S(2)}, u32[]{:S(2)}) collective-permute-start(bf16[192,768]{1,0:T(8,128)(2,1)S(1)} %slice.14), channel_id=1, source_target_pairs={{0,2},{2,0},{5,7},{7,5},{8,10},{10,8},{13,15},{15,13},{16,18},{18,... | collective-permute-start | bytes 884744 | tf_op jit(solution)/shard_map/ppermute | solution.py:383
  12.7 2.4 %slice.17 = bf16[768,768]{1,0:T(8,128)(2,1)} slice(bf16[960,768]{1,0:T(8,128)(2,1)} %get-tuple-element.34), slice={[0:768], [0:768]} | slice | bytes 2359296 | tf_op jit(solution)/shard_map/slice | solution.py:407
  15.0 3.2 %collective-permute-start.3 = (bf16[768,768]{1,0:T(8,128)(2,1)}, bf16[768,768]{1,0:T(8,128)(2,1)}, u32[]{:S(2)}, u32[]{:S(2)}) collective-permute-start(bf16[768,768]{1,0:T(8,128)(2,1)} %slice.17), channel_id=1, source_target_pairs={{0,2},{2,0},{5,7},{7,5},{8,10},{10,8},{13,15},{15,13},{16,18},{18,... | collective-permute-start | bytes 3538952 | tf_op jit(solution)/shard_map/ppermute | solution.py:383
  18.2 0.0 copy-done.12
  18.2 0.6 fusion.3.place
  18.9 0.1 select_bitcast_fusion.4
  18.9 0.0 copy-start.2
  19.0 2.9 %collective-permute-done.2.gx = bf16[192,768]{1,0:T(8,128)(2,1)S(1)} collective-permute-done((bf16[192,768]{1,0:T(8,128)(2,1)S(1)}, bf16[192,768]{1,0:T(8,128)(2,1)S(1)}, u32[]{:S(2)}, u32[]{:S(2)}) %collective-permute-start.2) | collective-permute-done | bytes 294944 | tf_op jit(solution)/shard_map/ppermute | solution.py:383
  21.9 20.2 %collective-permute-done.ga.pa = bf16[960,768]{1,0:T(8,128)(2,1)S(1)} collective-permute-done((bf16[960,768]{1,0:T(8,128)(2,1)}, bf16[960,768]{1,0:T(8,128)(2,1)S(1)}, u32[]{:S(2)}, u32[]{:S(2)}) %collective-permute-start) | collective-permute-done | bytes 1474592 | tf_op jit(solution)/shard_map/ppermute | solution.py:383
  42.0 2.6 %collective-permute-done.1.gb.pb = bf16[960,768]{1,0:T(8,128)(2,1)} collective-permute-done((bf16[960,768]{1,0:T(8,128)(2,1)}, bf16[960,768]{1,0:T(8,128)(2,1)}, u32[]{:S(2)}, u32[]{:S(2)}) %collective-permute-start.1) | collective-permute-done | bytes 1474592 | tf_op jit(solution)/shard_map/ppermute | solution.py:383
  44.6 2.8 %collective-permute-start.6 = (f32[192,768]{1,0:T(8,128)S(1)}, f32[192,768]{1,0:T(8,128)}, u32[]{:S(2)}, u32[]{:S(2)}) collective-permute-start(f32[192,768]{1,0:T(8,128)S(1)} %get-tuple-element.47), channel_id=1, source_target_pairs={{0,2},{2,0},{5,7},{7,5},{8,10},{10,8},{13,15},{15,13},{16,18},{18,... | collective-permute-start | bytes 1769480 | tf_op jit(solution)/shard_map/ppermute | solution.py:383
  47.4 4.7 %shard_map.78 = (f32[192,768]{1,0:T(8,128)}, f32[192,768]{1,0:T(8,128)}, f32[192,768]{1,0:T(8,128)}, f32[192,768]{1,0:T(8,128)}) custom-call(s32[4]{0:T(128)} %fusion.3.place, bf16[960,768]{1,0:T(8,128)(2,1)} %copy-done.3, bf16[960,768]{1,0:T(8,128)(2,1)} %collective-permute-done.1.gb.pb, bf16[192,768]{1,0:T(8,128)(2,1)} %copy-done.9, ...), custom_call_target="tpu_custom_call" | custom-call | flops 1 | bytes 1024 | tf_op jit(solution)/shard_map/pallas_call | solution.py:312
  52.1 0.0 copy-start.8
  52.1 1.2 %broadcast_select_fusion.5 = f32[192,768]{1,0:T(8,128)S(1)} fusion(f32[192,768]{1,0:T(8,128)} %get-tuple-element.42.gb, f32[192,768]{1,0:T(8,128)S(1)} %get-tuple-element.47, pred[]{:T(512)S(6)} %eq.3), kind=kLoop, calls=%fused_computation.15 | loop fusion | flops 147456 | bytes 1769473 | tf_op jit(solution)/shard_map/jit(_where)/select_n | solution.py:412
  53.3 0.1 collective-permute-start.4
  53.4 0.0 copy-done.2
  53.4 0.1 broadcast_select_fusion.4
  53.5 2.1 %collective-permute-start.5 = (f32[192,768]{1,0:T(8,128)S(1)}, f32[192,768]{1,0:T(8,128)S(1)}, u32[]{:S(2)}, u32[]{:S(2)}) collective-permute-start(f32[192,768]{1,0:T(8,128)S(1)} %broadcast_select_fusion.4), channel_id=1, source_target_pairs={{0,3},{1,0},{2,1},{3,2},{5,4},{6,5},{7,6},{4,7},{8,11},{9,8},{10,9... | collective-permute-start | bytes 1769480 | tf_op jit(solution)/shard_map/ppermute | solution.py:383
  55.6 6.0 %collective-permute-start.7 = (f32[192,768]{1,0:T(8,128)S(1)}, f32[192,768]{1,0:T(8,128)S(1)}, u32[]{:S(2)}, u32[]{:S(2)}) collective-permute-start(f32[192,768]{1,0:T(8,128)S(1)} %copy-done.10), channel_id=1, source_target_pairs={{0,2},{2,0},{5,7},{7,5},{8,10},{10,8},{13,15},{15,13},{16,18},{18,... | collective-permute-start | bytes 1769480 | tf_op jit(solution)/shard_map/ppermute | solution.py:383
  61.6 0.0 collective-permute-done.3.px
  61.6 21.6 %shard_map.79 = (f32[384,512]{1,0:T(8,128)}, f32[768,768]{1,0:T(8,128)}, f32[128,128]{1,0:T(8,128)}) custom-call(s32[4]{0:T(128)} %fusion.3.place, f32[192,768]{1,0:T(8,128)} %get-tuple-element.41.ga, f32[192,768]{1,0:T(8,128)} %get-tuple-element.42.gb, f32[192,768]{1,0:T(8,128)} %get-tuple-element.43.gx, f32[192,768]{1,0:T(8,128)} %get-tuple-element.40.go, ...), custom_call_target="tpu_custom_call" | custom-call | flops 9059696640 | bytes 1024 | tf_op jit(solution)/shard_map/pallas_call | solution.py:312
  83.2 0.0 collective-permute-done.4.ma
  83.2 0.0 copy-start.5
  83.2 0.0 collective-permute-done.5.mb
  83.2 0.0 collective-permute-done.6.mx
  83.2 0.8 copy-done.5
  84.0 0.2 copy-done.6
  84.2 16.2 %shard_map.80 = (f32[192,768]{1,0:T(8,128)}, f32[192,768]{1,0:T(8,128)}, f32[192,768]{1,0:T(8,128)}, f32[192,768]{1,0:T(8,128)}) custom-call(f32[384,512]{1,0:T(8,128)} %get-tuple-element.49.rest, f32[128,128]{1,0:T(8,128)} %get-tuple-element.50.inverse_2, f32[768,768]{1,0:T(8,128)} %get-tuple-element.51.solved_in, f32[192,768]{1,0:T(8,128)} %copy-done.5, ...), custom_call_target="tpu_custom_call" | custom-call | flops 9059696640 | bytes 1024 | tf_op jit(solution)/shard_map/pallas_call | solution.py:312
  100.4 0.0 collective-permute-done.7
  100.4 0.0 copy-start
  100.4 1.5 %collective-permute-start.8 = (f32[192,768]{1,0:T(8,128)}, f32[192,768]{1,0:T(8,128)S(1)}, u32[]{:S(2)}, u32[]{:S(2)}) collective-permute-start(f32[192,768]{1,0:T(8,128)} %get-tuple-element.63), channel_id=1, source_target_pairs={{0,1},{2,3},{5,6},{7,4},{8,9},{10,11},{13,14},{15,12},{16,17},{18,... | collective-permute-start | bytes 1769480 | tf_op jit(solution)/shard_map/ppermute | solution.py:383
  101.9 1.9 %collective-permute-start.9 = (f32[192,768]{1,0:T(8,128)}, f32[192,768]{1,0:T(8,128)S(1)}, u32[]{:S(2)}, u32[]{:S(2)}) collective-permute-start(f32[192,768]{1,0:T(8,128)} %get-tuple-element.64), channel_id=1, source_target_pairs={{0,2},{2,0},{5,7},{7,5},{8,10},{10,8},{13,15},{15,13},{16,18},{18,... | collective-permute-start | bytes 1769480 | tf_op jit(solution)/shard_map/ppermute | solution.py:383
  103.8 1.3 %collective-permute-start.10 = (f32[192,768]{1,0:T(8,128)}, f32[192,768]{1,0:T(8,128)S(1)}, u32[]{:S(2)}, u32[]{:S(2)}) collective-permute-start(f32[192,768]{1,0:T(8,128)} %get-tuple-element.65), channel_id=1, source_target_pairs={{2,1},{0,3},{7,6},{5,4},{10,9},{8,11},{15,14},{13,12},{18,17},{16,... | collective-permute-start | bytes 1769480 | tf_op jit(solution)/shard_map/ppermute | solution.py:383
  105.2 0.2 select_bitcast_fusion.3
  105.3 1.2 %fusion = f32[2,192,768]{2,1,0:T(8,128)} fusion(f32[1,192,768]{2,1,0:T(8,128)S(1)} %get-tuple-element.69, f32[1,192,768]{2,1,0:T(8,128)S(1)} %get-tuple-element.68, f32[2,192,768]{2,1,0:T(8,128)S(1)} %copy-done), kind=kLoop, calls=%fused_computation.1 | loop fusion | flops 1179648 | bytes 3538944 | tf_op jit(solution)/shard_map/add | solution.py:428
  106.5 3.0 %collective-permute-done.8 = f32[192,768]{1,0:T(8,128)S(1)} collective-permute-done((f32[192,768]{1,0:T(8,128)}, f32[192,768]{1,0:T(8,128)S(1)}, u32[]{:S(2)}, u32[]{:S(2)}) %collective-permute-start.8) | collective-permute-done | bytes 589856 | tf_op jit(solution)/shard_map/ppermute | solution.py:383
  109.5 6.7 %collective-permute-done.9 = f32[192,768]{1,0:T(8,128)S(1)} collective-permute-done((f32[192,768]{1,0:T(8,128)}, f32[192,768]{1,0:T(8,128)S(1)}, u32[]{:S(2)}, u32[]{:S(2)}) %collective-permute-start.9) | collective-permute-done | bytes 589856 | tf_op jit(solution)/shard_map/ppermute | solution.py:383
  116.2 0.0 collective-permute-done.10
  116.2 0.1 select_bitcast_fusion.1
  116.4 1.2 %fusion.1 = f32[2,768,192]{1,2,0:T(8,128)} fusion(f32[2,768,192]{1,2,0:T(8,128)S(1)} %copy-done.1, f32[1,192,768]{2,1,0:T(8,128)S(1)} %get-tuple-element.67, f32[1,192,768]{2,1,0:T(8,128)S(1)} %get-tuple-element.66, pred[2]{0:T(512)(128)(4,1)S(1)} %broadcast_compare_fusion), kind=kLoop, calls=%fused_computation.3 | loop fusion | flops 589824 | bytes 3538946 | tf_op jit(solution)/shard_map/jit(_where)/select_n | solution.py:430
  (16 shorter events, 0.0 us)
Async XLA Ops:
  4.8 37.3 %collective-permute-start = (bf16[960,768]{1,0:T(8,128)(2,1)}, bf16[960,768]{1,0:T(8,128)(2,1)S(1)}, u32[]{:S(2)}, u32[]{:S(2)}) collective-permute-start(bf16[960,768]{1,0:T(8,128)(2,1)} %get-tuple-element.34), channel_id=1, source_target_pairs={{1,2},{3,0},{6,7},{4,5},{9,10},{11,8},{14,15},{12,13},{17,18},{19,... | collective-permute-start | bytes 4423688 | tf_op jit(solution)/shard_map/ppermute | solution.py:383
  6.1 38.6 %collective-permute-start.1 = (bf16[960,768]{1,0:T(8,128)(2,1)}, bf16[960,768]{1,0:T(8,128)(2,1)}, u32[]{:S(2)}, u32[]{:S(2)}) collective-permute-start(bf16[960,768]{1,0:T(8,128)(2,1)} %get-tuple-element.39.go.po), channel_id=1, source_target_pairs={{1,0},{3,2},{6,5},{4,7},{9,8},{11,10},{14,13},{12,15},{17,16},{19,... | collective-permute-start | bytes 4423688 | tf_op jit(solution)/shard_map/ppermute | solution.py:383
  8.4 9.9 %copy-start.12 = (s32[4]{0:T(128)S(1)}, s32[4]{0:T(128)}, u32[]{:S(2)}) copy-start(s32[4]{0:T(128)} %constant.36.clone) | copy-start | bytes 52
  8.4 10.5 %copy-start.11 = (s32[2]{0:T(128)S(1)}, s32[2]{0:T(128)}, u32[]{:S(2)}) copy-start(s32[2]{0:T(128)} %param.10) | copy-start | bytes 28
  8.4 10.5 %copy-start.1 = (f32[2,768,192]{1,2,0:T(8,128)S(1)}, f32[2,768,192]{1,2,0:T(8,128)}, u32[]{:S(2)}) copy-start(f32[2,768,192]{1,2,0:T(8,128)} %param.9) | copy-start | bytes 3538948
  8.4 13.5 %collective-permute-start.2 = (bf16[192,768]{1,0:T(8,128)(2,1)S(1)}, bf16[192,768]{1,0:T(8,128)(2,1)S(1)}, u32[]{:S(2)}, u32[]{:S(2)}) collective-permute-start(bf16[192,768]{1,0:T(8,128)(2,1)S(1)} %slice.14), channel_id=1, source_target_pairs={{0,2},{2,0},{5,7},{7,5},{8,10},{10,8},{13,15},{15,13},{16,18},{18,... | collective-permute-start | bytes 884744 | tf_op jit(solution)/shard_map/ppermute | solution.py:383
  15.0 46.5 %collective-permute-start.3 = (bf16[768,768]{1,0:T(8,128)(2,1)}, bf16[768,768]{1,0:T(8,128)(2,1)}, u32[]{:S(2)}, u32[]{:S(2)}) collective-permute-start(bf16[768,768]{1,0:T(8,128)(2,1)} %slice.17), channel_id=1, source_target_pairs={{0,2},{2,0},{5,7},{7,5},{8,10},{10,8},{13,15},{15,13},{16,18},{18,... | collective-permute-start | bytes 3538952 | tf_op jit(solution)/shard_map/ppermute | solution.py:383
  18.9 34.5 %copy-start.2 = (f32[192,768]{1,0:T(8,128)}, f32[192,768]{1,0:T(8,128)S(1)}, u32[]{:S(2)}) copy-start(f32[192,768]{1,0:T(8,128)S(1)} %get-tuple-element.48.mo) | copy-start | bytes 1769476
  21.9 25.5 %copy-start.9 = (bf16[192,768]{1,0:T(8,128)(2,1)}, bf16[192,768]{1,0:T(8,128)(2,1)S(1)}, u32[]{:S(2)}) copy-start(bf16[192,768]{1,0:T(8,128)(2,1)S(1)} %collective-permute-done.2.gx) | copy-start | bytes 884740
  42.0 5.4 %copy-start.3 = (bf16[960,768]{1,0:T(8,128)(2,1)}, bf16[960,768]{1,0:T(8,128)(2,1)S(1)}, u32[]{:S(2)}) copy-start(bf16[960,768]{1,0:T(8,128)(2,1)S(1)} %collective-permute-done.ga.pa) | copy-start | bytes 4423684
  44.6 38.6 %collective-permute-start.6 = (f32[192,768]{1,0:T(8,128)S(1)}, f32[192,768]{1,0:T(8,128)}, u32[]{:S(2)}, u32[]{:S(2)}) collective-permute-start(f32[192,768]{1,0:T(8,128)S(1)} %get-tuple-element.47), channel_id=1, source_target_pairs={{0,2},{2,0},{5,7},{7,5},{8,10},{10,8},{13,15},{15,13},{16,18},{18,... | collective-permute-start | bytes 1769480 | tf_op jit(solution)/shard_map/ppermute | solution.py:383
  52.1 1.3 %copy-start.8 = (f32[192,768]{1,0:T(8,128)S(1)}, f32[192,768]{1,0:T(8,128)}, u32[]{:S(2)}) copy-start(f32[192,768]{1,0:T(8,128)} %get-tuple-element.41.ga) | copy-start | bytes 1769476
  53.3 2.3 %copy-start.10 = (f32[192,768]{1,0:T(8,128)S(1)}, f32[192,768]{1,0:T(8,128)}, u32[]{:S(2)}) copy-start(f32[192,768]{1,0:T(8,128)} %get-tuple-element.43.gx) | copy-start | bytes 1769476
  53.3 29.8 %collective-permute-start.4 = (f32[192,768]{1,0:T(8,128)S(1)}, f32[192,768]{1,0:T(8,128)S(1)}, u32[]{:S(2)}, u32[]{:S(2)}) collective-permute-start(f32[192,768]{1,0:T(8,128)S(1)} %broadcast_select_fusion.5), channel_id=1, source_target_pairs={{0,1},{1,2},{2,3},{3,0},{5,6},{6,7},{7,4},{4,5},{8,9},{9,10},{10,1... | collective-permute-start | bytes 1769480 | tf_op jit(solution)/shard_map/ppermute | solution.py:383
  53.5 29.7 %collective-permute-start.5 = (f32[192,768]{1,0:T(8,128)S(1)}, f32[192,768]{1,0:T(8,128)S(1)}, u32[]{:S(2)}, u32[]{:S(2)}) collective-permute-start(f32[192,768]{1,0:T(8,128)S(1)} %broadcast_select_fusion.4), channel_id=1, source_target_pairs={{0,3},{1,0},{2,1},{3,2},{5,4},{6,5},{7,6},{4,7},{8,11},{9,8},{10,9... | collective-permute-start | bytes 1769480 | tf_op jit(solution)/shard_map/ppermute | solution.py:383
  55.6 44.8 %collective-permute-start.7 = (f32[192,768]{1,0:T(8,128)S(1)}, f32[192,768]{1,0:T(8,128)S(1)}, u32[]{:S(2)}, u32[]{:S(2)}) collective-permute-start(f32[192,768]{1,0:T(8,128)S(1)} %copy-done.10), channel_id=1, source_target_pairs={{0,2},{2,0},{5,7},{7,5},{8,10},{10,8},{13,15},{15,13},{16,18},{18,... | collective-permute-start | bytes 1769480 | tf_op jit(solution)/shard_map/ppermute | solution.py:383
  83.2 0.8 copy-start.5
  83.2 1.0 copy-start.6
  84.2 20.9 %copy-start.4 = (f32[192,768]{1,0:T(8,128)S(1)}, f32[192,768]{1,0:T(8,128)}, u32[]{:S(2)}) copy-start(f32[192,768]{1,0:T(8,128)} %get-tuple-element.40.go) | copy-start | bytes 1769476
  100.4 4.9 %copy-start = (f32[2,192,768]{2,1,0:T(8,128)S(1)}, f32[2,192,768]{2,1,0:T(8,128)}, u32[]{:S(2)}) copy-start(f32[2,192,768]{2,1,0:T(8,128)} %factor.1) | copy-start | bytes 3538948
  100.4 9.1 %collective-permute-start.8 = (f32[192,768]{1,0:T(8,128)}, f32[192,768]{1,0:T(8,128)S(1)}, u32[]{:S(2)}, u32[]{:S(2)}) collective-permute-start(f32[192,768]{1,0:T(8,128)} %get-tuple-element.63), channel_id=1, source_target_pairs={{0,1},{2,3},{5,6},{7,4},{8,9},{10,11},{13,14},{15,12},{16,17},{18,... | collective-permute-start | bytes 1769480 | tf_op jit(solution)/shard_map/ppermute | solution.py:383
  101.9 14.4 %collective-permute-start.9 = (f32[192,768]{1,0:T(8,128)}, f32[192,768]{1,0:T(8,128)S(1)}, u32[]{:S(2)}, u32[]{:S(2)}) collective-permute-start(f32[192,768]{1,0:T(8,128)} %get-tuple-element.64), channel_id=1, source_target_pairs={{0,2},{2,0},{5,7},{7,5},{8,10},{10,8},{13,15},{15,13},{16,18},{18,... | collective-permute-start | bytes 1769480 | tf_op jit(solution)/shard_map/ppermute | solution.py:383
  103.8 12.4 %collective-permute-start.10 = (f32[192,768]{1,0:T(8,128)}, f32[192,768]{1,0:T(8,128)S(1)}, u32[]{:S(2)}, u32[]{:S(2)}) collective-permute-start(f32[192,768]{1,0:T(8,128)} %get-tuple-element.65), channel_id=1, source_target_pairs={{2,1},{0,3},{7,6},{5,4},{10,9},{8,11},{15,14},{13,12},{18,17},{16,... | collective-permute-start | bytes 1769480 | tf_op jit(solution)/shard_map/ppermute | solution.py:383
  105.3 10.9 %copy-start.7 = (f32[192,768]{1,0:T(8,128)S(1)}, f32[192,768]{1,0:T(8,128)}, u32[]{:S(2)}) copy-start(f32[192,768]{1,0:T(8,128)} %get-tuple-element.62) | copy-start | bytes 1769476

commit v6 on v5

--- a/solution.py
+++ b/solution.py
@@ -206,30 +206,39 @@
     wait_all(stores)
 
 
-def gram_kernel(place, ga, gb, gx, go, ra, rb, rx, ro, whole, gram, sems):
-    part = ra.shape[0]
-    pieces = [piece.at[4 * part :] for piece in (ga, gb)] + [gx, go.at[4 * part :]]
-    wait_all(fetch([(piece, whole.at[part * i : part * (i + 1)]) for i, piece in enumerate(pieces)], sems))
-    gram[...] = lax.dot_general(whole[...], whole[...], TN, preferred_element_type=f32)
-    for i, piece in enumerate((ra, rb, rx, ro)):
-        piece[...] = gram[pl.ds(pl.multiple_of(place[i], 64), part), :]
-
-
-def power_kernel(place, ga, gb, gx, go, pa, pb, px, po, rest, solved, last_inverse,
-                 factor, basis_high, basis_low, turned_high, turned_low, table, lower_high, lower_low,
-                 old_high, old_low, sems):
+def code(values, column, out, powers, place, row):
+    rows = slice(row, row + values.shape[0])
+    largest = jnp.maximum(jnp.max(jnp.abs(values), axis=1, keepdims=True), 1e-30)
+    power = jnp.ceil(jnp.log2(largest))
+    steps = jnp.floor(values * jnp.exp2(15.0 - power) + 0.5)
+    out[rows, block_of(column)] = jnp.clip(steps, -32767.0, 32767.0).astype(jnp.int32).astype(jnp.int16)
+    lanes = lax.broadcasted_iota(jnp.int32, values.shape, 1)
+    powers[place, rows, :] = jnp.where(lanes == column, power, powers[place, rows, :])
+
+
+def refresh_kernel(place, ma, mb, mx, mo, pa, pb, px, po, ra, rb, rx, ro,
+                   factor, basis_high, basis_low, turned_high, turned_low, table, lower_high, lower_low,
+                   old_high, old_low, whole, gram, solved, raw, moment_high, moment_low, done, powers, sems):
     size = factor.shape[0]
     part = size // 4
-    half = size // 2
     basis, turned, lower = Pair(basis_high, basis_low), Pair(turned_high, turned_low), Pair(lower_high, lower_low)
+    moment = Pair(moment_high, moment_low)
+    outs = (ra, rb, rx, ro)
     moves = []
-    for i, (gram, piece) in enumerate(((ga, pa), (gb, pb), (gx, px), (go, po))):
+    for i, piece in enumerate((pa, pb, px, po)):
+        moves.append((piece.at[4 * part :], whole.at[part * i : part * (i + 1)]))
+    for i, piece in enumerate((pa, pb, px, po)):
         rows = pl.ds(pl.multiple_of(place[i], 64), part)
-        moves.append((gram, factor.at[rows]))
-        for n, target in enumerate((basis_high, basis_low, old_high, old_low)):
-            moves.append((piece.at[part * n : part * (n + 1)], target.at[rows]))
-    wait_all(fetch(moves, sems))
-    factor[...] = (1.0 - ema_decay) * factor[...] + ema_decay * (
+        for n, target in enumerate((old_high, old_low, basis_high, basis_low)):
+            source = piece.at[part * ((n + 2) % 4) : part * ((n + 2) % 4 + 1)]
+            moves.append((source, target.at[rows]))
+    for i, piece in enumerate((ma, mb, mx, mo)):
+        moves.append((piece, raw.at[part * i : part * (i + 1)]))
+    copies = fetch(moves, sems)
+    wait_all(copies[:4])
+    gram[...] = lax.dot_general(whole[...], whole[...], TN, preferred_element_type=f32)
+    wait_all(copies[4:20])
+    factor[...] = (1.0 - ema_decay) * gram[...] + ema_decay * (
         old_high[...].astype(f32) + old_low[...].astype(f32)
     )
     turned[...] = dot3(basis[...], halves(factor[...]), TN)
@@ -240,68 +249,106 @@
     def start(rows, cols):
         solved[rows, cols] = dot3(turned[rows, :], basis[:, cols], NN)
 
-    whole = chunks(0, size)
-    part_of = functools.partial
-    first = turned[:LANES, :]
-    block = dot3(first, first, NT)
-    work = [part_of(cross, rows, cols) for cols in whole for rows in whole if rows.start >= cols.start]
-    work += [part_of(start, whole[0], cols) for cols in whole]
-    inverse = [inverse_factor(block, work)]
-    block = panel_and_next(table, lower, inverse[0], 0, size)
-    work = trailing(table, lower, 0, size) + solved_row(solved, inverse[0], 0)
-    work += [part_of(start, whole[1], cols) for cols in whole]
-    inverse.append(inverse_factor(block, work))
-    block = panel_and_next(table, lower, inverse[1], 1, size)
-    work = trailing(table, lower, 1, size) + [part_of(start, whole[2], cols) for cols in whole]
-    work += rows_update(solved, lower, block_of(1), block_of(0)) + solved_row(solved, inverse[1], 1)
-    work += rows_update(solved, lower, slice(2 * LANES, size), slice(0, 2 * LANES))
-    inverse.append(inverse_factor(block, work))
-    last_inverse[...] = inverse[2]
-    rest[:, :LANES] = joined(halves(table[half:, 2 * LANES : half]), halves(inverse[2]), NT)
-    rest[:, LANES:] = table[half:, half:]
-
-
-def rotate_kernel(rest, inverse_2, solved_in, ma, mb, mx, mo, ra, rb, rx, ro,
-                  table, solved, lower_high, lower_low, moment_high, moment_low, done, raw, sems):
-    size, part = solved.shape[0], ra.shape[0]
-    half = size // 2
-    lower, moment = Pair(lower_high, lower_low), Pair(moment_high, moment_low)
-    moves = [(solved_in, solved)]
-    for i, piece in enumerate((ma, mb, mx, mo)):
-        moves.append((piece, raw.at[part * i : part * (i + 1)]))
-    copies = fetch(moves, sems)
-    table[:, half:] = rest[:, LANES:]
-    lower[half:, 2 * LANES : half] = rest[:, :LANES]
-    strip = lower[half : half + LANES, block_of(2)]
-    block = table[:LANES, block_of(3)] - joined(strip, strip, NT)
+    def code_gram(i):
+        values = gram[pl.ds(pl.multiple_of(place[i], 64), part), :]
+        for k in range(size // LANES):
+            code(values[:, block_of(k)], k, outs[i], powers, i, part)
+
+    def split_moment():
+        wait_all(copies[20:])
+        moment[...] = raw[...]
 
     def product(cols, rows):
         done[rows, cols] = dot3(moment[rows, :], halves(solved[cols, :]), NT)
 
+    def code_done(k, i):
+        code(done[part * i : part * (i + 1), block_of(k)], k, outs[i], powers, i, 0)
+
     def products(cols):
-        return [functools.partial(product, cols, rows) for rows in chunks(0, size)]
+        work = [part_of(product, cols, rows) for rows in whole_chunks]
+        first, last = cols.start // LANES, cols.stop // LANES
+        return work + [part_of(code_done, k, i) for k in range(first, last) for i in range(4)]
 
     def left(k):
         return slice((k + 1) * LANES, size)
 
-    def split_moment():
-        wait_all(copies[1:])
-        moment[...] = raw[...]
-
-    work = trailing(table, lower, 2, size, half) + [copies[0].wait] + solved_row(solved, inverse_2[...], 2)
-    work += rows_update(solved, lower, left(2), block_of(2)) + [split_moment] + products(slice(0, half))
-    inverse = inverse_factor(block, work)
-    block = panel_and_next(table, lower, inverse, 3, size, half)
-    work = trailing(table, lower, 3, size, half) + solved_row(solved, inverse, 3)
-    work += rows_update(solved, lower, left(3), block_of(3)) + products(block_of(3))
-    inverse = inverse_factor(block, work)
-    block = panel_and_next(table, lower, inverse, 4, size, half)
-    work = solved_row(solved, inverse, 4) + rows_update(solved, lower, left(4), block_of(4)) + products(block_of(4))
+    part_of = functools.partial
+    whole_chunks = chunks(0, size)
+    head = turned[:LANES, :]
+    block = dot3(head, head, NT)
+    work = [part_of(cross, rows, cols) for cols in whole_chunks for rows in whole_chunks if rows.start >= cols.start]
+    work += [part_of(start, whole_chunks[0], cols) for cols in whole_chunks]
+    inverse = inverse_factor(block, work)
+    block = panel_and_next(table, lower, inverse, 0, size)
+    work = trailing(table, lower, 0, size) + solved_row(solved, inverse, 0)
+    work += [part_of(start, whole_chunks[1], cols) for cols in whole_chunks]
+    work += [split_moment, part_of(code_gram, 0)]
+    inverse = inverse_factor(block, work)
+    block = panel_and_next(table, lower, inverse, 1, size)
+    work = trailing(table, lower, 1, size) + [part_of(start, whole_chunks[2], cols) for cols in whole_chunks]
+    work += rows_update(solved, lower, block_of(1), block_of(0)) + solved_row(solved, inverse, 1)
+    work += rows_update(solved, lower, slice(2 * LANES, size), slice(0, 2 * LANES))
+    inverse = inverse_factor(block, work)
+    block = panel_and_next(table, lower, inverse, 2, size)
+    work = trailing(table, lower, 2, size) + solved_row(solved, inverse, 2)
+    work += rows_update(solved, lower, left(2), block_of(2)) + products(slice(0, 2 * LANES))
+    inverse = inverse_factor(block, work)
+    block = panel_and_next(table, lower, inverse, 3, size)
+    work = trailing(table, lower, 3, size) + solved_row(solved, inverse, 3)
+    work += rows_update(solved, lower, left(3), block_of(3)) + products(slice(2 * LANES, 4 * LANES))
+    inverse = inverse_factor(block, work)
+    block = panel_and_next(table, lower, inverse, 4, size)
+    work = solved_row(solved, inverse, 4) + rows_update(solved, lower, left(4), block_of(4))
+    work += products(block_of(4)) + [part_of(code_gram, i) for i in (1, 2, 3)]
     inverse = inverse_factor(block, work)
     for piece in solved_row(solved, inverse, 5) + products(block_of(5)):
         piece()
-    for i, piece in enumerate((ra, rb, rx, ro)):
-        piece[...] = done[part * i : part * (i + 1), :]
+    for i, out in enumerate(outs):
+        out[2 * part :, :] = jnp.zeros((16, size), jnp.int16)
+        out[2 * part :, : 2 * part] = jnp.swapaxes(powers[i], 0, 1)[:16, :].astype(jnp.int32).astype(jnp.int16)
+
+
+def unpack_kernel(choice, ra, rb, rx, ro, factor, moment, factor_new, moment_new,
+                  held, old_factor, old_moment, new_factor, new_moment, held_sems, sems, out_sems):
+    part, size = factor.shape[1:]
+    owns, one = choice[0], choice[1]
+
+    @pl.when(owns > 0)
+    def _():
+        for n, piece in enumerate((rx, ro)):
+            pltpu.make_async_copy(piece, held.at[n], held_sems.at[n]).start()
+
+    @pl.when(owns <= 0)
+    def _():
+        for n, piece in enumerate((ra, rb)):
+            pltpu.make_async_copy(piece, held.at[n], held_sems.at[n]).start()
+
+    blocks = (one, 1 - one)
+    loads = fetch(
+        [(array.at[blocks[n]], old.at[n]) for n in range(2) for array, old in ((moment, old_moment), (factor, old_factor))],
+        sems,
+    )
+    stores = []
+    for n, block in enumerate(blocks):
+        pltpu.make_async_copy((ra, rb)[n], held.at[n], held_sems.at[n]).wait()
+        powers = held[n, 2 * part :, : 2 * part].astype(jnp.int32).astype(f32)
+        scales = jnp.exp2(jnp.swapaxes(powers, 0, 1) - 15.0)
+        due = choice[2 + block] > 0
+        for m, (rows, new, out) in enumerate(
+            ((slice(0, part), new_moment, moment_new), (slice(part, 2 * part), new_factor, factor_new))
+        ):
+            loads[2 * n + m].wait()
+            for k in range(size // LANES):
+                cols = block_of(k)
+                scale = jnp.broadcast_to(scales[rows, k : k + 1], (part, LANES))
+                values = held[n, rows, cols].astype(jnp.int32).astype(f32) * scale
+                if m:
+                    new[n, :, cols] = ema_decay * old_factor[n, :, cols] + (1.0 - ema_decay) * values
+                else:
+                    new[n, :, cols] = jnp.where(due, values, old_moment[n, :, cols])
+            stores.append(pltpu.make_async_copy(new.at[n], out.at[block], out_sems.at[2 * n + m]))
+            stores[-1].start()
+    wait_all(stores)
 
 
 def call(kernel, outs, scratch, flops, remote, *args, place=None):
@@ -315,7 +362,7 @@
         in_specs=specs,
         out_specs=[vmem] * len(outs),
         scratch_shapes=[pltpu.VMEM(shape, dtype) for shape, dtype in scratch]
-        + ([pltpu.SemaphoreType.DMA((20,))] if remote else []),
+        + ([pltpu.SemaphoreType.DMA((24,))] if remote else []),
         cost_estimate=pl.CostEstimate(flops=flops, bytes_accessed=1024, transcendentals=0),
         compiler_params=pltpu.CompilerParams(vmem_limit_bytes=56 << 20),
     )(*lead, *args, *remote)
@@ -341,29 +388,28 @@
     )(choice, basis, factor, gradient)
 
 
-def gram_call(place, parts, across, part):
-    size = across.shape[1]
+def refresh_call(place, moments, messages):
+    part, size = moments[0].shape
     whole = (size, size)
-    up, down, own = parts
-    return call(gram_kernel, [((part, size), f32)] * 4, [(whole, bf16), (whole, f32)], 1,
-                [up, down, across, own], place=place)
-
-
-def power_call(place, gram_parts, parts, across):
-    part, size = gram_parts[0].shape
-    whole = (size, size)
-    up, down, own = parts
-    outs = [((size // 2, size // 2 + LANES), f32), (whole, f32), ((LANES, LANES), f32)]
-    scratch = [(whole, f32)] + [(whole, bf16)] * 4 + [(whole, f32)] + [(whole, bf16)] * 4
-    return call(power_kernel, outs, scratch, 20 * size**3, [*gram_parts, up, down, across, own], place=place)
-
-
-def rotate_call(rest, solved, inverse, up, down, across, own):
-    part, size = own.shape
-    whole = (size, size)
-    outs = [((part, size), f32)] * 4
-    scratch = [((size // 2, size), f32), (whole, f32)] + [(whole, bf16)] * 4 + [(whole, f32)] * 2
-    return call(rotate_kernel, outs, scratch, 20 * size**3, [solved, up, down, across, own], rest, inverse)
+    outs = [((2 * part + 16, size), jnp.int16)] * 4
+    scratch = [(whole, f32)] + [(whole, bf16)] * 4 + [(whole, f32)] + [(whole, bf16)] * 5
+    scratch += [(whole, f32)] * 3 + [(whole, bf16)] * 2 + [(whole, f32), ((4, 2 * part, LANES), f32)]
+    return call(refresh_kernel, outs, scratch, 50 * size**3, [*moments, *messages], place=place)
+
+
+def unpack_call(choice, messages, factor, moment):
+    stay = pl.BlockSpec(memory_space=pl.ANY)
+    return pl.pallas_call(
+        unpack_kernel,
+        out_shape=[jax.ShapeDtypeStruct(factor.shape, f32), jax.ShapeDtypeStruct(moment.shape, f32)],
+        in_specs=[pl.BlockSpec(memory_space=pltpu.SMEM)] + [stay] * 6,
+        out_specs=[stay] * 2,
+        scratch_shapes=[pltpu.VMEM((2, *messages[0].shape), jnp.int16)]
+        + [pltpu.VMEM(factor.shape, f32)] * 4
+        + [pltpu.SemaphoreType.DMA((count,)) for count in (2, 4, 4)],
+        cost_estimate=pl.CostEstimate(flops=1, bytes_accessed=1024, transcendentals=0),
+        compiler_params=pltpu.CompilerParams(vmem_limit_bytes=56 << 20),
+    )(choice, *messages, factor, moment)
 
 
 def on_device(gradient, factor, eigenbasis, moment, refresh_due):
@@ -389,46 +435,21 @@
     def choose(value):
         return jnp.where(first_is_1, value[1], value[0]), jnp.where(first_is_1, value[0], value[1])
 
-    def arrange(first, second):
-        return jnp.stack([jnp.where(first_is_1, second, first), jnp.where(first_is_1, first, second)])
-
-    def give_back(pieces):
-        first = jnp.where(owns, exchange(pieces[2], across), exchange(pieces[0], up_back))
-        second = jnp.where(owns, pieces[3], exchange(pieces[1], down_back))
-        return arrange(first, second)
-
     place = lax.rem(position + jnp.array([3, 1, 2, 0], jnp.int32), ring) * part
 
+    moment_turned = jnp.swapaxes(moment, 1, 2)
+    moment_first, moment_second = choose(moment_turned)
+    moments = [exchange(moment_first, up), exchange(moment_second, down), exchange(moment_first, across), moment_second]
     one = first_is_1.astype(jnp.int32)
     first, second = pack_call(jnp.stack([one, 1 - one]), eigenbasis, factor, jnp.swapaxes(gradient, 1, 2))
-    moment_first, moment_second = choose(jnp.swapaxes(moment, 1, 2))
-    parts = [exchange(first, up), exchange(second, down), second]
-    gradient_across = exchange(first[4 * part :], across)
-    pair_across = exchange(first[: 4 * part], across)
-    parts, gradient_across, moment_first, moment_second = lax.optimization_barrier(
-        (parts, gradient_across, moment_first, moment_second)
-    )
-    gram_parts = gram_call(place, parts, gradient_across, part)
-    to_next = jnp.where(owns, gram_parts[1], moment_first)
-    to_last = jnp.where(owns, gram_parts[0], moment_second)
-    from_last = exchange(to_next, [(a, (a + 1) % ring) for a in range(ring)])
-    from_next = exchange(to_last, [(a, (a - 1) % ring) for a in range(ring)])
-    moment_across, gram_across = exchange(moment_first, across), exchange(gram_parts[2], across)
-    powered = power_call(place, gram_parts, parts, pair_across)
-    powered, from_last, from_next, moment_across = lax.optimization_barrier(
-        (powered, from_last, from_next, moment_across)
-    )
-    rotated_parts = rotate_call(*powered, from_last, from_next, moment_across, moment_second)
-    rotated_parts, from_last, from_next, gram_across = lax.optimization_barrier(
-        (rotated_parts, from_last, from_next, gram_across)
-    )
-    gram_rows = arrange(
-        jnp.where(owns, gram_across, from_next), jnp.where(owns, gram_parts[3], from_last)
-    )
-    factor_new = ema_decay * factor + (1.0 - ema_decay) * gram_rows
-    rotated = jnp.swapaxes(give_back(rotated_parts), 1, 2)
-    moment_new = jnp.where((refresh_due > 0)[:, None, None], rotated, moment)
-    return factor_new, moment_new
+    messages = [exchange(first, up), exchange(second, down), exchange(first, across), second]
+    results = refresh_call(place, moments, messages)
+    returned = [
+        exchange(results[0], up_back), exchange(results[1], down_back), exchange(results[2], across), results[3]
+    ]
+    choice = jnp.concatenate([jnp.stack([owns.astype(jnp.int32), one]), refresh_due])
+    factor_new, moment_new = unpack_call(choice, returned, factor, moment_turned)
+    return factor_new, jnp.swapaxes(moment_new, 1, 2)
 
 
 def solution(mesh):

time: 119 us -> 129 us (1.084)
  waiting for transfers between devices: 35.4 us -> 60.2 us
  starting transfers between devices: 25.6 us -> 19.9 us
  Pallas kernels: 45.9 us -> 41.2 us
  other arithmetic: 5.33 us -> 1.89 us
    ppermute x11 -> x9, waiting for transfers between devices: 35.4 us -> 60.2 us  [exchange(): return lax.ppermute(value, ('dp', 'tensor'), pairs)]
    pallas_call x3 -> x1, Pallas kernels: 42.4 us -> 33.5 us  [call(): pl.pallas_call(kernel, out_shape=[jax.ShapeDtypeStruct(shape, dtype) for...]
    ppermute x11 -> x9, starting transfers between devices: 25.6 us -> 19.9 us  [exchange(): return lax.ppermute(value, ('dp', 'tensor'), pairs)]
    pallas_call x0 -> x1, Pallas kernels: none -> 4.04 us  [unpack_call(): pl.pallas_call(unpack_kernel, out_shape=[jax.ShapeDtypeStruct(factor.shap...]
    slice x2 -> x0, local copies, waits for them, and re-layouts: 3.34 us -> none  [the longest x1 2.36 us: on_device(): pair_across = exchange(first[:4 * part], across)]
    unnamed x26, local copies, waits for them, and re-layouts: 1.03 us -> 3.69 us
    select_n x3 -> x0, other arithmetic: 2.48 us -> none  [the longest x1 1.22 us: on_device(): moment_new = jnp.where((refresh_due > 0)[:, None, None], rotated, moment)]
  transfers between devices with their start and end apart: 11 -> 9, of which waited for: 5 -> 4; matrix products, arithmetic and copies ran while one was open for 6% -> 1% of each run, Pallas kernels for 36% -> 0%
where the time goes in v6:
time: 129 us; the launch traced here: 128 us
  waiting for transfers between devices  60.2 us (47%)
  Pallas kernels  41.2 us (32%)
  starting transfers between devices  19.9 us (15%)
  local copies, waits for them, and re-layouts  3.69 us (3%)
  other arithmetic  1.89 us (1%)
    ppermute x9, waiting for transfers between devices, exchange(): return lax.ppermute(value, ('dp', 'tensor'), pairs)  60.2 us
    pallas_call x1, Pallas kernels, call(): pl.pallas_call(kernel, out_shape=[jax.ShapeDtypeStruct(shape, dtype) for...  33.5 us
    ppermute x9, starting transfers between devices, exchange(): return lax.ppermute(value, ('dp', 'tensor'), pairs)  19.9 us
    pallas_call x1, Pallas kernels, unpack_call(): pl.pallas_call(unpack_kernel, out_shape=[jax.ShapeDtypeStruct(factor.shap...  4.04 us
    unnamed x26, local copies, waits for them, and re-layouts  3.69 us
    pallas_call x1, Pallas kernels, pack_call(): pl.pallas_call(pack_kernel, out_shape=[jax.ShapeDtypeStruct((5 * part, si...  3.67 us
  transfers between devices with their start and end apart: 9, of which 4 were waited for; matrix products, arithmetic and copies ran while one was open for 1% of the time, Pallas kernels for 0%

profile of v6, /device:TPU:4, one launch (start us, length us, event | category | flops | bytes accessed | tf_op | source)
XLA Modules:
  0.0 127.9 jit_solution(9770695668075759927)
XLA Ops:
  0.6 0.6 pad_add_fusion.1.choice
  1.2 0.0 copy-start
  1.2 3.7 %shard_map.77 = (bf16[960,768]{1,0:T(8,128)(2,1)}, bf16[960,768]{1,0:T(8,128)(2,1)}) custom-call(s32[2]{0:T(128)} %pad_add_fusion.1.choice, f32[2,192,768]{2,1,0:T(8,128)} %basis.1, f32[2,192,768]{2,1,0:T(8,128)} %factor.3, bf16[2,192,768]{2,1,0:T(8,128)(2,1)} %bitcast.12), custom_call_target="tpu_custom_call" | custom-call | flops 1 | bytes 1024 | tf_op jit(solution)/shard_map/pallas_call | solution.py:374
  4.9 4.2 %collective-permute-start.5 = (bf16[960,768]{1,0:T(8,128)(2,1)}, bf16[960,768]{1,0:T(8,128)(2,1)S(1)}, u32[]{:S(2)}, u32[]{:S(2)}) collective-permute-start(bf16[960,768]{1,0:T(8,128)(2,1)} %get-tuple-element.10), channel_id=1, source_target_pairs={{0,2},{2,0},{5,7},{7,5},{8,10},{10,8},{13,15},{15,13},{16,18},{18,... | collective-permute-start | bytes 4423688 | tf_op jit(solution)/shard_map/ppermute | solution.py:429
  9.1 1.3 %collective-permute-start.3 = (bf16[960,768]{1,0:T(8,128)(2,1)}, bf16[960,768]{1,0:T(8,128)(2,1)S(1)}, u32[]{:S(2)}, u32[]{:S(2)}) collective-permute-start(bf16[960,768]{1,0:T(8,128)(2,1)} %get-tuple-element.10), channel_id=1, source_target_pairs={{1,2},{3,0},{6,7},{4,5},{9,10},{11,8},{14,15},{12,13},{17,18},{19,... | collective-permute-start | bytes 4423688 | tf_op jit(solution)/shard_map/ppermute | solution.py:429
  10.4 1.3 %collective-permute-start.4 = (bf16[960,768]{1,0:T(8,128)(2,1)}, bf16[960,768]{1,0:T(8,128)(2,1)S(1)}, u32[]{:S(2)}, u32[]{:S(2)}) collective-permute-start(bf16[960,768]{1,0:T(8,128)(2,1)} %get-tuple-element.11.po), channel_id=1, source_target_pairs={{1,0},{3,2},{6,5},{4,7},{9,8},{11,10},{14,13},{12,15},{17,16},{19,... | collective-permute-start | bytes 4423688 | tf_op jit(solution)/shard_map/ppermute | solution.py:429
  11.7 0.0 copy-done
  11.7 0.0 copy-start.12
  11.7 0.1 select_bitcast_fusion
  11.8 0.0 copy-start.4
  11.8 1.3 %collective-permute-start.1 = (f32[192,768]{1,0:T(8,128)S(1)}, f32[192,768]{1,0:T(8,128)S(1)}, u32[]{:S(2)}, u32[]{:S(2)}) collective-permute-start(f32[192,768]{1,0:T(8,128)S(1)} %get-tuple-element.18.mo), channel_id=1, source_target_pairs={{1,0},{3,2},{6,5},{4,7},{9,8},{11,10},{14,13},{12,15},{17,16},{19,... | collective-permute-start | bytes 1769480 | tf_op jit(solution)/shard_map/ppermute | solution.py:429
  13.1 3.2 %collective-permute-start.2 = (f32[192,768]{1,0:T(8,128)S(1)}, f32[192,768]{1,0:T(8,128)S(1)}, u32[]{:S(2)}, u32[]{:S(2)}) collective-permute-start(f32[192,768]{1,0:T(8,128)S(1)} %get-tuple-element.19), channel_id=1, source_target_pairs={{0,2},{2,0},{5,7},{7,5},{8,10},{10,8},{13,15},{15,13},{16,18},{18,... | collective-permute-start | bytes 1769480 | tf_op jit(solution)/shard_map/ppermute | solution.py:429
  16.3 38.0 %collective-permute-done.1.mb = f32[192,768]{1,0:T(8,128)S(1)} collective-permute-done((f32[192,768]{1,0:T(8,128)S(1)}, f32[192,768]{1,0:T(8,128)S(1)}, u32[]{:S(2)}, u32[]{:S(2)}) %collective-permute-start.1) | collective-permute-done | bytes 589856 | tf_op jit(solution)/shard_map/ppermute | solution.py:429
  54.3 0.0 copy-start.9
  54.3 1.3 %collective-permute-start = (f32[192,768]{1,0:T(8,128)S(1)}, f32[192,768]{1,0:T(8,128)S(1)}, u32[]{:S(2)}, u32[]{:S(2)}) collective-permute-start(f32[192,768]{1,0:T(8,128)S(1)} %get-tuple-element.19), channel_id=1, source_target_pairs={{1,2},{3,0},{6,7},{4,5},{9,10},{11,8},{14,15},{12,13},{17,18},{19,... | collective-permute-start | bytes 1769480 | tf_op jit(solution)/shard_map/ppermute | solution.py:429
  55.6 0.0 copy-done.12
  55.6 0.6 fusion.1.place
  56.2 0.0 copy-start.5
  56.2 0.0 collective-permute-done.2.mx
  56.2 0.0 copy-start.10
  56.2 9.9 %collective-permute-done.ma = f32[192,768]{1,0:T(8,128)S(1)} collective-permute-done((f32[192,768]{1,0:T(8,128)S(1)}, f32[192,768]{1,0:T(8,128)S(1)}, u32[]{:S(2)}, u32[]{:S(2)}) %collective-permute-start) | collective-permute-done | bytes 589856 | tf_op jit(solution)/shard_map/ppermute | solution.py:429
  66.1 0.0 copy-start.11
  66.1 0.0 collective-permute-done.5.px
  66.1 0.0 copy-start.6
  66.1 0.0 collective-permute-done.3.pa
  66.1 0.0 copy-start.7
  66.1 0.0 collective-permute-done.4.pb
  66.1 0.0 copy-done.4
  66.1 0.0 copy-done.9
  66.1 0.0 copy-done.10
  66.1 0.8 copy-done.11
  66.9 0.5 copy-done.6
  67.4 0.5 copy-done.7
  67.8 0.0 copy-start.8
  67.8 1.1 copy-done.8
  69.0 33.5 %shard_map.78 = (s16[400,768]{1,0:T(8,128)(2,1)}, s16[400,768]{1,0:T(8,128)(2,1)}, s16[400,768]{1,0:T(8,128)(2,1)}, s16[400,768]{1,0:T(8,128)(2,1)}) custom-call(s32[4]{0:T(128)} %fusion.1.place, f32[192,768]{1,0:T(8,128)} %copy-done.11, f32[192,768]{1,0:T(8,128)} %copy-done.9, f32[192,768]{1,0:T(8,128)} %copy-done.10, f32[192,768]{1,0:T(8,128)} %copy-done.4, ...), custom_call_target="tpu_custom_call" | custom-call | flops 22649241600 | bytes 1024 | tf_op jit(solution)/shard_map/pallas_call | solution.py:359
  102.4 1.5 %collective-permute-start.6 = (s16[400,768]{1,0:T(8,128)(2,1)}, s16[400,768]{1,0:T(8,128)(2,1)S(1)}, u32[]{:S(2)}, u32[]{:S(2)}) collective-permute-start(s16[400,768]{1,0:T(8,128)(2,1)} %get-tuple-element.12), channel_id=1, source_target_pairs={{2,1},{0,3},{7,6},{5,4},{10,9},{8,11},{15,14},{13,12},{18,17},{16,... | collective-permute-start | bytes 1843208 | tf_op jit(solution)/shard_map/ppermute | solution.py:429
  103.9 1.9 %collective-permute-start.7 = (s16[400,768]{1,0:T(8,128)(2,1)}, s16[400,768]{1,0:T(8,128)(2,1)S(1)}, u32[]{:S(2)}, u32[]{:S(2)}) collective-permute-start(s16[400,768]{1,0:T(8,128)(2,1)} %get-tuple-element.13), channel_id=1, source_target_pairs={{0,1},{2,3},{5,6},{7,4},{8,9},{10,11},{13,14},{15,12},{16,17},{18,... | collective-permute-start | bytes 1843208 | tf_op jit(solution)/shard_map/ppermute | solution.py:429
  105.9 4.0 %collective-permute-start.8 = (s16[400,768]{1,0:T(8,128)(2,1)}, s16[400,768]{1,0:T(8,128)(2,1)S(1)}, u32[]{:S(2)}, u32[]{:S(2)}) collective-permute-start(s16[400,768]{1,0:T(8,128)(2,1)} %get-tuple-element.14), channel_id=1, source_target_pairs={{0,2},{2,0},{5,7},{7,5},{8,10},{10,8},{13,15},{15,13},{16,18},{18,... | collective-permute-start | bytes 1843208 | tf_op jit(solution)/shard_map/ppermute | solution.py:429
  109.9 0.0 copy-done.5
  109.9 0.7 pad_add_fusion.choice
  110.6 7.9 %collective-permute-done.6.ra = s16[400,768]{1,0:T(8,128)(2,1)S(1)} collective-permute-done((s16[400,768]{1,0:T(8,128)(2,1)}, s16[400,768]{1,0:T(8,128)(2,1)S(1)}, u32[]{:S(2)}, u32[]{:S(2)}) %collective-permute-start.6) | collective-permute-done | bytes 614432 | tf_op jit(solution)/shard_map/ppermute | solution.py:429
  118.5 0.0 collective-permute-done.7.rb
  118.5 4.4 %collective-permute-done.8.rx = s16[400,768]{1,0:T(8,128)(2,1)S(1)} collective-permute-done((s16[400,768]{1,0:T(8,128)(2,1)}, s16[400,768]{1,0:T(8,128)(2,1)S(1)}, u32[]{:S(2)}, u32[]{:S(2)}) %collective-permute-start.8) | collective-permute-done | bytes 614432 | tf_op jit(solution)/shard_map/ppermute | solution.py:429
  122.8 0.0 copy-done.1
  122.8 0.0 copy-done.2
  122.8 0.8 copy-done.3
  123.7 4.0 %shard_map.79 = (f32[2,192,768]{2,1,0:T(8,128)}, f32[2,192,768]{2,1,0:T(8,128)}) custom-call(s32[4]{0:T(128)} %pad_add_fusion.choice, s16[400,768]{1,0:T(8,128)(2,1)} %copy-done.1, s16[400,768]{1,0:T(8,128)(2,1)} %copy-done.2, s16[400,768]{1,0:T(8,128)(2,1)} %copy-done.3, s16[400,768]{1,0:T(8,128)(2,1)} %get-tuple-element.15.ro, f32[2,192,768]{2,1,0:T(8,128)} %factor.3, ...), custom_call_target="tpu_custom_call" | custom-call | flops 1 | bytes 1024 | tf_op jit(solution)/shard_map/pallas_call | solution.py:402
  (3 shorter events, 0.0 us)
Async XLA Ops:
  1.2 10.4 %copy-start = (f32[2,768,192]{1,2,0:T(8,128)S(1)}, f32[2,768,192]{1,2,0:T(8,128)}, u32[]{:S(2)}) copy-start(f32[2,768,192]{1,2,0:T(8,128)} %param.9) | copy-start | bytes 3538948
  4.9 61.2 %collective-permute-start.5 = (bf16[960,768]{1,0:T(8,128)(2,1)}, bf16[960,768]{1,0:T(8,128)(2,1)S(1)}, u32[]{:S(2)}, u32[]{:S(2)}) collective-permute-start(bf16[960,768]{1,0:T(8,128)(2,1)} %get-tuple-element.10), channel_id=1, source_target_pairs={{0,2},{2,0},{5,7},{7,5},{8,10},{10,8},{13,15},{15,13},{16,18},{18,... | collective-permute-start | bytes 4423688 | tf_op jit(solution)/shard_map/ppermute | solution.py:429
  9.1 57.0 %collective-permute-start.3 = (bf16[960,768]{1,0:T(8,128)(2,1)}, bf16[960,768]{1,0:T(8,128)(2,1)S(1)}, u32[]{:S(2)}, u32[]{:S(2)}) collective-permute-start(bf16[960,768]{1,0:T(8,128)(2,1)} %get-tuple-element.10), channel_id=1, source_target_pairs={{1,2},{3,0},{6,7},{4,5},{9,10},{11,8},{14,15},{12,13},{17,18},{19,... | collective-permute-start | bytes 4423688 | tf_op jit(solution)/shard_map/ppermute | solution.py:429
  10.4 55.7 %collective-permute-start.4 = (bf16[960,768]{1,0:T(8,128)(2,1)}, bf16[960,768]{1,0:T(8,128)(2,1)S(1)}, u32[]{:S(2)}, u32[]{:S(2)}) collective-permute-start(bf16[960,768]{1,0:T(8,128)(2,1)} %get-tuple-element.11.po), channel_id=1, source_target_pairs={{1,0},{3,2},{6,5},{4,7},{9,8},{11,10},{14,13},{12,15},{17,16},{19,... | collective-permute-start | bytes 4423688 | tf_op jit(solution)/shard_map/ppermute | solution.py:429
  11.7 43.9 %copy-start.12 = (s32[4]{0:T(128)S(1)}, s32[4]{0:T(128)}, u32[]{:S(2)}) copy-start(s32[4]{0:T(128)} %constant.31.clone) | copy-start | bytes 52
  11.8 54.3 %copy-start.4 = (f32[192,768]{1,0:T(8,128)}, f32[192,768]{1,0:T(8,128)S(1)}, u32[]{:S(2)}) copy-start(f32[192,768]{1,0:T(8,128)S(1)} %get-tuple-element.18.mo) | copy-start | bytes 1769476
  11.8 42.5 %collective-permute-start.1 = (f32[192,768]{1,0:T(8,128)S(1)}, f32[192,768]{1,0:T(8,128)S(1)}, u32[]{:S(2)}, u32[]{:S(2)}) collective-permute-start(f32[192,768]{1,0:T(8,128)S(1)} %get-tuple-element.18.mo), channel_id=1, source_target_pairs={{1,0},{3,2},{6,5},{4,7},{9,8},{11,10},{14,13},{12,15},{17,16},{19,... | collective-permute-start | bytes 1769480 | tf_op jit(solution)/shard_map/ppermute | solution.py:429
  13.1 43.1 %collective-permute-start.2 = (f32[192,768]{1,0:T(8,128)S(1)}, f32[192,768]{1,0:T(8,128)S(1)}, u32[]{:S(2)}, u32[]{:S(2)}) collective-permute-start(f32[192,768]{1,0:T(8,128)S(1)} %get-tuple-element.19), channel_id=1, source_target_pairs={{0,2},{2,0},{5,7},{7,5},{8,10},{10,8},{13,15},{15,13},{16,18},{18,... | collective-permute-start | bytes 1769480 | tf_op jit(solution)/shard_map/ppermute | solution.py:429
  54.3 11.8 %copy-start.9 = (f32[192,768]{1,0:T(8,128)}, f32[192,768]{1,0:T(8,128)S(1)}, u32[]{:S(2)}) copy-start(f32[192,768]{1,0:T(8,128)S(1)} %collective-permute-done.1.mb) | copy-start | bytes 1769476
  54.3 11.8 %collective-permute-start = (f32[192,768]{1,0:T(8,128)S(1)}, f32[192,768]{1,0:T(8,128)S(1)}, u32[]{:S(2)}, u32[]{:S(2)}) collective-permute-start(f32[192,768]{1,0:T(8,128)S(1)} %get-tuple-element.19), channel_id=1, source_target_pairs={{1,2},{3,0},{6,7},{4,5},{9,10},{11,8},{14,15},{12,13},{17,18},{19,... | collective-permute-start | bytes 1769480 | tf_op jit(solution)/shard_map/ppermute | solution.py:429
  56.2 53.8 %copy-start.5 = (s32[2]{0:T(128)S(1)}, s32[2]{0:T(128)}, u32[]{:S(2)}) copy-start(s32[2]{0:T(128)} %param.10) | copy-start | bytes 28
  56.2 10.0 %copy-start.10 = (f32[192,768]{1,0:T(8,128)}, f32[192,768]{1,0:T(8,128)S(1)}, u32[]{:S(2)}) copy-start(f32[192,768]{1,0:T(8,128)S(1)} %collective-permute-done.2.mx) | copy-start | bytes 1769476
  66.1 0.8 copy-start.11
  66.1 1.3 %copy-start.6 = (bf16[960,768]{1,0:T(8,128)(2,1)}, bf16[960,768]{1,0:T(8,128)(2,1)S(1)}, u32[]{:S(2)}) copy-start(bf16[960,768]{1,0:T(8,128)(2,1)S(1)} %collective-permute-done.5.px) | copy-start | bytes 4423684
  66.1 1.7 %copy-start.7 = (bf16[960,768]{1,0:T(8,128)(2,1)}, bf16[960,768]{1,0:T(8,128)(2,1)S(1)}, u32[]{:S(2)}) copy-start(bf16[960,768]{1,0:T(8,128)(2,1)S(1)} %collective-permute-done.3.pa) | copy-start | bytes 4423684
  67.8 1.1 copy-start.8
  102.4 16.0 %collective-permute-start.6 = (s16[400,768]{1,0:T(8,128)(2,1)}, s16[400,768]{1,0:T(8,128)(2,1)S(1)}, u32[]{:S(2)}, u32[]{:S(2)}) collective-permute-start(s16[400,768]{1,0:T(8,128)(2,1)} %get-tuple-element.12), channel_id=1, source_target_pairs={{2,1},{0,3},{7,6},{5,4},{10,9},{8,11},{15,14},{13,12},{18,17},{16,... | collective-permute-start | bytes 1843208 | tf_op jit(solution)/shard_map/ppermute | solution.py:429
  103.9 14.5 %collective-permute-start.7 = (s16[400,768]{1,0:T(8,128)(2,1)}, s16[400,768]{1,0:T(8,128)(2,1)S(1)}, u32[]{:S(2)}, u32[]{:S(2)}) collective-permute-start(s16[400,768]{1,0:T(8,128)(2,1)} %get-tuple-element.13), channel_id=1, source_target_pairs={{0,1},{2,3},{5,6},{7,4},{8,9},{10,11},{13,14},{15,12},{16,17},{18,... | collective-permute-start | bytes 1843208 | tf_op jit(solution)/shard_map/ppermute | solution.py:429
  105.9 17.0 %collective-permute-start.8 = (s16[400,768]{1,0:T(8,128)(2,1)}, s16[400,768]{1,0:T(8,128)(2,1)S(1)}, u32[]{:S(2)}, u32[]{:S(2)}) collective-permute-start(s16[400,768]{1,0:T(8,128)(2,1)} %get-tuple-element.14), channel_id=1, source_target_pairs={{0,2},{2,0},{5,7},{7,5},{8,10},{10,8},{13,15},{15,13},{16,18},{18,... | collective-permute-start | bytes 1843208 | tf_op jit(solution)/shard_map/ppermute | solution.py:429
  118.5 4.4 %copy-start.1 = (s16[400,768]{1,0:T(8,128)(2,1)}, s16[400,768]{1,0:T(8,128)(2,1)S(1)}, u32[]{:S(2)}) copy-start(s16[400,768]{1,0:T(8,128)(2,1)S(1)} %collective-permute-done.6.ra) | copy-start | bytes 1843204
  118.5 4.4 %copy-start.2 = (s16[400,768]{1,0:T(8,128)(2,1)}, s16[400,768]{1,0:T(8,128)(2,1)S(1)}, u32[]{:S(2)}) copy-start(s16[400,768]{1,0:T(8,128)(2,1)S(1)} %collective-permute-done.7.rb) | copy-start | bytes 1843204
  122.8 0.8 copy-start.3

commit v7 on v6

--- a/solution.py
+++ b/solution.py
@@ -11,6 +11,7 @@
 f32 = jnp.float32
 bf16 = jnp.bfloat16
 LANES = 128
+VMEM = 62 << 20
 GROUP = 8
 NN = (((1,), (0,)), ((), ()))
 NT = (((1,), (1,)), ((), ()))
@@ -185,19 +186,19 @@
         copy.wait()
 
 
-def pack_kernel(choice, basis, factor, gradient, first, second, raw, packed, sems, more_sems, out_sems):
+def pack_kernel(choice, basis, factor, moment, gradient, first, second, raw, packed, sems, more_sems, out_sems):
     part = basis.shape[1]
-    tops = [slice(0, 2 * part), slice(2 * part, 5 * part)]
-    sources = [(n, i) for n in range(2) for i in range(2)]
-    loads = fetch([((basis, factor)[i].at[choice[n]], raw.at[n, i]) for n, i in sources], sems)
-    straight = fetch([(gradient.at[choice[n]], packed.at[n, 4 * part :]) for n in range(2)], more_sems)
+    tops = [slice(0, 2 * part), slice(2 * part, 4 * part), slice(4 * part, 7 * part)]
+    sources = [(n, i) for i in range(3) for n in range(2)]
+    loads = fetch([((basis, factor, moment)[i].at[choice[n]], raw.at[n, i]) for n, i in sources], sems)
+    straight = fetch([(gradient.at[choice[n]], packed.at[n, 6 * part :]) for n in range(2)], more_sems)
     stores = []
     for m, (n, i) in enumerate(sources):
         loads[m].wait()
         packed[n, 2 * part * i : 2 * part * i + part, :], packed[n, 2 * part * i + part : 2 * part * (i + 1), :] = (
             halves(raw[n, i])
         )
-        if i:
+        if i == 2:
             straight[n].wait()
         stores.append(
             pltpu.make_async_copy(packed.at[n, tops[i]], (first, second)[n].at[tops[i]], out_sems.at[m])
@@ -216,9 +217,9 @@
     powers[place, rows, :] = jnp.where(lanes == column, power, powers[place, rows, :])
 
 
-def refresh_kernel(place, ma, mb, mx, mo, pa, pb, px, po, ra, rb, rx, ro,
+def refresh_kernel(place, pa, pb, px, po, ra, rb, rx, ro,
                    factor, basis_high, basis_low, turned_high, turned_low, table, lower_high, lower_low,
-                   old_high, old_low, whole, gram, solved, raw, moment_high, moment_low, done, powers, sems):
+                   old_high, old_low, whole, gram, solved, moment_high, moment_low, done, powers, sems):
     size = factor.shape[0]
     part = size // 4
     basis, turned, lower = Pair(basis_high, basis_low), Pair(turned_high, turned_low), Pair(lower_high, lower_low)
@@ -226,14 +227,16 @@
     outs = (ra, rb, rx, ro)
     moves = []
     for i, piece in enumerate((pa, pb, px, po)):
-        moves.append((piece.at[4 * part :], whole.at[part * i : part * (i + 1)]))
+        moves.append((piece.at[6 * part :], whole.at[part * i : part * (i + 1)]))
     for i, piece in enumerate((pa, pb, px, po)):
         rows = pl.ds(pl.multiple_of(place[i], 64), part)
         for n, target in enumerate((old_high, old_low, basis_high, basis_low)):
             source = piece.at[part * ((n + 2) % 4) : part * ((n + 2) % 4 + 1)]
             moves.append((source, target.at[rows]))
-    for i, piece in enumerate((ma, mb, mx, mo)):
-        moves.append((piece, raw.at[part * i : part * (i + 1)]))
+    for i, piece in enumerate((pa, pb, px, po)):
+        for n, target in enumerate((moment_high, moment_low)):
+            source = piece.at[part * (n + 4) : part * (n + 5)]
+            moves.append((source, target.at[part * i : part * (i + 1)]))
     copies = fetch(moves, sems)
     wait_all(copies[:4])
     gram[...] = lax.dot_general(whole[...], whole[...], TN, preferred_element_type=f32)
@@ -254,10 +257,6 @@
         for k in range(size // LANES):
             code(values[:, block_of(k)], k, outs[i], powers, i, part)
 
-    def split_moment():
-        wait_all(copies[20:])
-        moment[...] = raw[...]
-
     def product(cols, rows):
         done[rows, cols] = dot3(moment[rows, :], halves(solved[cols, :]), NT)
 
@@ -282,7 +281,7 @@
     block = panel_and_next(table, lower, inverse, 0, size)
     work = trailing(table, lower, 0, size) + solved_row(solved, inverse, 0)
     work += [part_of(start, whole_chunks[1], cols) for cols in whole_chunks]
-    work += [split_moment, part_of(code_gram, 0)]
+    work += [part_of(wait_all, copies[20:]), part_of(code_gram, 0)]
     inverse = inverse_factor(block, work)
     block = panel_and_next(table, lower, inverse, 1, size)
     work = trailing(table, lower, 1, size) + [part_of(start, whole_chunks[2], cols) for cols in whole_chunks]
@@ -311,7 +310,7 @@
 def unpack_kernel(choice, ra, rb, rx, ro, factor, moment, factor_new, moment_new,
                   held, old_factor, old_moment, new_factor, new_moment, held_sems, sems, out_sems):
     part, size = factor.shape[1:]
-    owns, one = choice[0], choice[1]
+    one, owns = choice[0], choice[2]
 
     @pl.when(owns > 0)
     def _():
@@ -333,7 +332,7 @@
         pltpu.make_async_copy((ra, rb)[n], held.at[n], held_sems.at[n]).wait()
         powers = held[n, 2 * part :, : 2 * part].astype(jnp.int32).astype(f32)
         scales = jnp.exp2(jnp.swapaxes(powers, 0, 1) - 15.0)
-        due = choice[2 + block] > 0
+        due = choice[3 + block] > 0
         for m, (rows, new, out) in enumerate(
             ((slice(0, part), new_moment, moment_new), (slice(part, 2 * part), new_factor, factor_new))
         ):
@@ -362,39 +361,39 @@
         in_specs=specs,
         out_specs=[vmem] * len(outs),
         scratch_shapes=[pltpu.VMEM(shape, dtype) for shape, dtype in scratch]
-        + ([pltpu.SemaphoreType.DMA((24,))] if remote else []),
+        + ([pltpu.SemaphoreType.DMA((28,))] if remote else []),
         cost_estimate=pl.CostEstimate(flops=flops, bytes_accessed=1024, transcendentals=0),
-        compiler_params=pltpu.CompilerParams(vmem_limit_bytes=56 << 20),
+        compiler_params=pltpu.CompilerParams(vmem_limit_bytes=VMEM),
     )(*lead, *args, *remote)
 
 
-def pack_call(choice, basis, factor, gradient):
+def pack_call(choice, basis, factor, moment, gradient):
     part, size = basis.shape[1:]
     stay = pl.BlockSpec(memory_space=pl.ANY)
     return pl.pallas_call(
         pack_kernel,
-        out_shape=[jax.ShapeDtypeStruct((5 * part, size), bf16)] * 2,
-        in_specs=[pl.BlockSpec(memory_space=pltpu.SMEM)] + [stay] * 3,
+        out_shape=[jax.ShapeDtypeStruct((7 * part, size), bf16)] * 2,
+        in_specs=[pl.BlockSpec(memory_space=pltpu.SMEM)] + [stay] * 4,
         out_specs=[stay] * 2,
         scratch_shapes=[
-            pltpu.VMEM((2, 2, part, size), f32),
-            pltpu.VMEM((2, 5 * part, size), bf16),
-            pltpu.SemaphoreType.DMA((4,)),
+            pltpu.VMEM((2, 3, part, size), f32),
+            pltpu.VMEM((2, 7 * part, size), bf16),
+            pltpu.SemaphoreType.DMA((6,)),
             pltpu.SemaphoreType.DMA((2,)),
-            pltpu.SemaphoreType.DMA((4,)),
+            pltpu.SemaphoreType.DMA((6,)),
         ],
         cost_estimate=pl.CostEstimate(flops=1, bytes_accessed=1024, transcendentals=0),
-        compiler_params=pltpu.CompilerParams(vmem_limit_bytes=56 << 20),
-    )(choice, basis, factor, gradient)
-
-
-def refresh_call(place, moments, messages):
-    part, size = moments[0].shape
+        compiler_params=pltpu.CompilerParams(vmem_limit_bytes=VMEM),
+    )(choice, basis, factor, moment, gradient)
+
+
+def refresh_call(place, messages):
+    part, size = messages[0].shape[0] // 7, messages[0].shape[1]
     whole = (size, size)
     outs = [((2 * part + 16, size), jnp.int16)] * 4
     scratch = [(whole, f32)] + [(whole, bf16)] * 4 + [(whole, f32)] + [(whole, bf16)] * 5
-    scratch += [(whole, f32)] * 3 + [(whole, bf16)] * 2 + [(whole, f32), ((4, 2 * part, LANES), f32)]
-    return call(refresh_kernel, outs, scratch, 50 * size**3, [*moments, *messages], place=place)
+    scratch += [(whole, f32)] * 2 + [(whole, bf16)] * 2 + [(whole, f32), ((4, 2 * part, LANES), f32)]
+    return call(refresh_kernel, outs, scratch, 50 * size**3, messages, place=place)
 
 
 def unpack_call(choice, messages, factor, moment):
@@ -408,7 +407,7 @@
         + [pltpu.VMEM(factor.shape, f32)] * 4
         + [pltpu.SemaphoreType.DMA((count,)) for count in (2, 4, 4)],
         cost_estimate=pl.CostEstimate(flops=1, bytes_accessed=1024, transcendentals=0),
-        compiler_params=pltpu.CompilerParams(vmem_limit_bytes=56 << 20),
+        compiler_params=pltpu.CompilerParams(vmem_limit_bytes=VMEM),
     )(choice, *messages, factor, moment)
 
 
@@ -432,22 +431,17 @@
     up_back, down_back = [(2, 1), (0, 3)], [(0, 1), (2, 3)]
     first_is_1 = role < 2
 
-    def choose(value):
-        return jnp.where(first_is_1, value[1], value[0]), jnp.where(first_is_1, value[0], value[1])
-
     place = lax.rem(position + jnp.array([3, 1, 2, 0], jnp.int32), ring) * part
 
     moment_turned = jnp.swapaxes(moment, 1, 2)
-    moment_first, moment_second = choose(moment_turned)
-    moments = [exchange(moment_first, up), exchange(moment_second, down), exchange(moment_first, across), moment_second]
     one = first_is_1.astype(jnp.int32)
-    first, second = pack_call(jnp.stack([one, 1 - one]), eigenbasis, factor, jnp.swapaxes(gradient, 1, 2))
+    choice = jnp.concatenate([jnp.stack([one, 1 - one, owns.astype(jnp.int32)]), refresh_due])
+    first, second = pack_call(choice, eigenbasis, factor, moment_turned, jnp.swapaxes(gradient, 1, 2))
     messages = [exchange(first, up), exchange(second, down), exchange(first, across), second]
-    results = refresh_call(place, moments, messages)
+    results = refresh_call(place, messages)
     returned = [
         exchange(results[0], up_back), exchange(results[1], down_back), exchange(results[2], across), results[3]
     ]
-    choice = jnp.concatenate([jnp.stack([owns.astype(jnp.int32), one]), refresh_due])
     factor_new, moment_new = unpack_call(choice, returned, factor, moment_turned)
     return factor_new, jnp.swapaxes(moment_new, 1, 2)
 

time: 129 us -> 117 us (0.907)
  starting transfers between devices: 19.9 us -> 14 us
  local copies, waits for them, and re-layouts: 3.69 us -> 0.85 us
  waiting for transfers between devices: 60.2 us -> 57.9 us
    ppermute x9 -> x6, starting transfers between devices: 19.9 us -> 14 us  [exchange(): return lax.ppermute(value, ('dp', 'tensor'), pairs)]
    unnamed x26 -> x8, local copies, waits for them, and re-layouts: 3.69 us -> 0.85 us
    ppermute x9 -> x6, waiting for transfers between devices: 60.2 us -> 57.9 us  [exchange(): return lax.ppermute(value, ('dp', 'tensor'), pairs)]
  transfers between devices with their start and end apart: 9 -> 6, of which waited for: 4 -> 4; matrix products, arithmetic and copies ran while one was open for 1% -> 0% of each run, Pallas kernels for 0% -> 0%
where the time goes in v7:
time: 117 us
  waiting for transfers between devices  57.9 us (49%)
  Pallas kernels  41.7 us (36%)
  starting transfers between devices  14 us (12%)
  other arithmetic  1.82 us (2%)
    ppermute x6, waiting for transfers between devices, exchange(): return lax.ppermute(value, ('dp', 'tensor'), pairs)  57.9 us
    pallas_call x1, Pallas kernels, call(): pl.pallas_call(kernel, out_shape=[jax.ShapeDtypeStruct(shape, dtype) for...  33.5 us
    ppermute x6, starting transfers between devices, exchange(): return lax.ppermute(value, ('dp', 'tensor'), pairs)  14 us
    pallas_call x1, Pallas kernels, pack_call(): pl.pallas_call(pack_kernel, out_shape=[jax.ShapeDtypeStruct((7 * part, si...  4.18 us
    pallas_call x1, Pallas kernels, unpack_call(): pl.pallas_call(unpack_kernel, out_shape=[jax.ShapeDtypeStruct(factor.shap...  4.04 us
  transfers between devices with their start and end apart: 6, of which 4 were waited for; matrix products, arithmetic and copies ran while one was open for 0% of the time, Pallas kernels for 0%

profile of v7, /device:TPU:4, one launch (start us, length us, event | category | flops | bytes accessed | tf_op | source)
XLA Modules:
  0.0 117.1 jit_solution(5724996737236969057)
XLA Ops:
  0.6 1.3 %pad_add_fusion.choice = s32[5]{0:T(128)} fusion(s32[2]{0:T(128)} %param.10, s32[1]{0:T(128)} %bitcast.2, s32[1]{0:T(128)} %bitcast.1, s32[1]{0:T(128)} %bitcast), kind=kLoop, calls=%fused_computation.4 | loop fusion | flops 15 | bytes 40 | tf_op jit(solution)/shard_map/concatenate | solution.py:438
  1.9 0.0 copy-start.3
  1.9 4.2 %shard_map.77 = (bf16[1344,768]{1,0:T(8,128)(2,1)}, bf16[1344,768]{1,0:T(8,128)(2,1)}) custom-call(s32[5]{0:T(128)} %pad_add_fusion.choice, f32[2,192,768]{2,1,0:T(8,128)} %basis.1, f32[2,192,768]{2,1,0:T(8,128)} %factor.3, f32[2,192,768]{2,1,0:T(8,128)} %bitcast.6, bf16[2,192,768]{2,1,0:T(8,128)(2,1)} %bitcast.8), custom_call_target="tpu_custom_call" | custom-call | flops 1 | bytes 1024 | tf_op jit(solution)/shard_map/pallas_call | solution.py:373
  6.1 4.2 %collective-permute-start.2 = (bf16[1344,768]{1,0:T(8,128)(2,1)}, bf16[1344,768]{1,0:T(8,128)(2,1)}, u32[]{:S(2)}, u32[]{:S(2)}) collective-permute-start(bf16[1344,768]{1,0:T(8,128)(2,1)} %get-tuple-element.10), channel_id=1, source_target_pairs={{0,2},{2,0},{5,7},{7,5},{8,10},{10,8},{13,15},{15,13},{16,18},{18,... | collective-permute-start | bytes 6193160 | tf_op jit(solution)/shard_map/ppermute | solution.py:428
  10.3 1.3 %collective-permute-start = (bf16[1344,768]{1,0:T(8,128)(2,1)}, bf16[1344,768]{1,0:T(8,128)(2,1)}, u32[]{:S(2)}, u32[]{:S(2)}) collective-permute-start(bf16[1344,768]{1,0:T(8,128)(2,1)} %get-tuple-element.10), channel_id=1, source_target_pairs={{1,2},{3,0},{6,7},{4,5},{9,10},{11,8},{14,15},{12,13},{17,18},{19,... | collective-permute-start | bytes 6193160 | tf_op jit(solution)/shard_map/ppermute | solution.py:428
  11.6 1.3 %collective-permute-start.1 = (bf16[1344,768]{1,0:T(8,128)(2,1)}, bf16[1344,768]{1,0:T(8,128)(2,1)}, u32[]{:S(2)}, u32[]{:S(2)}) collective-permute-start(bf16[1344,768]{1,0:T(8,128)(2,1)} %get-tuple-element.11.po), channel_id=1, source_target_pairs={{1,0},{3,2},{6,5},{4,7},{9,8},{11,10},{14,13},{12,15},{17,16},{19,... | collective-permute-start | bytes 6193160 | tf_op jit(solution)/shard_map/ppermute | solution.py:428
  12.9 0.0 copy-done.3
  12.9 0.5 fusion.1.place
  13.4 43.1 %collective-permute-done.2.px = bf16[1344,768]{1,0:T(8,128)(2,1)} collective-permute-done((bf16[1344,768]{1,0:T(8,128)(2,1)}, bf16[1344,768]{1,0:T(8,128)(2,1)}, u32[]{:S(2)}, u32[]{:S(2)}) %collective-permute-start.2) | collective-permute-done | bytes 2064416 | tf_op jit(solution)/shard_map/ppermute | solution.py:428
  56.5 1.9 %collective-permute-done.pa = bf16[1344,768]{1,0:T(8,128)(2,1)} collective-permute-done((bf16[1344,768]{1,0:T(8,128)(2,1)}, bf16[1344,768]{1,0:T(8,128)(2,1)}, u32[]{:S(2)}, u32[]{:S(2)}) %collective-permute-start) | collective-permute-done | bytes 2064416 | tf_op jit(solution)/shard_map/ppermute | solution.py:428
  58.4 0.0 collective-permute-done.1.pb
  58.4 33.5 %shard_map.78 = (s16[400,768]{1,0:T(8,128)(2,1)}, s16[400,768]{1,0:T(8,128)(2,1)}, s16[400,768]{1,0:T(8,128)(2,1)}, s16[400,768]{1,0:T(8,128)(2,1)}) custom-call(s32[4]{0:T(128)} %fusion.1.place, bf16[1344,768]{1,0:T(8,128)(2,1)} %collective-permute-done.pa, bf16[1344,768]{1,0:T(8,128)(2,1)} %collective-permute-done.1.pb, ...), custom_call_target="tpu_custom_call" | custom-call | flops 22649241600 | bytes 1024 | tf_op jit(solution)/shard_map/pallas_call | solution.py:358
  91.9 1.5 %collective-permute-start.3 = (s16[400,768]{1,0:T(8,128)(2,1)}, s16[400,768]{1,0:T(8,128)(2,1)S(1)}, u32[]{:S(2)}, u32[]{:S(2)}) collective-permute-start(s16[400,768]{1,0:T(8,128)(2,1)} %get-tuple-element.12), channel_id=1, source_target_pairs={{2,1},{0,3},{7,6},{5,4},{10,9},{8,11},{15,14},{13,12},{18,17},{16,... | collective-permute-start | bytes 1843208 | tf_op jit(solution)/shard_map/ppermute | solution.py:428
  93.4 1.7 %collective-permute-start.4 = (s16[400,768]{1,0:T(8,128)(2,1)}, s16[400,768]{1,0:T(8,128)(2,1)S(1)}, u32[]{:S(2)}, u32[]{:S(2)}) collective-permute-start(s16[400,768]{1,0:T(8,128)(2,1)} %get-tuple-element.13), channel_id=1, source_target_pairs={{0,1},{2,3},{5,6},{7,4},{8,9},{10,11},{13,14},{15,12},{16,17},{18,... | collective-permute-start | bytes 1843208 | tf_op jit(solution)/shard_map/ppermute | solution.py:428
  95.1 4.0 %collective-permute-start.5 = (s16[400,768]{1,0:T(8,128)(2,1)}, s16[400,768]{1,0:T(8,128)(2,1)S(1)}, u32[]{:S(2)}, u32[]{:S(2)}) collective-permute-start(s16[400,768]{1,0:T(8,128)(2,1)} %get-tuple-element.14), channel_id=1, source_target_pairs={{0,2},{2,0},{5,7},{7,5},{8,10},{10,8},{13,15},{15,13},{16,18},{18,... | collective-permute-start | bytes 1843208 | tf_op jit(solution)/shard_map/ppermute | solution.py:428
  99.1 8.8 %collective-permute-done.3.ra = s16[400,768]{1,0:T(8,128)(2,1)S(1)} collective-permute-done((s16[400,768]{1,0:T(8,128)(2,1)}, s16[400,768]{1,0:T(8,128)(2,1)S(1)}, u32[]{:S(2)}, u32[]{:S(2)}) %collective-permute-start.3) | collective-permute-done | bytes 614432 | tf_op jit(solution)/shard_map/ppermute | solution.py:428
  107.9 0.0 copy-start
  107.9 0.0 collective-permute-done.4.rb
  107.9 0.0 copy-start.1
  107.9 4.2 %collective-permute-done.5.rx = s16[400,768]{1,0:T(8,128)(2,1)S(1)} collective-permute-done((s16[400,768]{1,0:T(8,128)(2,1)}, s16[400,768]{1,0:T(8,128)(2,1)S(1)}, u32[]{:S(2)}, u32[]{:S(2)}) %collective-permute-start.5) | collective-permute-done | bytes 614432 | tf_op jit(solution)/shard_map/ppermute | solution.py:428
  112.1 0.0 copy-start.2
  112.1 0.0 copy-done
  112.1 0.0 copy-done.1
  112.1 0.8 copy-done.2
  112.9 4.0 %shard_map.79 = (f32[2,192,768]{2,1,0:T(8,128)}, f32[2,192,768]{2,1,0:T(8,128)}) custom-call(s32[5]{0:T(128)} %pad_add_fusion.choice, s16[400,768]{1,0:T(8,128)(2,1)} %copy-done, s16[400,768]{1,0:T(8,128)(2,1)} %copy-done.1, s16[400,768]{1,0:T(8,128)(2,1)} %copy-done.2, s16[400,768]{1,0:T(8,128)(2,1)} %get-tuple-element.15.ro, f32[2,192,768]{2,1,0:T(8,128)} %factor.3, ...), custom_call_target="tpu_custom_call" | custom-call | flops 1 | bytes 1024 | tf_op jit(solution)/shard_map/pallas_call | solution.py:401
Async XLA Ops:
  1.9 10.9 %copy-start.3 = (s32[4]{0:T(128)S(1)}, s32[4]{0:T(128)}, u32[]{:S(2)}) copy-start(s32[4]{0:T(128)} %constant.31.clone) | copy-start | bytes 52
  6.1 50.4 %collective-permute-start.2 = (bf16[1344,768]{1,0:T(8,128)(2,1)}, bf16[1344,768]{1,0:T(8,128)(2,1)}, u32[]{:S(2)}, u32[]{:S(2)}) collective-permute-start(bf16[1344,768]{1,0:T(8,128)(2,1)} %get-tuple-element.10), channel_id=1, source_target_pairs={{0,2},{2,0},{5,7},{7,5},{8,10},{10,8},{13,15},{15,13},{16,18},{18,... | collective-permute-start | bytes 6193160 | tf_op jit(solution)/shard_map/ppermute | solution.py:428
  10.3 48.1 %collective-permute-start = (bf16[1344,768]{1,0:T(8,128)(2,1)}, bf16[1344,768]{1,0:T(8,128)(2,1)}, u32[]{:S(2)}, u32[]{:S(2)}) collective-permute-start(bf16[1344,768]{1,0:T(8,128)(2,1)} %get-tuple-element.10), channel_id=1, source_target_pairs={{1,2},{3,0},{6,7},{4,5},{9,10},{11,8},{14,15},{12,13},{17,18},{19,... | collective-permute-start | bytes 6193160 | tf_op jit(solution)/shard_map/ppermute | solution.py:428
  11.6 46.8 %collective-permute-start.1 = (bf16[1344,768]{1,0:T(8,128)(2,1)}, bf16[1344,768]{1,0:T(8,128)(2,1)}, u32[]{:S(2)}, u32[]{:S(2)}) collective-permute-start(bf16[1344,768]{1,0:T(8,128)(2,1)} %get-tuple-element.11.po), channel_id=1, source_target_pairs={{1,0},{3,2},{6,5},{4,7},{9,8},{11,10},{14,13},{12,15},{17,16},{19,... | collective-permute-start | bytes 6193160 | tf_op jit(solution)/shard_map/ppermute | solution.py:428
  91.9 16.0 %collective-permute-start.3 = (s16[400,768]{1,0:T(8,128)(2,1)}, s16[400,768]{1,0:T(8,128)(2,1)S(1)}, u32[]{:S(2)}, u32[]{:S(2)}) collective-permute-start(s16[400,768]{1,0:T(8,128)(2,1)} %get-tuple-element.12), channel_id=1, source_target_pairs={{2,1},{0,3},{7,6},{5,4},{10,9},{8,11},{15,14},{13,12},{18,17},{16,... | collective-permute-start | bytes 1843208 | tf_op jit(solution)/shard_map/ppermute | solution.py:428
  93.4 14.5 %collective-permute-start.4 = (s16[400,768]{1,0:T(8,128)(2,1)}, s16[400,768]{1,0:T(8,128)(2,1)S(1)}, u32[]{:S(2)}, u32[]{:S(2)}) collective-permute-start(s16[400,768]{1,0:T(8,128)(2,1)} %get-tuple-element.13), channel_id=1, source_target_pairs={{0,1},{2,3},{5,6},{7,4},{8,9},{10,11},{13,14},{15,12},{16,17},{18,... | collective-permute-start | bytes 1843208 | tf_op jit(solution)/shard_map/ppermute | solution.py:428
  95.1 17.0 %collective-permute-start.5 = (s16[400,768]{1,0:T(8,128)(2,1)}, s16[400,768]{1,0:T(8,128)(2,1)S(1)}, u32[]{:S(2)}, u32[]{:S(2)}) collective-permute-start(s16[400,768]{1,0:T(8,128)(2,1)} %get-tuple-element.14), channel_id=1, source_target_pairs={{0,2},{2,0},{5,7},{7,5},{8,10},{10,8},{13,15},{15,13},{16,18},{18,... | collective-permute-start | bytes 1843208 | tf_op jit(solution)/shard_map/ppermute | solution.py:428
  107.9 4.2 %copy-start = (s16[400,768]{1,0:T(8,128)(2,1)}, s16[400,768]{1,0:T(8,128)(2,1)S(1)}, u32[]{:S(2)}) copy-start(s16[400,768]{1,0:T(8,128)(2,1)S(1)} %collective-permute-done.3.ra) | copy-start | bytes 1843204
  107.9 4.2 %copy-start.1 = (s16[400,768]{1,0:T(8,128)(2,1)}, s16[400,768]{1,0:T(8,128)(2,1)S(1)}, u32[]{:S(2)}) copy-start(s16[400,768]{1,0:T(8,128)(2,1)S(1)} %collective-permute-done.4.rb) | copy-start | bytes 1843204
  112.1 0.8 copy-start.2

commit v8 on v7

--- a/solution.py
+++ b/solution.py
@@ -11,7 +11,6 @@
 f32 = jnp.float32
 bf16 = jnp.bfloat16
 LANES = 128
-VMEM = 62 << 20
 GROUP = 8
 NN = (((1,), (0,)), ((), ()))
 NT = (((1,), (1,)), ((), ()))
@@ -186,23 +185,48 @@
         copy.wait()
 
 
-def pack_kernel(choice, basis, factor, moment, gradient, first, second, raw, packed, sems, more_sems, out_sems):
+def whereabouts():
+    ring = lax.axis_size("tensor")
+    here = lax.axis_index("tensor")
+    role = lax.rem(here - lax.rem(lax.axis_index("dp"), 2) + ring, ring)
+    owns = 1 - lax.rem(role, 2)
+    one = 1 - role // 2
+    blocks = (one, 1 - one)
+    owners = (lax.rem(here + 1 + owns, ring), lax.rem(here + ring - 1 + owns, ring))
+    return here, owns, blocks, owners
+
+
+def turn(value, steps, part):
+    for bit in (1, 2):
+        moved = jnp.concatenate([value[:, bit * part :], value[:, : bit * part]], 1)
+        value = jnp.where(lax.rem(steps // bit, 2) > 0, moved, value)
+    return value
+
+
+def pack_kernel(basis, factor, moment, gradient, first, second, raw, raw_gradient, packed, sems, more_sems, out_sems):
     part = basis.shape[1]
-    tops = [slice(0, 2 * part), slice(2 * part, 4 * part), slice(4 * part, 7 * part)]
+    here, owns, blocks, owners = whereabouts()
+    tops = [slice(0, 2 * part), slice(2 * part, 3 * part), slice(3 * part, 5 * part), slice(5 * part, 6 * part)]
     sources = [(n, i) for i in range(3) for n in range(2)]
-    loads = fetch([((basis, factor, moment)[i].at[choice[n]], raw.at[n, i]) for n, i in sources], sems)
-    straight = fetch([(gradient.at[choice[n]], packed.at[n, 6 * part :]) for n in range(2)], more_sems)
+    loads = fetch([((basis, factor, moment)[i].at[blocks[n]], raw.at[n, i]) for n, i in sources], sems)
+    loads += fetch([(gradient.at[blocks[n]], raw_gradient.at[n]) for n in range(2)], more_sems)
     stores = []
-    for m, (n, i) in enumerate(sources):
+    for m, (n, i) in enumerate(sources + [(0, 3), (1, 3)]):
         loads[m].wait()
-        packed[n, 2 * part * i : 2 * part * i + part, :], packed[n, 2 * part * i + part : 2 * part * (i + 1), :] = (
-            halves(raw[n, i])
-        )
-        if i == 2:
-            straight[n].wait()
-        stores.append(
-            pltpu.make_async_copy(packed.at[n, tops[i]], (first, second)[n].at[tops[i]], out_sems.at[m])
-        )
+        rows = tops[i]
+        if i == 1:
+            turned = turn(raw[n, 1], here, part)
+            other = turned[:, part : 2 * part]
+            if n == 0:
+                other = jnp.where(owns > 0, other, turned[:, 2 * part : 3 * part])
+            packed[n, rows, :] = jnp.concatenate(halves(jnp.concatenate([turned[:, :part], other], 1)), 1)
+        elif i == 3:
+            packed[n, rows, :] = turn(raw_gradient[n].astype(f32), owners[n], part).astype(bf16)
+        else:
+            high, low = halves(raw[n, i])
+            packed[n, rows.start : rows.start + part, :] = high
+            packed[n, rows.start + part : rows.stop, :] = low
+        stores.append(pltpu.make_async_copy(packed.at[n, rows], (first, second)[n].at[rows], out_sems.at[m]))
         stores[-1].start()
     wait_all(stores)
 
@@ -217,33 +241,46 @@
     powers[place, rows, :] = jnp.where(lanes == column, power, powers[place, rows, :])
 
 
-def refresh_kernel(place, pa, pb, px, po, ra, rb, rx, ro,
+def refresh_kernel(pa, pb, px, po, own, ra, rb, rx, ro,
                    factor, basis_high, basis_low, turned_high, turned_low, table, lower_high, lower_low,
-                   old_high, old_low, whole, gram, solved, moment_high, moment_low, done, powers, sems):
+                   own_rows, half_rows, whole, gram, solved, moment_high, moment_low, done, powers, sems):
     size = factor.shape[0]
     part = size // 4
     basis, turned, lower = Pair(basis_high, basis_low), Pair(turned_high, turned_low), Pair(lower_high, lower_low)
     moment = Pair(moment_high, moment_low)
     outs = (ra, rb, rx, ro)
-    moves = []
+    turns = (3, 1, 2, 0)
+    here, _, blocks, _ = whereabouts()
+    gradient_moves, moves, moment_moves = [], [(own.at[blocks[1]], own_rows)], []
     for i, piece in enumerate((pa, pb, px, po)):
-        moves.append((piece.at[6 * part :], whole.at[part * i : part * (i + 1)]))
-    for i, piece in enumerate((pa, pb, px, po)):
-        rows = pl.ds(pl.multiple_of(place[i], 64), part)
-        for n, target in enumerate((old_high, old_low, basis_high, basis_low)):
-            source = piece.at[part * ((n + 2) % 4) : part * ((n + 2) % 4 + 1)]
-            moves.append((source, target.at[rows]))
-    for i, piece in enumerate((pa, pb, px, po)):
-        for n, target in enumerate((moment_high, moment_low)):
-            source = piece.at[part * (n + 4) : part * (n + 5)]
-            moves.append((source, target.at[part * i : part * (i + 1)]))
-    copies = fetch(moves, sems)
+        rows = slice(part * turns[i], part * (turns[i] + 1))
+        gradient_moves.append((piece.at[5 * part :], whole.at[rows]))
+        moves += [(piece.at[:part], basis_high.at[rows]), (piece.at[part : 2 * part], basis_low.at[rows])]
+        if turns[i]:
+            moves.append((piece.at[2 * part : 3 * part], half_rows.at[turns[i] - 1]))
+        there = slice(part * i, part * (i + 1))
+        moment_moves.append((piece.at[3 * part : 4 * part], moment_high.at[there]))
+        moment_moves.append((piece.at[4 * part : 5 * part], moment_low.at[there]))
+    copies = fetch(gradient_moves + moves + moment_moves, sems)
     wait_all(copies[:4])
     gram[...] = lax.dot_general(whole[...], whole[...], TN, preferred_element_type=f32)
-    wait_all(copies[4:20])
-    factor[...] = (1.0 - ema_decay) * gram[...] + ema_decay * (
-        old_high[...].astype(f32) + old_low[...].astype(f32)
-    )
+    wait_all(copies[4 : 4 + len(moves)])
+    mine = turn(own_rows[...], here, part)
+    pairs = []
+    for n in range(3):
+        both = half_rows[n, :, : 2 * part].astype(f32) + half_rows[n, :, 2 * part :].astype(f32)
+        pairs.append((both[:, :part], both[:, part:]))
+    (f11, f12), (f22, f23), (f33, f31) = pairs
+    across = [jnp.swapaxes(mine[:, part * n : part * (n + 1)], 0, 1) for n in (1, 2, 3)]
+    lines = [
+        [mine],
+        [across[0], f11, f12, jnp.swapaxes(f31, 0, 1)],
+        [across[1], jnp.swapaxes(f12, 0, 1), f22, f23],
+        [across[2], f31, jnp.swapaxes(f23, 0, 1), f33],
+    ]
+    for n, line in enumerate(lines):
+        rows = slice(part * n, part * (n + 1))
+        factor[rows, :] = (1.0 - ema_decay) * gram[rows, :] + ema_decay * jnp.concatenate(line, 1)
     turned[...] = dot3(basis[...], halves(factor[...]), TN)
 
     def cross(rows, cols):
@@ -253,7 +290,7 @@
         solved[rows, cols] = dot3(turned[rows, :], basis[:, cols], NN)
 
     def code_gram(i):
-        values = gram[pl.ds(pl.multiple_of(place[i], 64), part), :]
+        values = gram[part * turns[i] : part * (turns[i] + 1), :]
         for k in range(size // LANES):
             code(values[:, block_of(k)], k, outs[i], powers, i, part)
 
@@ -281,7 +318,7 @@
     block = panel_and_next(table, lower, inverse, 0, size)
     work = trailing(table, lower, 0, size) + solved_row(solved, inverse, 0)
     work += [part_of(start, whole_chunks[1], cols) for cols in whole_chunks]
-    work += [part_of(wait_all, copies[20:]), part_of(code_gram, 0)]
+    work += [part_of(wait_all, copies[4 + len(moves) :]), part_of(code_gram, 0)]
     inverse = inverse_factor(block, work)
     block = panel_and_next(table, lower, inverse, 1, size)
     work = trailing(table, lower, 1, size) + [part_of(start, whole_chunks[2], cols) for cols in whole_chunks]
@@ -307,10 +344,10 @@
         out[2 * part :, : 2 * part] = jnp.swapaxes(powers[i], 0, 1)[:16, :].astype(jnp.int32).astype(jnp.int16)
 
 
-def unpack_kernel(choice, ra, rb, rx, ro, factor, moment, factor_new, moment_new,
-                  held, old_factor, old_moment, new_factor, new_moment, held_sems, sems, out_sems):
+def unpack_kernel(flags, ra, rb, rx, ro, factor, moment, factor_new, moment_new,
+                  held, new_factor, new_moment, decoded, held_sems, out_sems):
     part, size = factor.shape[1:]
-    one, owns = choice[0], choice[2]
+    _, owns, blocks, owners = whereabouts()
 
     @pl.when(owns > 0)
     def _():
@@ -322,102 +359,72 @@
         for n, piece in enumerate((ra, rb)):
             pltpu.make_async_copy(piece, held.at[n], held_sems.at[n]).start()
 
-    blocks = (one, 1 - one)
-    loads = fetch(
-        [(array.at[blocks[n]], old.at[n]) for n in range(2) for array, old in ((moment, old_moment), (factor, old_factor))],
-        sems,
-    )
     stores = []
     for n, block in enumerate(blocks):
         pltpu.make_async_copy((ra, rb)[n], held.at[n], held_sems.at[n]).wait()
         powers = held[n, 2 * part :, : 2 * part].astype(jnp.int32).astype(f32)
         scales = jnp.exp2(jnp.swapaxes(powers, 0, 1) - 15.0)
-        due = choice[3 + block] > 0
+        due = flags[block] > 0
         for m, (rows, new, out) in enumerate(
             ((slice(0, part), new_moment, moment_new), (slice(part, 2 * part), new_factor, factor_new))
         ):
-            loads[2 * n + m].wait()
             for k in range(size // LANES):
                 cols = block_of(k)
                 scale = jnp.broadcast_to(scales[rows, k : k + 1], (part, LANES))
                 values = held[n, rows, cols].astype(jnp.int32).astype(f32) * scale
                 if m:
-                    new[n, :, cols] = ema_decay * old_factor[n, :, cols] + (1.0 - ema_decay) * values
+                    decoded[:, cols] = values
                 else:
-                    new[n, :, cols] = jnp.where(due, values, old_moment[n, :, cols])
+                    new[n, :, cols] = jnp.where(due, values, moment[block, :, cols])
+            if m:
+                values = turn(decoded[...], 4 - owners[n], part)
+                new[n] = ema_decay * factor[block] + (1.0 - ema_decay) * values
             stores.append(pltpu.make_async_copy(new.at[n], out.at[block], out_sems.at[2 * n + m]))
             stores[-1].start()
     wait_all(stores)
 
 
-def call(kernel, outs, scratch, flops, remote, *args, place=None):
-    smem = pl.BlockSpec(memory_space=pltpu.SMEM)
-    vmem = pl.BlockSpec(memory_space=pltpu.VMEM)
-    lead = () if place is None else (place,)
-    specs = [smem] * len(lead) + [vmem] * len(args) + [pl.BlockSpec(memory_space=pl.ANY)] * len(remote)
+def call(kernel, shapes, scratch, sems, flops, arrays, room, flags=None, results=pltpu.VMEM, far=()):
+    spaces = [pltpu.HBM if i in far else pltpu.VMEM for i in range(len(arrays))]
+    lead = () if flags is None else (flags,)
     return pl.pallas_call(
         kernel,
-        out_shape=[jax.ShapeDtypeStruct(shape, dtype) for shape, dtype in outs],
-        in_specs=specs,
-        out_specs=[vmem] * len(outs),
+        out_shape=[jax.ShapeDtypeStruct(shape, dtype) for shape, dtype in shapes],
+        in_specs=[pl.BlockSpec(memory_space=pltpu.SMEM)] * len(lead) + [pl.BlockSpec(memory_space=space) for space in spaces],
+        out_specs=[pl.BlockSpec(memory_space=results)] * len(shapes),
         scratch_shapes=[pltpu.VMEM(shape, dtype) for shape, dtype in scratch]
-        + ([pltpu.SemaphoreType.DMA((28,))] if remote else []),
+        + [pltpu.SemaphoreType.DMA((count,)) for count in sems],
         cost_estimate=pl.CostEstimate(flops=flops, bytes_accessed=1024, transcendentals=0),
-        compiler_params=pltpu.CompilerParams(vmem_limit_bytes=VMEM),
-    )(*lead, *args, *remote)
-
-
-def pack_call(choice, basis, factor, moment, gradient):
+        compiler_params=pltpu.CompilerParams(vmem_limit_bytes=room << 20),
+    )(*lead, *arrays)
+
+
+def pack_call(basis, factor, moment, gradient):
     part, size = basis.shape[1:]
-    stay = pl.BlockSpec(memory_space=pl.ANY)
-    return pl.pallas_call(
-        pack_kernel,
-        out_shape=[jax.ShapeDtypeStruct((7 * part, size), bf16)] * 2,
-        in_specs=[pl.BlockSpec(memory_space=pltpu.SMEM)] + [stay] * 4,
-        out_specs=[stay] * 2,
-        scratch_shapes=[
-            pltpu.VMEM((2, 3, part, size), f32),
-            pltpu.VMEM((2, 7 * part, size), bf16),
-            pltpu.SemaphoreType.DMA((6,)),
-            pltpu.SemaphoreType.DMA((2,)),
-            pltpu.SemaphoreType.DMA((6,)),
-        ],
-        cost_estimate=pl.CostEstimate(flops=1, bytes_accessed=1024, transcendentals=0),
-        compiler_params=pltpu.CompilerParams(vmem_limit_bytes=VMEM),
-    )(choice, basis, factor, moment, gradient)
-
-
-def refresh_call(place, messages):
-    part, size = messages[0].shape[0] // 7, messages[0].shape[1]
+    scratch = [((2, 3, part, size), f32), ((2, part, size), bf16), ((2, 6 * part, size), bf16)]
+    outs = [((6 * part, size), bf16)] * 2
+    return call(pack_kernel, outs, scratch, (6, 2, 8), 1, [basis, factor, moment, gradient], 62,
+                results=pltpu.HBM, far=range(4))
+
+
+def refresh_call(messages, factor):
+    part, size = factor.shape[1:]
     whole = (size, size)
     outs = [((2 * part + 16, size), jnp.int16)] * 4
-    scratch = [(whole, f32)] + [(whole, bf16)] * 4 + [(whole, f32)] + [(whole, bf16)] * 5
+    scratch = [(whole, f32)] + [(whole, bf16)] * 4 + [(whole, f32)] + [(whole, bf16)] * 2
+    scratch += [((part, size), f32), ((3, part, size), bf16), (whole, bf16)]
     scratch += [(whole, f32)] * 2 + [(whole, bf16)] * 2 + [(whole, f32), ((4, 2 * part, LANES), f32)]
-    return call(refresh_kernel, outs, scratch, 50 * size**3, messages, place=place)
-
-
-def unpack_call(choice, messages, factor, moment):
-    stay = pl.BlockSpec(memory_space=pl.ANY)
-    return pl.pallas_call(
-        unpack_kernel,
-        out_shape=[jax.ShapeDtypeStruct(factor.shape, f32), jax.ShapeDtypeStruct(moment.shape, f32)],
-        in_specs=[pl.BlockSpec(memory_space=pltpu.SMEM)] + [stay] * 6,
-        out_specs=[stay] * 2,
-        scratch_shapes=[pltpu.VMEM((2, *messages[0].shape), jnp.int16)]
-        + [pltpu.VMEM(factor.shape, f32)] * 4
-        + [pltpu.SemaphoreType.DMA((count,)) for count in (2, 4, 4)],
-        cost_estimate=pl.CostEstimate(flops=1, bytes_accessed=1024, transcendentals=0),
-        compiler_params=pltpu.CompilerParams(vmem_limit_bytes=VMEM),
-    )(choice, *messages, factor, moment)
+    return call(refresh_kernel, outs, scratch, (28,), 50 * size**3, [*messages, factor], 42, far=(3, 4))
+
+
+def unpack_call(flags, messages, factor, moment):
+    scratch = [((2, *messages[0].shape), jnp.int16)] + [(factor.shape, f32)] * 2 + [(factor.shape[1:], f32)]
+    outs = [(factor.shape, f32), (moment.shape, f32)]
+    return call(unpack_kernel, outs, scratch, (2, 4), 1, [*messages, factor, moment], 20, flags, pltpu.HBM)
 
 
 def on_device(gradient, factor, eigenbasis, moment, refresh_due):
-    part, size = factor.shape[1], factor.shape[2]
     groups, ring = lax.axis_size("dp"), lax.axis_size("tensor")
-    core = lax.rem(lax.axis_index("dp"), 2)
-    position = lax.axis_index("tensor")
-    role = lax.rem(position - core + ring, ring)
-    owns = lax.rem(role, 2) == 0
 
     def exchange(value, roles):
         pairs = [
@@ -429,20 +436,14 @@
 
     up, down, across = [(1, 2), (3, 0)], [(1, 0), (3, 2)], [(0, 2), (2, 0)]
     up_back, down_back = [(2, 1), (0, 3)], [(0, 1), (2, 3)]
-    first_is_1 = role < 2
-
-    place = lax.rem(position + jnp.array([3, 1, 2, 0], jnp.int32), ring) * part
-
-    moment_turned = jnp.swapaxes(moment, 1, 2)
-    one = first_is_1.astype(jnp.int32)
-    choice = jnp.concatenate([jnp.stack([one, 1 - one, owns.astype(jnp.int32)]), refresh_due])
-    first, second = pack_call(choice, eigenbasis, factor, moment_turned, jnp.swapaxes(gradient, 1, 2))
+    turned = jnp.swapaxes(moment, 1, 2)
+    first, second = pack_call(eigenbasis, factor, turned, jnp.swapaxes(gradient, 1, 2))
     messages = [exchange(first, up), exchange(second, down), exchange(first, across), second]
-    results = refresh_call(place, messages)
+    results = refresh_call(messages, factor)
     returned = [
         exchange(results[0], up_back), exchange(results[1], down_back), exchange(results[2], across), results[3]
     ]
-    factor_new, moment_new = unpack_call(choice, returned, factor, moment_turned)
+    factor_new, moment_new = unpack_call(refresh_due, returned, factor, turned)
     return factor_new, jnp.swapaxes(moment_new, 1, 2)
 
 

time: 117 us -> 109 us (0.932)
  waiting for transfers between devices: 57.9 us -> 51.7 us
  other arithmetic: 1.82 us -> 0 us
  Pallas kernels: 41.7 us -> 40.2 us
    pallas_call x2 -> x0, Pallas kernels: 8.22 us -> none  [the longest x1 4.18 us: pack_call(): pl.pallas_call(pack_kernel, out_shape=[jax.ShapeDtypeStruct((7 * part, si...]
    pallas_call x1 -> x3, Pallas kernels: 33.5 us -> 40.2 us  [call(): pl.pallas_call(kernel, out_shape=[jax.ShapeDtypeStruct(shape, dtype) for...]
    ppermute x6, waiting for transfers between devices: 57.9 us -> 51.7 us  [exchange(): return lax.ppermute(value, ('dp', 'tensor'), pairs)]
    concatenate x1 -> x0, other arithmetic: 1.28 us -> none  [on_device(): jnp.concatenate([jnp.stack([one, 1 - one, owns.astype(jnp.int32)]), refre...]
where the time goes in v8:
time: 109 us; the launch traced here: 108 us
  waiting for transfers between devices  51.7 us (47%)
  Pallas kernels  40.2 us (37%)
  starting transfers between devices  14.2 us (13%)
  local copies, waits for them, and re-layouts  1.49 us (1%)
    ppermute x6, waiting for transfers between devices, exchange(): return lax.ppermute(value, ('dp', 'tensor'), pairs)  51.7 us
    pallas_call x3, Pallas kernels, call(): pl.pallas_call(kernel, out_shape=[jax.ShapeDtypeStruct(shape, dtype) for...  40.2 us
    ppermute x6, starting transfers between devices, exchange(): return lax.ppermute(value, ('dp', 'tensor'), pairs)  14.2 us
  transfers between devices with their start and end apart: 6, of which 4 were waited for; matrix products, arithmetic and copies ran while one was open for 0% of the time, Pallas kernels for 0%

profile of v8, /device:TPU:4, one launch (start us, length us, event | category | flops | bytes accessed | tf_op | source)
XLA Modules:
  0.0 108.5 jit_solution(16254623102926571762)
XLA Ops:
  0.6 0.0 copy-start
  0.6 4.1 %shard_map.68 = (bf16[1152,768]{1,0:T(8,128)(2,1)}, bf16[1152,768]{1,0:T(8,128)(2,1)}) custom-call(f32[2,192,768]{2,1,0:T(8,128)} %basis.1, f32[2,192,768]{2,1,0:T(8,128)} %factor.3, f32[2,192,768]{2,1,0:T(8,128)} %bitcast.3, bf16[2,192,768]{2,1,0:T(8,128)(2,1)} %bitcast.5), custom_call_target="tpu_custom_call" | custom-call | flops 1 | bytes 1024 | tf_op jit(solution)/shard_map/pallas_call | solution.py:390
  4.7 4.2 %collective-permute-start.2 = (bf16[1152,768]{1,0:T(8,128)(2,1)}, bf16[1152,768]{1,0:T(8,128)(2,1)S(1)}, u32[]{:S(2)}, u32[]{:S(2)}) collective-permute-start(bf16[1152,768]{1,0:T(8,128)(2,1)} %get-tuple-element.10), channel_id=1, source_target_pairs={{0,2},{2,0},{5,7},{7,5},{8,10},{10,8},{13,15},{15,13},{16,18},{18,... | collective-permute-start | bytes 5308424 | tf_op jit(solution)/shard_map/ppermute | solution.py:435
  8.9 1.3 %collective-permute-start = (bf16[1152,768]{1,0:T(8,128)(2,1)}, bf16[1152,768]{1,0:T(8,128)(2,1)S(1)}, u32[]{:S(2)}, u32[]{:S(2)}) collective-permute-start(bf16[1152,768]{1,0:T(8,128)(2,1)} %get-tuple-element.10), channel_id=1, source_target_pairs={{1,2},{3,0},{6,7},{4,5},{9,10},{11,8},{14,15},{12,13},{17,18},{19,... | collective-permute-start | bytes 5308424 | tf_op jit(solution)/shard_map/ppermute | solution.py:435
  10.2 0.0 copy-start.1
  10.2 0.0 copy-start.2
  10.3 1.4 %collective-permute-start.1 = (bf16[1152,768]{1,0:T(8,128)(2,1)}, bf16[1152,768]{1,0:T(8,128)(2,1)S(1)}, u32[]{:S(2)}, u32[]{:S(2)}) collective-permute-start(bf16[1152,768]{1,0:T(8,128)(2,1)} %get-tuple-element.11.po), channel_id=1, source_target_pairs={{1,0},{3,2},{6,5},{4,7},{9,8},{11,10},{14,13},{12,15},{17,16},{19,... | collective-permute-start | bytes 5308424 | tf_op jit(solution)/shard_map/ppermute | solution.py:435
  11.7 37.0 %collective-permute-done.2.px = bf16[1152,768]{1,0:T(8,128)(2,1)S(1)} collective-permute-done((bf16[1152,768]{1,0:T(8,128)(2,1)}, bf16[1152,768]{1,0:T(8,128)(2,1)S(1)}, u32[]{:S(2)}, u32[]{:S(2)}) %collective-permute-start.2) | collective-permute-done | bytes 1769504 | tf_op jit(solution)/shard_map/ppermute | solution.py:435
  48.7 1.9 %collective-permute-done.pa = bf16[1152,768]{1,0:T(8,128)(2,1)S(1)} collective-permute-done((bf16[1152,768]{1,0:T(8,128)(2,1)}, bf16[1152,768]{1,0:T(8,128)(2,1)S(1)}, u32[]{:S(2)}, u32[]{:S(2)}) %collective-permute-start) | collective-permute-done | bytes 1769504 | tf_op jit(solution)/shard_map/ppermute | solution.py:435
  50.6 0.0 collective-permute-done.1.pb
  50.6 0.0 copy-done
  50.6 0.0 copy-start.3
  50.6 1.5 %copy-done.3 = bf16[1152,768]{1,0:T(8,128)(2,1)S(1)} copy-done((bf16[1152,768]{1,0:T(8,128)(2,1)S(1)}, bf16[1152,768]{1,0:T(8,128)(2,1)}, u32[]{:S(2)}) %copy-start.3) | copy-done | bytes 1769496
  52.1 32.8 %shard_map.69 = (s16[400,768]{1,0:T(8,128)(2,1)S(1)}, s16[400,768]{1,0:T(8,128)(2,1)S(1)}, s16[400,768]{1,0:T(8,128)(2,1)S(1)}, s16[400,768]{1,0:T(8,128)(2,1)S(1)}) custom-call(bf16[1152,768]{1,0:T(8,128)(2,1)S(1)} %collective-permute-done.pa, bf16[1152,768]{1,0:T(8,128)(2,1)S(1)} %collective-permute-done.1.pb, ...), custom_call_target="tpu_custom_call" | custom-call | flops 22649241600 | bytes 1024 | tf_op jit(solution)/shard_map/pallas_call | solution.py:390
  84.9 1.6 %collective-permute-start.3 = (s16[400,768]{1,0:T(8,128)(2,1)S(1)}, s16[400,768]{1,0:T(8,128)(2,1)S(1)}, u32[]{:S(2)}, u32[]{:S(2)}) collective-permute-start(s16[400,768]{1,0:T(8,128)(2,1)S(1)} %get-tuple-element.12), channel_id=1, source_target_pairs={{2,1},{0,3},{7,6},{5,4},{10,9},{8,11},{15,14},{13,12},{18,17},{16,... | collective-permute-start | bytes 1843208 | tf_op jit(solution)/shard_map/ppermute | solution.py:435
  86.5 1.7 %collective-permute-start.4 = (s16[400,768]{1,0:T(8,128)(2,1)S(1)}, s16[400,768]{1,0:T(8,128)(2,1)S(1)}, u32[]{:S(2)}, u32[]{:S(2)}) collective-permute-start(s16[400,768]{1,0:T(8,128)(2,1)S(1)} %get-tuple-element.13), channel_id=1, source_target_pairs={{0,1},{2,3},{5,6},{7,4},{8,9},{10,11},{13,14},{15,12},{16,17},{18,... | collective-permute-start | bytes 1843208 | tf_op jit(solution)/shard_map/ppermute | solution.py:435
  88.2 4.0 %collective-permute-start.5 = (s16[400,768]{1,0:T(8,128)(2,1)S(1)}, s16[400,768]{1,0:T(8,128)(2,1)S(1)}, u32[]{:S(2)}, u32[]{:S(2)}) collective-permute-start(s16[400,768]{1,0:T(8,128)(2,1)S(1)} %get-tuple-element.14), channel_id=1, source_target_pairs={{0,2},{2,0},{5,7},{7,5},{8,10},{10,8},{13,15},{15,13},{16,18},{18,... | collective-permute-start | bytes 1843208 | tf_op jit(solution)/shard_map/ppermute | solution.py:435
  92.2 8.4 %collective-permute-done.3.ra = s16[400,768]{1,0:T(8,128)(2,1)S(1)} collective-permute-done((s16[400,768]{1,0:T(8,128)(2,1)S(1)}, s16[400,768]{1,0:T(8,128)(2,1)S(1)}, u32[]{:S(2)}, u32[]{:S(2)}) %collective-permute-start.3) | collective-permute-done | bytes 614432 | tf_op jit(solution)/shard_map/ppermute | solution.py:435
  100.7 0.0 collective-permute-done.4.rb
  100.7 4.3 %collective-permute-done.5.rx = s16[400,768]{1,0:T(8,128)(2,1)S(1)} collective-permute-done((s16[400,768]{1,0:T(8,128)(2,1)S(1)}, s16[400,768]{1,0:T(8,128)(2,1)S(1)}, u32[]{:S(2)}, u32[]{:S(2)}) %collective-permute-start.5) | collective-permute-done | bytes 614432 | tf_op jit(solution)/shard_map/ppermute | solution.py:435
  104.9 0.0 copy-done.1
  105.0 0.0 copy-done.2
  105.0 3.3 %shard_map.70 = (f32[2,192,768]{2,1,0:T(8,128)}, f32[2,192,768]{2,1,0:T(8,128)}) custom-call(s32[2]{0:T(128)S(1)} %copy-done.2, s16[400,768]{1,0:T(8,128)(2,1)S(1)} %collective-permute-done.3.ra, s16[400,768]{1,0:T(8,128)(2,1)S(1)} %collective-permute-done.4.rb, s16[400,768]{1,0:T(8,128)(2,1)S(1)} %collective-permute-done.5.rx, ...), custom_call_target="tpu_custom_call" | custom-call | flops 1 | bytes 1024 | tf_op jit(solution)/shard_map/pallas_call | solution.py:390
Async XLA Ops:
  0.6 50.0 %copy-start = (f32[2,192,768]{2,1,0:T(8,128)S(1)}, f32[2,192,768]{2,1,0:T(8,128)}, u32[]{:S(2)}) copy-start(f32[2,192,768]{2,1,0:T(8,128)} %factor.3) | copy-start | bytes 3538948
  4.7 44.0 %collective-permute-start.2 = (bf16[1152,768]{1,0:T(8,128)(2,1)}, bf16[1152,768]{1,0:T(8,128)(2,1)S(1)}, u32[]{:S(2)}, u32[]{:S(2)}) collective-permute-start(bf16[1152,768]{1,0:T(8,128)(2,1)} %get-tuple-element.10), channel_id=1, source_target_pairs={{0,2},{2,0},{5,7},{7,5},{8,10},{10,8},{13,15},{15,13},{16,18},{18,... | collective-permute-start | bytes 5308424 | tf_op jit(solution)/shard_map/ppermute | solution.py:435
  8.9 41.7 %collective-permute-start = (bf16[1152,768]{1,0:T(8,128)(2,1)}, bf16[1152,768]{1,0:T(8,128)(2,1)S(1)}, u32[]{:S(2)}, u32[]{:S(2)}) collective-permute-start(bf16[1152,768]{1,0:T(8,128)(2,1)} %get-tuple-element.10), channel_id=1, source_target_pairs={{1,2},{3,0},{6,7},{4,5},{9,10},{11,8},{14,15},{12,13},{17,18},{19,... | collective-permute-start | bytes 5308424 | tf_op jit(solution)/shard_map/ppermute | solution.py:435
  10.2 94.7 %copy-start.1 = (f32[2,768,192]{1,2,0:T(8,128)S(1)}, f32[2,768,192]{1,2,0:T(8,128)}, u32[]{:S(2)}) copy-start(f32[2,768,192]{1,2,0:T(8,128)} %param.8) | copy-start | bytes 3538948
  10.2 94.7 %copy-start.2 = (s32[2]{0:T(128)S(1)}, s32[2]{0:T(128)}, u32[]{:S(2)}) copy-start(s32[2]{0:T(128)} %flags.1) | copy-start | bytes 28
  10.3 40.4 %collective-permute-start.1 = (bf16[1152,768]{1,0:T(8,128)(2,1)}, bf16[1152,768]{1,0:T(8,128)(2,1)S(1)}, u32[]{:S(2)}, u32[]{:S(2)}) collective-permute-start(bf16[1152,768]{1,0:T(8,128)(2,1)} %get-tuple-element.11.po), channel_id=1, source_target_pairs={{1,0},{3,2},{6,5},{4,7},{9,8},{11,10},{14,13},{12,15},{17,16},{19,... | collective-permute-start | bytes 5308424 | tf_op jit(solution)/shard_map/ppermute | solution.py:435
  50.6 1.5 %copy-start.3 = (bf16[1152,768]{1,0:T(8,128)(2,1)S(1)}, bf16[1152,768]{1,0:T(8,128)(2,1)}, u32[]{:S(2)}) copy-start(bf16[1152,768]{1,0:T(8,128)(2,1)} %get-tuple-element.11.po) | copy-start | bytes 5308420
  84.9 15.8 %collective-permute-start.3 = (s16[400,768]{1,0:T(8,128)(2,1)S(1)}, s16[400,768]{1,0:T(8,128)(2,1)S(1)}, u32[]{:S(2)}, u32[]{:S(2)}) collective-permute-start(s16[400,768]{1,0:T(8,128)(2,1)S(1)} %get-tuple-element.12), channel_id=1, source_target_pairs={{2,1},{0,3},{7,6},{5,4},{10,9},{8,11},{15,14},{13,12},{18,17},{16,... | collective-permute-start | bytes 1843208 | tf_op jit(solution)/shard_map/ppermute | solution.py:435
  86.5 14.2 %collective-permute-start.4 = (s16[400,768]{1,0:T(8,128)(2,1)S(1)}, s16[400,768]{1,0:T(8,128)(2,1)S(1)}, u32[]{:S(2)}, u32[]{:S(2)}) collective-permute-start(s16[400,768]{1,0:T(8,128)(2,1)S(1)} %get-tuple-element.13), channel_id=1, source_target_pairs={{0,1},{2,3},{5,6},{7,4},{8,9},{10,11},{13,14},{15,12},{16,17},{18,... | collective-permute-start | bytes 1843208 | tf_op jit(solution)/shard_map/ppermute | solution.py:435
  88.2 16.8 %collective-permute-start.5 = (s16[400,768]{1,0:T(8,128)(2,1)S(1)}, s16[400,768]{1,0:T(8,128)(2,1)S(1)}, u32[]{:S(2)}, u32[]{:S(2)}) collective-permute-start(s16[400,768]{1,0:T(8,128)(2,1)S(1)} %get-tuple-element.14), channel_id=1, source_target_pairs={{0,2},{2,0},{5,7},{7,5},{8,10},{10,8},{13,15},{15,13},{16,18},{18,... | collective-permute-start | bytes 1843208 | tf_op jit(solution)/shard_map/ppermute | solution.py:435

commit v9 on v8

--- a/solution.py
+++ b/solution.py
@@ -414,7 +414,7 @@
     scratch = [(whole, f32)] + [(whole, bf16)] * 4 + [(whole, f32)] + [(whole, bf16)] * 2
     scratch += [((part, size), f32), ((3, part, size), bf16), (whole, bf16)]
     scratch += [(whole, f32)] * 2 + [(whole, bf16)] * 2 + [(whole, f32), ((4, 2 * part, LANES), f32)]
-    return call(refresh_kernel, outs, scratch, (28,), 50 * size**3, [*messages, factor], 42, far=(3, 4))
+    return call(refresh_kernel, outs, scratch, (28,), 50 * size**3, [*messages, factor], 44, far=(3, 4))
 
 
 def unpack_call(flags, messages, factor, moment):

time: 109 us -> 107 us (0.982)
  local copies, waits for them, and re-layouts: 1.49 us -> 0.02 us
    unnamed x8 -> x6, local copies, waits for them, and re-layouts: 1.49 us -> 0.02 us
where the time goes in v9:
time: 107 us
  waiting for transfers between devices  51.7 us (48%)
  Pallas kernels  39.9 us (37%)
  starting transfers between devices  14.3 us (13%)
    ppermute x6, waiting for transfers between devices, exchange(): return lax.ppermute(value, ('dp', 'tensor'), pairs)  51.7 us
    pallas_call x3, Pallas kernels, call(): pl.pallas_call(kernel, out_shape=[jax.ShapeDtypeStruct(shape, dtype) for...  39.9 us
    ppermute x6, starting transfers between devices, exchange(): return lax.ppermute(value, ('dp', 'tensor'), pairs)  14.3 us
  transfers between devices with their start and end apart: 6, of which 4 were waited for; matrix products, arithmetic and copies ran while one was open for 0% of the time, Pallas kernels for 0%

profile of v9, /device:TPU:4, one launch (start us, length us, event | category | flops | bytes accessed | tf_op | source)
XLA Modules:
  0.0 106.7 jit_solution(4941201357189618171)
XLA Ops:
  0.6 0.0 copy-start
  0.6 4.1 %shard_map.68 = (bf16[1152,768]{1,0:T(8,128)(2,1)}, bf16[1152,768]{1,0:T(8,128)(2,1)}) custom-call(f32[2,192,768]{2,1,0:T(8,128)} %basis.1, f32[2,192,768]{2,1,0:T(8,128)} %factor.3, f32[2,192,768]{2,1,0:T(8,128)} %bitcast.3, bf16[2,192,768]{2,1,0:T(8,128)(2,1)} %bitcast.5), custom_call_target="tpu_custom_call" | custom-call | flops 1 | bytes 1024 | tf_op jit(solution)/shard_map/pallas_call | solution.py:390
  4.7 4.2 %collective-permute-start.2 = (bf16[1152,768]{1,0:T(8,128)(2,1)}, bf16[1152,768]{1,0:T(8,128)(2,1)S(1)}, u32[]{:S(2)}, u32[]{:S(2)}) collective-permute-start(bf16[1152,768]{1,0:T(8,128)(2,1)} %get-tuple-element.10), channel_id=1, source_target_pairs={{0,2},{2,0},{5,7},{7,5},{8,10},{10,8},{13,15},{15,13},{16,18},{18,... | collective-permute-start | bytes 5308424 | tf_op jit(solution)/shard_map/ppermute | solution.py:435
  8.9 1.3 %collective-permute-start = (bf16[1152,768]{1,0:T(8,128)(2,1)}, bf16[1152,768]{1,0:T(8,128)(2,1)S(1)}, u32[]{:S(2)}, u32[]{:S(2)}) collective-permute-start(bf16[1152,768]{1,0:T(8,128)(2,1)} %get-tuple-element.10), channel_id=1, source_target_pairs={{1,2},{3,0},{6,7},{4,5},{9,10},{11,8},{14,15},{12,13},{17,18},{19,... | collective-permute-start | bytes 5308424 | tf_op jit(solution)/shard_map/ppermute | solution.py:435
  10.2 0.0 copy-start.1
  10.2 0.0 copy-start.2
  10.3 1.4 %collective-permute-start.1 = (bf16[1152,768]{1,0:T(8,128)(2,1)}, bf16[1152,768]{1,0:T(8,128)(2,1)S(1)}, u32[]{:S(2)}, u32[]{:S(2)}) collective-permute-start(bf16[1152,768]{1,0:T(8,128)(2,1)} %get-tuple-element.11.po), channel_id=1, source_target_pairs={{1,0},{3,2},{6,5},{4,7},{9,8},{11,10},{14,13},{12,15},{17,16},{19,... | collective-permute-start | bytes 5308424 | tf_op jit(solution)/shard_map/ppermute | solution.py:435
  11.7 37.0 %collective-permute-done.2.px = bf16[1152,768]{1,0:T(8,128)(2,1)S(1)} collective-permute-done((bf16[1152,768]{1,0:T(8,128)(2,1)}, bf16[1152,768]{1,0:T(8,128)(2,1)S(1)}, u32[]{:S(2)}, u32[]{:S(2)}) %collective-permute-start.2) | collective-permute-done | bytes 1769504 | tf_op jit(solution)/shard_map/ppermute | solution.py:435
  48.7 1.9 %collective-permute-done.pa = bf16[1152,768]{1,0:T(8,128)(2,1)S(1)} collective-permute-done((bf16[1152,768]{1,0:T(8,128)(2,1)}, bf16[1152,768]{1,0:T(8,128)(2,1)S(1)}, u32[]{:S(2)}, u32[]{:S(2)}) %collective-permute-start) | collective-permute-done | bytes 1769504 | tf_op jit(solution)/shard_map/ppermute | solution.py:435
  50.6 0.0 collective-permute-done.1.pb
  50.6 0.0 copy-done
  50.6 32.5 %shard_map.69 = (s16[400,768]{1,0:T(8,128)(2,1)S(1)}, s16[400,768]{1,0:T(8,128)(2,1)S(1)}, s16[400,768]{1,0:T(8,128)(2,1)S(1)}, s16[400,768]{1,0:T(8,128)(2,1)S(1)}) custom-call(bf16[1152,768]{1,0:T(8,128)(2,1)S(1)} %collective-permute-done.pa, bf16[1152,768]{1,0:T(8,128)(2,1)S(1)} %collective-permute-done.1.pb, ...), custom_call_target="tpu_custom_call" | custom-call | flops 22649241600 | bytes 1024 | tf_op jit(solution)/shard_map/pallas_call | solution.py:390
  83.1 1.6 %collective-permute-start.3 = (s16[400,768]{1,0:T(8,128)(2,1)S(1)}, s16[400,768]{1,0:T(8,128)(2,1)S(1)}, u32[]{:S(2)}, u32[]{:S(2)}) collective-permute-start(s16[400,768]{1,0:T(8,128)(2,1)S(1)} %get-tuple-element.12), channel_id=1, source_target_pairs={{2,1},{0,3},{7,6},{5,4},{10,9},{8,11},{15,14},{13,12},{18,17},{16,... | collective-permute-start | bytes 1843208 | tf_op jit(solution)/shard_map/ppermute | solution.py:435
  84.7 1.7 %collective-permute-start.4 = (s16[400,768]{1,0:T(8,128)(2,1)S(1)}, s16[400,768]{1,0:T(8,128)(2,1)S(1)}, u32[]{:S(2)}, u32[]{:S(2)}) collective-permute-start(s16[400,768]{1,0:T(8,128)(2,1)S(1)} %get-tuple-element.13), channel_id=1, source_target_pairs={{0,1},{2,3},{5,6},{7,4},{8,9},{10,11},{13,14},{15,12},{16,17},{18,... | collective-permute-start | bytes 1843208 | tf_op jit(solution)/shard_map/ppermute | solution.py:435
  86.4 4.0 %collective-permute-start.5 = (s16[400,768]{1,0:T(8,128)(2,1)S(1)}, s16[400,768]{1,0:T(8,128)(2,1)S(1)}, u32[]{:S(2)}, u32[]{:S(2)}) collective-permute-start(s16[400,768]{1,0:T(8,128)(2,1)S(1)} %get-tuple-element.14), channel_id=1, source_target_pairs={{0,2},{2,0},{5,7},{7,5},{8,10},{10,8},{13,15},{15,13},{16,18},{18,... | collective-permute-start | bytes 1843208 | tf_op jit(solution)/shard_map/ppermute | solution.py:435
  90.5 8.4 %collective-permute-done.3.ra = s16[400,768]{1,0:T(8,128)(2,1)S(1)} collective-permute-done((s16[400,768]{1,0:T(8,128)(2,1)S(1)}, s16[400,768]{1,0:T(8,128)(2,1)S(1)}, u32[]{:S(2)}, u32[]{:S(2)}) %collective-permute-start.3) | collective-permute-done | bytes 614432 | tf_op jit(solution)/shard_map/ppermute | solution.py:435
  98.9 0.0 collective-permute-done.4.rb
  98.9 4.3 %collective-permute-done.5.rx = s16[400,768]{1,0:T(8,128)(2,1)S(1)} collective-permute-done((s16[400,768]{1,0:T(8,128)(2,1)S(1)}, s16[400,768]{1,0:T(8,128)(2,1)S(1)}, u32[]{:S(2)}, u32[]{:S(2)}) %collective-permute-start.5) | collective-permute-done | bytes 614432 | tf_op jit(solution)/shard_map/ppermute | solution.py:435
  103.2 0.0 copy-done.1
  103.2 0.0 copy-done.2
  103.2 3.3 %shard_map.70 = (f32[2,192,768]{2,1,0:T(8,128)}, f32[2,192,768]{2,1,0:T(8,128)}) custom-call(s32[2]{0:T(128)S(1)} %copy-done.2, s16[400,768]{1,0:T(8,128)(2,1)S(1)} %collective-permute-done.3.ra, s16[400,768]{1,0:T(8,128)(2,1)S(1)} %collective-permute-done.4.rb, s16[400,768]{1,0:T(8,128)(2,1)S(1)} %collective-permute-done.5.rx, ...), custom_call_target="tpu_custom_call" | custom-call | flops 1 | bytes 1024 | tf_op jit(solution)/shard_map/pallas_call | solution.py:390
Async XLA Ops:
  0.6 50.0 %copy-start = (f32[2,192,768]{2,1,0:T(8,128)S(1)}, f32[2,192,768]{2,1,0:T(8,128)}, u32[]{:S(2)}) copy-start(f32[2,192,768]{2,1,0:T(8,128)} %factor.3) | copy-start | bytes 3538948
  4.7 44.0 %collective-permute-start.2 = (bf16[1152,768]{1,0:T(8,128)(2,1)}, bf16[1152,768]{1,0:T(8,128)(2,1)S(1)}, u32[]{:S(2)}, u32[]{:S(2)}) collective-permute-start(bf16[1152,768]{1,0:T(8,128)(2,1)} %get-tuple-element.10), channel_id=1, source_target_pairs={{0,2},{2,0},{5,7},{7,5},{8,10},{10,8},{13,15},{15,13},{16,18},{18,... | collective-permute-start | bytes 5308424 | tf_op jit(solution)/shard_map/ppermute | solution.py:435
  8.9 41.7 %collective-permute-start = (bf16[1152,768]{1,0:T(8,128)(2,1)}, bf16[1152,768]{1,0:T(8,128)(2,1)S(1)}, u32[]{:S(2)}, u32[]{:S(2)}) collective-permute-start(bf16[1152,768]{1,0:T(8,128)(2,1)} %get-tuple-element.10), channel_id=1, source_target_pairs={{1,2},{3,0},{6,7},{4,5},{9,10},{11,8},{14,15},{12,13},{17,18},{19,... | collective-permute-start | bytes 5308424 | tf_op jit(solution)/shard_map/ppermute | solution.py:435
  10.2 93.0 %copy-start.1 = (f32[2,768,192]{1,2,0:T(8,128)S(1)}, f32[2,768,192]{1,2,0:T(8,128)}, u32[]{:S(2)}) copy-start(f32[2,768,192]{1,2,0:T(8,128)} %param.8) | copy-start | bytes 3538948
  10.2 92.9 %copy-start.2 = (s32[2]{0:T(128)S(1)}, s32[2]{0:T(128)}, u32[]{:S(2)}) copy-start(s32[2]{0:T(128)} %flags.1) | copy-start | bytes 28
  10.3 40.4 %collective-permute-start.1 = (bf16[1152,768]{1,0:T(8,128)(2,1)}, bf16[1152,768]{1,0:T(8,128)(2,1)S(1)}, u32[]{:S(2)}, u32[]{:S(2)}) collective-permute-start(bf16[1152,768]{1,0:T(8,128)(2,1)} %get-tuple-element.11.po), channel_id=1, source_target_pairs={{1,0},{3,2},{6,5},{4,7},{9,8},{11,10},{14,13},{12,15},{17,16},{19,... | collective-permute-start | bytes 5308424 | tf_op jit(solution)/shard_map/ppermute | solution.py:435
  83.1 15.8 %collective-permute-start.3 = (s16[400,768]{1,0:T(8,128)(2,1)S(1)}, s16[400,768]{1,0:T(8,128)(2,1)S(1)}, u32[]{:S(2)}, u32[]{:S(2)}) collective-permute-start(s16[400,768]{1,0:T(8,128)(2,1)S(1)} %get-tuple-element.12), channel_id=1, source_target_pairs={{2,1},{0,3},{7,6},{5,4},{10,9},{8,11},{15,14},{13,12},{18,17},{16,... | collective-permute-start | bytes 1843208 | tf_op jit(solution)/shard_map/ppermute | solution.py:435
  84.7 14.2 %collective-permute-start.4 = (s16[400,768]{1,0:T(8,128)(2,1)S(1)}, s16[400,768]{1,0:T(8,128)(2,1)S(1)}, u32[]{:S(2)}, u32[]{:S(2)}) collective-permute-start(s16[400,768]{1,0:T(8,128)(2,1)S(1)} %get-tuple-element.13), channel_id=1, source_target_pairs={{0,1},{2,3},{5,6},{7,4},{8,9},{10,11},{13,14},{15,12},{16,17},{18,... | collective-permute-start | bytes 1843208 | tf_op jit(solution)/shard_map/ppermute | solution.py:435
  86.4 16.8 %collective-permute-start.5 = (s16[400,768]{1,0:T(8,128)(2,1)S(1)}, s16[400,768]{1,0:T(8,128)(2,1)S(1)}, u32[]{:S(2)}, u32[]{:S(2)}) collective-permute-start(s16[400,768]{1,0:T(8,128)(2,1)S(1)} %get-tuple-element.14), channel_id=1, source_target_pairs={{0,2},{2,0},{5,7},{7,5},{8,10},{10,8},{13,15},{15,13},{16,18},{18,... | collective-permute-start | bytes 1843208 | tf_op jit(solution)/shard_map/ppermute | solution.py:435
